TPU v7x, 256 devices: a whole 4x4x8 slice. The times are simulated.
256 devices in a mesh: ctx: 64 (over x, z, core), tp: 4 (over y).
Axes of the slice: x: 4, y: 4, z: 8, core: 2. Of those that a mesh axis runs over, the one named last changes fastest.
Arguments:
- queries: bfloat16 [16384, 4096], P('ctx', 'tp'), may hold values from -6 to 6
- keys: bfloat16 [16384, 4096], P('ctx', 'tp'), may hold values from -6 to 6
- values: bfloat16 [16384, 4096], P('ctx', 'tp'), may hold values from -6 to 6
- gates: bfloat16 [16384, 4096], P('ctx', 'tp'), may hold values from -8 to 8
- cotangent: bfloat16 [16384, 4096], P('ctx', 'tp'), may hold values from -6 to 6
- doc_ids: int32 [16384], P('ctx'), may hold values from 0 to 31, never falling along the last dimension, each value on 1 to 1024 neighbouring positions
Outputs:
- query_grad: bfloat16 [16384, 4096], P('ctx', 'tp')
- key_grad: bfloat16 [16384, 4096], P('ctx', 'tp')
- value_grad: bfloat16 [16384, 4096], P('ctx', 'tp')
- gate_grad: bfloat16 [16384, 4096], P('ctx', 'tp')
Inputs may be any that keep to these rules, and one draw needn't show every extreme that they name: doc_ids never fall along the sequence; each document holds 1 to 1024 positions, at least one exactly 1024.
All inputs are finite; a program needn't handle non-finite values.
Results may differ from a plain program's by a relative error of at most 0.0058.
Values may be sent and summed in bfloat16 or wider, within the bound.
No kernel may reach another device: no remote copies, remote signals or barrier semaphores. Data moves between devices by JAX's collectives and lax.ppermute only.
A program may use at most 192 MiB of HBM per device.

v0:
```python
import jax
import jax.numpy as jnp
from jax import lax
from jax.sharding import PartitionSpec as P

HEADS = 32
HEAD = 128


EPSILON = 1e-06


def entering(value, axis, join, neutral, backward):
    count, mine = (lax.axis_size(axis), lax.axis_index(axis))
    pieces = jax.tree.map(lambda part: lax.all_gather(part, axis), value)
    if backward:
        pieces = jax.tree.map(lambda part: part[::-1], pieces)
        mine = count - 1 - mine
    total = jax.tree.map(
        lambda part, zero: jnp.full_like(part, 0) + jnp.asarray(zero, part.dtype), value, neutral
    )

    def lap(position, total):
        longer = join(total, jax.tree.map(lambda part: part[position], pieces))
        return jax.tree.map(lambda new, old: jnp.where(position < mine, new, old), longer, total)

    return lax.fori_loop(0, count - 1, lap, total)


def carry_join(earlier, later):
    empty_later = later[1] < 0.0
    joined = later[0] + jnp.where(earlier[1] == later[1], earlier[0], 0.0)
    return (
        jnp.where(empty_later, earlier[0], joined),
        jnp.where(empty_later, earlier[1], later[1]),
    )


def body(queries, keys, values, gates, cotangent, doc_ids):
    length = queries.shape[0]
    heads_here = queries.shape[1] // HEAD
    feature_total = HEADS * HEAD
    query_rows = queries.reshape(length, heads_here, HEAD)
    key_rows = keys.reshape(length, heads_here, HEAD)
    value_rows = values.reshape(length, heads_here, HEAD)
    gate_rows = gates.reshape(length, heads_here, HEAD)
    grad_rows = cotangent.reshape(length, heads_here, HEAD)
    positions = jnp.arange(length, dtype=jnp.int32)
    causal = (positions[None, :] <= positions[:, None]) & (doc_ids[:, None] == doc_ids[None, :])
    first_id = doc_ids[0]
    last_id = doc_ids[length - 1]
    ids_float = doc_ids.astype(jnp.float32)
    scores = jnp.einsum("thd,shd->hts", query_rows, key_rows, preferred_element_type=jnp.float32)
    scores = jnp.where(causal[None], scores, 0.0).astype(jnp.bfloat16)
    tail_mask = (doc_ids == last_id).astype(jnp.bfloat16)[:, None, None]
    tail_state = jnp.einsum(
        "shd,she->hde", key_rows * tail_mask, value_rows, preferred_element_type=jnp.float32
    )
    identity = (jnp.zeros_like(tail_state), jnp.float32(-1.0))
    before, before_id = entering(
        (tail_state, last_id.astype(jnp.float32)), "ctx", carry_join, identity, False
    )
    before_bf = before.astype(jnp.bfloat16)
    head_hit = (ids_float == before_id).astype(jnp.float32)[:, None, None]
    attended = jnp.einsum("hts,she->the", scores, value_rows, preferred_element_type=jnp.float32)
    attended = attended + head_hit * jnp.einsum(
        "thd,hde->the", query_rows, before_bf, preferred_element_type=jnp.float32
    )
    gate_open = jax.nn.sigmoid(gate_rows.astype(jnp.float32))
    grad_float = grad_rows.astype(jnp.float32)
    upstream = grad_float * gate_open
    square_sum, cross_sum = lax.psum(
        (jnp.sum(attended * attended, axis=(1, 2)), jnp.sum(upstream * attended, axis=(1, 2))), "tp"
    )
    inverse = lax.rsqrt(square_sum / feature_total + EPSILON)
    normed = attended * inverse[:, None, None]
    gate_grad = (grad_float * normed * gate_open * (1.0 - gate_open)).astype(jnp.bfloat16)
    factor = inverse * inverse * inverse * cross_sum / feature_total
    out_grad = (upstream * inverse[:, None, None] - attended * factor[:, None, None]).astype(
        jnp.bfloat16
    )
    lead_mask = (doc_ids == first_id).astype(jnp.bfloat16)[:, None, None]
    lead_state = jnp.einsum(
        "thd,the->hde", query_rows * lead_mask, out_grad, preferred_element_type=jnp.float32
    )
    after, after_id = entering(
        (lead_state, first_id.astype(jnp.float32)), "ctx", carry_join, identity, True
    )
    after_bf = after.astype(jnp.bfloat16)
    tail_hit = (ids_float == after_id).astype(jnp.float32)[:, None, None]
    back_scores = jnp.einsum(
        "thd,shd->hts", out_grad, value_rows, preferred_element_type=jnp.float32
    )
    back_scores = jnp.where(causal[None], back_scores, 0.0).astype(jnp.bfloat16)
    query_grad = jnp.einsum(
        "hts,shd->thd", back_scores, key_rows, preferred_element_type=jnp.float32
    )
    query_grad = query_grad + head_hit * jnp.einsum(
        "the,hde->thd", out_grad, before_bf, preferred_element_type=jnp.float32
    )
    key_grad = jnp.einsum(
        "hts,thd->shd", back_scores, query_rows, preferred_element_type=jnp.float32
    )
    key_grad = key_grad + tail_hit * jnp.einsum(
        "she,hde->shd", value_rows, after_bf, preferred_element_type=jnp.float32
    )
    value_grad = jnp.einsum("hts,the->she", scores, out_grad, preferred_element_type=jnp.float32)
    value_grad = value_grad + tail_hit * jnp.einsum(
        "shd,hde->she", key_rows, after_bf, preferred_element_type=jnp.float32
    )
    flat_shape = (length, heads_here * HEAD)
    return (
        query_grad.astype(jnp.bfloat16).reshape(flat_shape),
        key_grad.astype(jnp.bfloat16).reshape(flat_shape),
        value_grad.astype(jnp.bfloat16).reshape(flat_shape),
        gate_grad.reshape(flat_shape),
    )


def solution(mesh):
    return jax.shard_map(
        body,
        mesh=mesh,
        in_specs=(
            P("ctx", "tp"),
            P("ctx", "tp"),
            P("ctx", "tp"),
            P("ctx", "tp"),
            P("ctx", "tp"),
            P("ctx"),
        ),
        out_specs=(P("ctx", "tp"), P("ctx", "tp"), P("ctx", "tp"), P("ctx", "tp")),
        check_vma=False,
    )
```

profile of v0, /device:TPU:1, one launch (start us, length us, event | category | flops | bytes accessed | tf_op | source)
XLA Modules:
  0.0 836.0 jit_solution(1256997889962779188)
XLA Ops:
  7.2 1.3 fusion.35
  8.6 1.3 compare_convert_fusion.3
  18.8 130.1 %all-reduce.2 = (f32[64]{0:T(128)S(1)}, f32[64]{0:T(128)S(1)}) all-reduce(f32[64]{0:T(128)S(1)} %dynamic-update-slice, f32[64]{0:T(128)S(1)} %dynamic-update-slice.1), channel_id=1, replica_groups=mesh['ctx'=64,'tp'=4] {'ctx'}, use_global_device_ids=true, to_apply=%add | all-reduce | flops 128 | bytes 1024
  149.1 1.7 select_convert_fusion.1
  151.7 1.5 convolution_bitcast_fusion.2
  153.2 6.2 all-gather.5.cloned.1.call-done
  159.4 243.5 %while.32 = (s32[]{:T(128)}, f32[8,128,128]{2,1,0:T(8,128)S(1)}, f32[]{:T(128)}, s32[]{:T(128)}, f32[64]{0:T(128)S(1)}, /*index=5*/f32[64,8,128,128]{3,2,1,0:T(8,128)}, s32[]{:T(128)}, s32[]{:T(128)}, f32[]{:T(128)}) while((s32[]{:T(128)}, f32[8,128,128]{2,1,0:T(8,128)S(1)}, f32[]{:T(128)}, s32[]{:T(128)}, f32[64]{0:T(128)S(1)}, ...), condition=%wide.region_1.2_spmd.clone, body=%wide.region_0.1_spmd.clone.sunk | while | flops 655368 | bytes 1573039 | solution.py:27
  161.3 1.3 select_select_fusion.4
  165.2 1.3 select_select_fusion.4
  184.5 1.3 select_select_fusion.4
  188.4 1.3 select_select_fusion.4
  207.7 1.3 select_select_fusion.4
  211.6 1.3 select_select_fusion.4
  230.9 1.3 select_select_fusion.4
  234.8 1.3 select_select_fusion.4
  238.6 1.3 select_select_fusion.4
  257.9 1.3 select_select_fusion.4
  261.8 1.3 select_select_fusion.4
  281.1 1.3 select_select_fusion.4
  285.0 1.3 select_select_fusion.4
  304.3 1.3 select_select_fusion.4
  308.2 1.3 select_select_fusion.4
  312.0 1.3 select_select_fusion.4
  331.4 1.3 select_select_fusion.4
  335.2 1.3 select_select_fusion.4
  354.6 1.3 select_select_fusion.4
  358.4 1.3 select_select_fusion.4
  377.7 1.3 select_select_fusion.4
  381.6 1.3 select_select_fusion.4
  385.5 1.3 select_select_fusion.4
  403.5 2.8 multiply_reduce_fusion.1
  406.4 8.4 %all-reduce.3 = (f32[256]{0:T(256)S(1)}, f32[256]{0:T(256)S(1)}) all-reduce(f32[256]{0:T(256)S(1)} %get-tuple-element.279, f32[256]{0:T(256)S(1)} %get-tuple-element.278), channel_id=1, replica_groups=mesh['ctx'=64,'tp'=4] {'tp'}, use_global_device_ids=true, to_apply=%region_5.6 | all-reduce | flops 512 | bytes 4096 | tf_op jit(solution)/shard_map/psum | solution.py:72
  414.8 2.4 multiply_convert_fusion
  419.3 1.6 select_convert_fusion
  422.5 2.0 copy.52
  424.6 2.1 copy.55
  428.4 130.2 %all-gather.7.cloned.1.call-done = f32[512,128,128]{2,1,0:T(8,128)} async-done(((f32[8,128,128]{2,1,0:T(8,128)}), f32[512,128,128]{2,1,0:T(8,128)}) %all-gather.7.cloned.1.call-update) | async-done | bytes 33554448 | tf_op jit(solution)/shard_map/all_gather | solution.py:15
  558.6 23.0 %rev.7 = f32[64,8,128,128]{3,2,1,0:T(8,128)} reverse(f32[64,8,128,128]{3,2,1,0:T(8,128)} %bitcast.106), dimensions={0} | reverse | bytes 67108864 | tf_op jit(solution)/shard_map/rev | solution.py:17
  581.6 243.7 %while.33 = (s32[]{:T(128)}, f32[8,128,128]{2,1,0:T(8,128)S(1)}, f32[]{:T(128)}, s32[]{:T(128)}, f32[64]{0:T(128)S(1)}, /*index=5*/f32[64,8,128,128]{3,2,1,0:T(8,128)}, s32[]{:T(128)}, s32[]{:T(128)}, f32[]{:T(128)}) while((s32[]{:T(128)}, f32[8,128,128]{2,1,0:T(8,128)S(1)}, f32[]{:T(128)}, s32[]{:T(128)}, f32[64]{0:T(128)S(1)}, ...), condition=%wide.region_7.8_spmd.clone, body=%wide.region_6.7_spmd.clone.sunk | while | flops 655368 | bytes 1573039 | solution.py:27
  583.4 1.3 select_select_fusion.5
  587.3 1.3 select_select_fusion.5
  598.9 1.3 select_select_fusion.5
  602.8 1.3 select_select_fusion.5
  614.4 1.3 select_select_fusion.5
  629.9 1.3 select_select_fusion.5
  645.3 1.3 select_select_fusion.5
  656.9 1.3 select_select_fusion.5
  825.2 1.6 fusion.9
  (284 shorter events, 214.2 us)
Async XLA Ops:
  7.2 4.3 copy-start
  7.2 152.3 %all-gather.5.cloned.1.call-start = ((), (), s32[]{:S(2)}) async-start(), calls=%async_computation | async-start | bytes 34078720 | tf_op jit(solution)/shard_map/all_gather | solution.py:15
  9.9 4.1 copy-start.13
  11.1 3.9 copy-start.12
  11.4 1.2 copy-start.5
  12.6 546.0 %all-gather.7.cloned.1.call-start = ((), (), s32[]{:S(2)}) async-start(), calls=%async_computation.1 | async-start | bytes 34078720 | tf_op jit(solution)/shard_map/all_gather | solution.py:15
  15.2 1.6 copy-start.15
  15.3 133.7 %copy-start.14 = (s32[256]{0:T(256)S(1)}, s32[256]{0:T(256)}, u32[]{:S(2)}) copy-start(s32[256]{0:T(256)} %param.15) | copy-start | bytes 3076
  150.8 1.0 copy-start.7
  414.8 3.2 copy-start.3
  417.3 0.8 copy-start.1
  418.1 2.9 copy-start.6
  419.3 2.1 copy-start.2
  420.9 1.6 copy-start.9
  421.4 5.2 copy-start.8
  424.6 3.4 copy-start.4
  426.7 1.4 copy-start.10
  581.6 243.7 %copy-start.11 = (bf16[256,1024]{1,0:T(8,128)(2,1)S(1)}, bf16[256,1024]{1,0:T(8,128)(2,1)}, u32[]{:S(2)}) copy-start(bf16[256,1024]{1,0:T(8,128)(2,1)} %param.11) | copy-start | bytes 1572868
Sparse Core Ops, SparseCore 0:
  12.7 146.6 all-gather.4
  419.3 139.1 all-gather.6
where the time goes:
time: 846 us; the launch traced here: 836 us
  loops' own time  250 us (30%)
  other arithmetic  168 us (20%)
  blocking collectives  139 us (16%)
  waiting for transfers between devices  136 us (16%)
  local copies, waits for them, and re-layouts  112 us (13%)
  between operations  15.6 us (2%)
  matrix products  14.9 us (2%)
    another operation x2, loops' own time, entering(): return lax.fori_loop(0, count - 1, lap, total)  250 us
    select_n x126, other arithmetic, lap(): jnp.where(position < mine, new, old)  164 us
    all_gather x2, waiting for transfers between devices, entering(): pieces = jax.tree.map(lambda part: lax.all_gather(part, axis), value)  136 us
    unnamed x1, blocking collectives  130 us
    dynamic_slice x126, local copies, waits for them, and re-layouts, lap(): longer = join(total, jax.tree.map(lambda part: part[position], pieces))  73.9 us
    rev x2, local copies, waits for them, and re-layouts, entering(): pieces = jax.tree.map(lambda part: part[::-1], pieces)  23.1 us
  transfers between devices with their start and end apart: 2, of which 2 were waited for; matrix products, arithmetic and copies ran while one was open for 2% of the time, Pallas kernels for 0%

commit v1 on v0

v1 whole, which is shorter than its diff:
```python
import functools

import jax
import jax.numpy as jnp
from jax import lax
from jax.experimental import pallas as pl
from jax.experimental.pallas import tpu as pltpu
from jax.sharding import PartitionSpec as P

HEADS = 32
HEAD = 128
EPSILON = 1e-06
FEATURES = HEADS * HEAD
BF = jnp.bfloat16
F32 = jnp.float32
IDS = 16
MIB = 1 << 20


def dot(a, b, dims):
    return lax.dot_general(a, b, (dims, ((), ())), preferred_element_type=F32)


NN = ((1,), (0,))
NT = ((1,), (1,))
TN = ((0,), (0,))


def head(h):
    return slice(h * HEAD, (h + 1) * HEAD)


def column(row, lanes):
    return jnp.broadcast_to(row, (lanes, row.shape[1])).T


def put_ids(ids, out_ref, states):
    last = jnp.broadcast_to(ids[:, -1:], (IDS, HEAD))
    first = jnp.broadcast_to(ids[:, :1], (IDS, HEAD))
    out_ref[states : states + IDS, :] = last.astype(F32).astype(BF)
    out_ref[states + IDS :, :] = first.astype(F32).astype(BF)


def tail_kernel(ids_ref, k_ref, v_ref, out_ref):
    ids = ids_ref[...]
    states = k_ref.shape[1]
    hit = (column(ids, HEAD) == ids[:, -1:]).astype(F32).astype(BF)
    for h in range(states // HEAD):
        state = dot(k_ref[:, head(h)] * hit, v_ref[:, head(h)], TN)
        out_ref[head(h), :] = state.astype(BF)
    put_ids(ids, out_ref, states)


def local_kernel(ids_ref, q_ref, k_ref, v_ref, g_ref, c_ref, scores_ref, local_ref, up_ref):
    ids = ids_ref[...]
    length = ids.shape[1]
    at = lax.broadcasted_iota(jnp.int32, (length, length), 0)
    of = lax.broadcasted_iota(jnp.int32, (length, length), 1)
    causal = (of <= at) & (column(ids, length) == ids)
    for h in range(q_ref.shape[1] // HEAD):
        scores = dot(q_ref[:, head(h)], k_ref[:, head(h)], NT)
        scores = jnp.where(causal, scores, 0.0).astype(BF)
        scores_ref[h] = scores
        local_ref[:, head(h)] = dot(scores, v_ref[:, head(h)], NN)
        gate = jax.nn.sigmoid(g_ref[:, head(h)].astype(F32))
        up_ref[:, head(h)] = c_ref[:, head(h)].astype(F32) * gate


def attend_kernel(ids_ref, q_ref, before_ref, local_ref, up_ref, attended_ref, sums_ref):
    ids = ids_ref[...]
    length = ids.shape[1]
    hit = (column(ids, HEAD) == ids[:, :1]).astype(F32).astype(BF)
    square = jnp.zeros((length, HEAD), F32)
    cross = jnp.zeros((length, HEAD), F32)
    for h in range(q_ref.shape[1] // HEAD):
        attended = local_ref[:, head(h)] + dot(q_ref[:, head(h)] * hit, before_ref[head(h), :], NN)
        attended_ref[:, head(h)] = attended
        square = square + attended * attended
        cross = cross + up_ref[:, head(h)] * attended
    sums_ref[0:1, :] = jnp.sum(square.T, axis=0, keepdims=True)
    sums_ref[1:2, :] = jnp.sum(cross.T, axis=0, keepdims=True)


def scales(parts):
    total = parts[0][...]
    for part in parts[1:]:
        total = total + part[...]
    inverse = lax.rsqrt(total[0:1, :] / FEATURES + EPSILON)
    factor = inverse * inverse * inverse * total[1:2, :] / FEATURES
    return inverse, factor


def lead_kernel(ids_ref, s0, s1, s2, s3, q_ref, attended_ref, up_ref, grad_ref, out_ref):
    ids = ids_ref[...]
    states = q_ref.shape[1]
    inverse, factor = scales((s0, s1, s2, s3))
    inverse, factor = column(inverse, HEAD), column(factor, HEAD)
    hit = (column(ids, HEAD) == ids[:, :1]).astype(F32).astype(BF)
    for h in range(states // HEAD):
        grad = up_ref[:, head(h)] * inverse - attended_ref[:, head(h)] * factor
        grad = grad.astype(BF)
        grad_ref[:, head(h)] = grad
        out_ref[head(h), :] = dot(q_ref[:, head(h)] * hit, grad, TN).astype(BF)
    put_ids(ids, out_ref, states)


def back_kernel(
    ids_ref, s0, s1, s2, s3, q_ref, k_ref, v_ref, g_ref, scores_ref, attended_ref, up_ref, grad_ref, before_ref,
    query_grad_ref, gate_grad_ref, key_part_ref, value_part_ref,
):
    ids = ids_ref[...]
    length = ids.shape[1]
    inverse, _ = scales((s0, s1, s2, s3))
    inverse = column(inverse, HEAD)
    hit = (column(ids, HEAD) == ids[:, :1]).astype(F32).astype(BF)
    at = lax.broadcasted_iota(jnp.int32, (length, length), 0)
    of = lax.broadcasted_iota(jnp.int32, (length, length), 1)
    causal = (of <= at) & (column(ids, length) == ids)
    for h in range(q_ref.shape[1] // HEAD):
        grad = grad_ref[:, head(h)]
        back = jnp.where(causal, dot(grad, v_ref[:, head(h)], NT), 0.0).astype(BF)
        query_grad = dot(back, k_ref[:, head(h)], NN) + dot(grad * hit, before_ref[head(h), :], NT)
        query_grad_ref[:, head(h)] = query_grad.astype(BF)
        key_part_ref[:, head(h)] = dot(back, q_ref[:, head(h)], TN)
        value_part_ref[:, head(h)] = dot(scores_ref[h], grad, TN)
        gate = jax.nn.sigmoid(g_ref[:, head(h)].astype(F32))
        gate_grad = up_ref[:, head(h)] * attended_ref[:, head(h)] * inverse * (1.0 - gate)
        gate_grad_ref[:, head(h)] = gate_grad.astype(BF)


def finish_kernel(ids_ref, k_ref, v_ref, after_ref, key_part_ref, value_part_ref, key_grad_ref, value_grad_ref):
    ids = ids_ref[...]
    hit = (column(ids, HEAD) == ids[:, -1:]).astype(F32).astype(BF)
    for h in range(k_ref.shape[1] // HEAD):
        after = after_ref[head(h), :]
        key_grad = key_part_ref[:, head(h)] + dot(v_ref[:, head(h)] * hit, after, NT)
        key_grad_ref[:, head(h)] = key_grad.astype(BF)
        value_grad = value_part_ref[:, head(h)] + dot(k_ref[:, head(h)] * hit, after, NN)
        value_grad_ref[:, head(h)] = value_grad.astype(BF)


def call(kernel, outs, flops, *args):
    whole = pl.BlockSpec(memory_space=pltpu.VMEM)
    size = sum(a.size * a.dtype.itemsize for a in (*args, *outs))
    return pl.pallas_call(
        kernel,
        out_shape=outs,
        in_specs=[whole] * len(args),
        out_specs=[whole] * len(outs),
        compiler_params=pltpu.CompilerParams(vmem_limit_bytes=24 * MIB),
        cost_estimate=pl.CostEstimate(flops=flops, bytes_accessed=size, transcendentals=0),
        name=kernel.__name__,
    )(*args)


def body(queries, keys, values, gates, cotangent, doc_ids):
    length, states = queries.shape
    count = lax.axis_size("ctx")
    heads = states // HEAD
    shape = jax.ShapeDtypeStruct
    ids = doc_ids.reshape(1, length)
    odd = lax.rem(lax.axis_index("ctx"), 2) == 1
    message = shape((states + 2 * IDS, HEAD), BF)
    wide = shape((length, states), F32)
    narrow = shape((length, states), BF)
    unit = 2 * length * length * states

    def swap(x):
        return lax.ppermute(x, "ctx", [(i, i ^ 1) for i in range(count)])

    def spread(x, way):
        pairs = [(i, (i + way * (2 if i % 2 == 0 else 4)) % count) for i in range(count)]
        return lax.ppermute(x, "ctx", pairs)

    def add(a, b):
        return (a.astype(F32) + b.astype(F32)).astype(BF)

    is_state = lax.broadcasted_iota(jnp.int32, message.shape, 0) < states

    def last_of(m):
        return m[states, 0]

    def first_of(m):
        return m[states + IDS, 0]

    (mine,) = call(tail_kernel, [message], unit // 2, ids, keys, values)
    theirs = swap(mine)
    even_part, odd_part = jnp.where(odd, theirs, mine), jnp.where(odd, mine, theirs)
    first_even, last_even = first_of(even_part), last_of(even_part)
    first_odd, last_odd = first_of(odd_part), last_of(odd_part)
    chip = jnp.where(is_state & (last_even == last_odd), add(mine, theirs), odd_part)
    came = spread(chip, 1)
    scores, local, up = call(
        local_kernel, [shape((heads, length, length), BF), wide, wide], 2 * unit, ids, queries, keys, values, gates, cotangent
    )
    came = jnp.where(last_of(came) == first_even, came[:states], 0)
    entering = add(came, swap(came))
    before = jnp.where(
        odd,
        jnp.where(
            first_odd == last_even,
            jnp.where(first_even == last_even, add(even_part[:states], entering), even_part[:states]),
            0,
        ),
        entering,
    )
    attended, sums = call(attend_kernel, [wide, shape((2, length), F32)], unit // 2, ids, queries, before, local, up)
    ranks = lax.axis_size("tp")
    parts = [sums] + [
        lax.ppermute(sums, "tp", [(i, (i + step) % ranks) for i in range(ranks)]) for step in (2, 1, 3)
    ]
    grad, lead = call(lead_kernel, [narrow, message], unit // 2, ids, *parts, queries, attended, up)

    other = swap(lead)
    lead_even, lead_odd = jnp.where(odd, other, lead), jnp.where(odd, lead, other)
    chip = jnp.where(is_state & (first_even == first_odd), add(lead, other), lead_even)
    came = spread(chip, -1)
    query_grad, gate_grad, key_part, value_part = call(
        back_kernel, [narrow, narrow, wide, wide], 5 * unit, ids, *parts, queries, keys, values, gates, scores, attended,
        up, grad, before,
    )
    came = jnp.where(first_of(came) == last_odd, came[:states], 0)
    leaving = add(came, swap(came))
    after = jnp.where(
        odd,
        leaving,
        jnp.where(
            first_odd == last_even,
            jnp.where(first_odd == last_odd, add(lead_odd[:states], leaving), lead_odd[:states]),
            0,
        ),
    )
    key_grad, value_grad = call(finish_kernel, [narrow, narrow], unit, ids, keys, values, after, key_part, value_part)
    return query_grad, key_grad, value_grad, gate_grad


def solution(mesh):
    return jax.shard_map(
        body,
        mesh=mesh,
        in_specs=(P("ctx", "tp"),) * 5 + (P("ctx"),),
        out_specs=(P("ctx", "tp"),) * 4,
        check_vma=False,
    )
```

time: 846 us -> 65.1 us (0.08); the launches traced: 836 us -> 64.7 us
  loops' own time: 250 us -> 0 us
  other arithmetic: 168 us -> 1 us
  blocking collectives: 139 us -> 0 us
  waiting for transfers between devices: 136 us -> 23.6 us
  local copies, waits for them, and re-layouts: 112 us -> 4.39 us
  starting transfers between devices: 0.08 us -> 17.9 us
  matrix products: 14.9 us -> 0 us
    another operation x2 -> x0, loops' own time: 250 us -> none  [entering(): return lax.fori_loop(0, count - 1, lap, total)]
    select_n x126 -> x7, other arithmetic: 164 us -> 0.98 us  [the longest x1 0.26 us: body(): jnp.where(is_state & (last_even == last_odd), add(mine, theirs), odd_part)]
    all_gather x2 -> x0, waiting for transfers between devices: 136 us -> none  [entering(): pieces = jax.tree.map(lambda part: lax.all_gather(part, axis), value)]
    unnamed x1 -> x0, blocking collectives: 130 us -> none
    dynamic_slice x126 -> x0, local copies, waits for them, and re-layouts: 73.9 us -> none  [lap(): longer = join(total, jax.tree.map(lambda part: part[position], pieces))]
    ppermute x0 -> x9, waiting for transfers between devices: none -> 23.6 us  [the longest x2 21.5 us: spread(): return lax.ppermute(x, 'ctx', pairs)]
    rev x2 -> x0, local copies, waits for them, and re-layouts: 23.1 us -> none  [entering(): pieces = jax.tree.map(lambda part: part[::-1], pieces)]
    ppermute x0 -> x9, starting transfers between devices: none -> 17.9 us  [the longest x4 8.51 us: swap(): return lax.ppermute(x, 'ctx', [(i, i ^ 1) for i in range(count)])]
  transfers between devices with their start and end apart: 2 -> 9, of which waited for: 2 -> 4; matrix products, arithmetic and copies ran while one was open for 2% -> 0% of each run, Pallas kernels for 0% -> 7%
where the time goes in v1:
time: 65.1 us; the launch traced here: 64.7 us
  waiting for transfers between devices  23.6 us (36%)
  starting transfers between devices  17.9 us (27%)
  between operations  9.87 us (15%)
  Pallas kernels  7.89 us (12%)
  local copies, waits for them, and re-layouts  4.39 us (7%)
  other arithmetic  1 us (2%)
    ppermute x2, waiting for transfers between devices, spread(): return lax.ppermute(x, 'ctx', pairs)  21.5 us
    ppermute x4, starting transfers between devices, swap(): return lax.ppermute(x, 'ctx', [(i, i ^ 1) for i in range(count)])  8.51 us
    pallas_call x6, Pallas kernels, call(): pl.pallas_call(kernel, out_shape=outs, in_specs=[whole] * len(args), out_...  7.89 us
    ppermute x3, starting transfers between devices, body(): lax.ppermute(sums, 'tp', [(i, (i + step) % ranks) for i in range(ranks)])  5.67 us
    ppermute x2, starting transfers between devices, spread(): return lax.ppermute(x, 'ctx', pairs)  3.77 us
    unnamed x16, local copies, waits for them, and re-layouts  2.78 us
  transfers between devices with their start and end apart: 9, of which 4 were waited for; matrix products, arithmetic and copies ran while one was open for 0% of the time, Pallas kernels for 7%

profile of v1, /device:TPU:1, one launch (start us, length us, event | category | flops | bytes accessed | tf_op | source)
XLA Modules:
  0.0 64.7 jit_solution(6196038767143495505)
XLA Ops:
  0.6 0.0 copy-start.7
  0.6 0.7 %copy-done.7 = s32[256]{0:T(256)S(1)} copy-done((s32[256]{0:T(256)S(1)}, s32[256]{0:T(256)}, u32[]{:S(2)}) %copy-start.7) | copy-done | bytes 1048
  1.3 0.0 copy-start
  1.3 1.0 %copy-done = bf16[256,1024]{1,0:T(8,128)(2,1)S(1)} copy-done((bf16[256,1024]{1,0:T(8,128)(2,1)S(1)}, bf16[256,1024]{1,0:T(8,128)(2,1)}, u32[]{:S(2)}) %copy-start) | copy-done | bytes 524312
  2.4 0.0 copy-start.2
  2.4 1.0 %copy-done.2 = bf16[256,1024]{1,0:T(8,128)(2,1)S(1)} copy-done((bf16[256,1024]{1,0:T(8,128)(2,1)S(1)}, bf16[256,1024]{1,0:T(8,128)(2,1)}, u32[]{:S(2)}) %copy-start.2) | copy-done | bytes 524312
  3.4 0.0 copy-start.6
  3.4 0.5 tail_kernel.1
  3.9 3.3 %collective-permute-start = (bf16[1056,128]{1,0:T(8,128)(2,1)S(1)}, bf16[1056,128]{1,0:T(8,128)(2,1)S(1)}, u32[]{:S(2)}, u32[]{:S(2)}) collective-permute-start(bf16[1056,128]{1,0:T(8,128)(2,1)S(1)} %tail_kernel.1), channel_id=1, source_target_pairs={{0,4},{4,0},{8,12},{12,8},{16,20},{20,16},{24,28},{28,24},{32,36},... | collective-permute-start | bytes 811016 | tf_op jit(solution)/shard_map/ppermute | solution.py:169
  7.2 1.2 %collective-permute-done = bf16[1056,128]{1,0:T(8,128)(2,1)S(1)} collective-permute-done((bf16[1056,128]{1,0:T(8,128)(2,1)S(1)}, bf16[1056,128]{1,0:T(8,128)(2,1)S(1)}, u32[]{:S(2)}, u32[]{:S(2)}) %collective-permute-start) | collective-permute-done | bytes 270368 | tf_op jit(solution)/shard_map/ppermute | solution.py:169
  8.4 0.0 copy-start.4
  8.4 0.0 copy-start.5
  8.4 0.5 fusion.10
  10.3 0.0 copy-start.1
  10.3 0.0 copy-start.3
  10.3 0.3 fusion.2
  10.5 1.3 %collective-permute-start.1 = (bf16[1056,128]{1,0:T(8,128)(2,1)S(1)}, bf16[1056,128]{1,0:T(8,128)(2,1)S(1)}, u32[]{:S(2)}, u32[]{:S(2)}) collective-permute-start(bf16[1056,128]{1,0:T(8,128)(2,1)S(1)} %fusion.2), channel_id=1, source_target_pairs={{0,8},{4,20},{8,16},{12,28},{16,24},{20,36},{24,32},{28,44},{32,40... | collective-permute-start | bytes 811016 | tf_op jit(solution)/shard_map/ppermute | solution.py:173
  11.9 11.9 %collective-permute-done.1 = bf16[1056,128]{1,0:T(8,128)(2,1)S(1)} collective-permute-done((bf16[1056,128]{1,0:T(8,128)(2,1)S(1)}, bf16[1056,128]{1,0:T(8,128)(2,1)S(1)}, u32[]{:S(2)}, u32[]{:S(2)}) %collective-permute-start.1) | collective-permute-done | bytes 270368 | tf_op jit(solution)/shard_map/ppermute | solution.py:173
  23.7 0.6 slice.47
  25.6 3.3 %collective-permute-start.2 = (bf16[1024,128]{1,0:T(8,128)(2,1)S(1)}, bf16[1024,128]{1,0:T(8,128)(2,1)S(1)}, u32[]{:S(2)}, u32[]{:S(2)}) collective-permute-start(bf16[1024,128]{1,0:T(8,128)(2,1)S(1)} %slice_select_fusion.2), channel_id=1, source_target_pairs={{0,4},{4,0},{8,12},{12,8},{16,20},{20,16},{24,28},{28,24},{32,36},... | collective-permute-start | bytes 786440 | tf_op jit(solution)/shard_map/ppermute | solution.py:169
  29.0 0.0 copy-done.6
  29.0 0.0 copy-done.4
  29.0 0.0 copy-done.5
  29.0 0.0 copy-done.1
  29.0 0.0 copy-done.3
  29.0 1.1 %local_kernel.1 = (bf16[8,256,256]{2,1,0:T(8,128)(2,1)S(1)}, f32[256,1024]{1,0:T(8,128)S(1)}, f32[256,1024]{1,0:T(8,128)S(1)}) custom-call(s32[1,256]{1,0:T(1,128)S(1)} %bitcast.9, bf16[256,1024]{1,0:T(8,128)(2,1)S(1)} %copy-done.4, bf16[256,1024]{1,0:T(8,128)(2,1)S(1)} %copy-done.1, bf16[256,1024]{1,0:T(8,128)(2,1)S(1)} %copy-done.3, ...), custom_call_target="tpu_custom_call" | custom-call | flops 268435456 | bytes 5768192 | tf_op jit(solution)/shard_map/local_kernel/pallas_call | solution.py:145
  32.7 0.0 collective-permute-done.2
  32.7 0.2 fusion.7.before_ref
  32.9 0.6 attend_kernel.1
  33.4 3.0 %collective-permute-start.3 = (f32[2,256]{1,0:T(2,128)S(1)}, f32[2,256]{1,0:T(2,128)S(1)}, u32[]{:S(2)}, u32[]{:S(2)}) collective-permute-start(f32[2,256]{1,0:T(2,128)S(1)} %get-tuple-element.19.s0), channel_id=1, source_target_pairs={{0,2},{1,3},{2,0},{3,1},{4,6},{5,7},{6,4},{7,5},{8,10},{9,11},{10,... | collective-permute-start | bytes 6152 | tf_op jit(solution)/shard_map/ppermute | solution.py:210
  36.4 0.4 collective-permute-start.4
  36.8 2.3 %collective-permute-start.5 = (f32[2,256]{1,0:T(2,128)S(1)}, f32[2,256]{1,0:T(2,128)S(1)}, u32[]{:S(2)}, u32[]{:S(2)}) collective-permute-start(f32[2,256]{1,0:T(2,128)S(1)} %get-tuple-element.19.s0), channel_id=1, source_target_pairs={{0,3},{1,0},{2,1},{3,2},{4,7},{5,4},{6,5},{7,6},{8,11},{9,8},{10,9... | collective-permute-start | bytes 6152 | tf_op jit(solution)/shard_map/ppermute | solution.py:210
  39.1 0.0 collective-permute-done.3.s1
  39.1 1.0 %collective-permute-done.4.s2 = f32[2,256]{1,0:T(2,128)S(1)} collective-permute-done((f32[2,256]{1,0:T(2,128)S(1)}, f32[2,256]{1,0:T(2,128)S(1)}, u32[]{:S(2)}, u32[]{:S(2)}) %collective-permute-start.4) | collective-permute-done | bytes 2080 | tf_op jit(solution)/shard_map/ppermute | solution.py:210
  40.1 0.0 collective-permute-done.5.s3
  40.1 0.6 lead_kernel.1
  40.7 1.6 %collective-permute-start.6 = (bf16[1056,128]{1,0:T(8,128)(2,1)S(1)}, bf16[1056,128]{1,0:T(8,128)(2,1)S(1)}, u32[]{:S(2)}, u32[]{:S(2)}) collective-permute-start(bf16[1056,128]{1,0:T(8,128)(2,1)S(1)} %get-tuple-element.24), channel_id=1, source_target_pairs={{0,4},{4,0},{8,12},{12,8},{16,20},{20,16},{24,28},{28,24},{32,36},... | collective-permute-start | bytes 811016 | tf_op jit(solution)/shard_map/ppermute | solution.py:169
  43.6 0.0 collective-permute-done.6
  43.6 0.3 fusion.3
  43.9 2.4 %collective-permute-start.7 = (bf16[1056,128]{1,0:T(8,128)(2,1)S(1)}, bf16[1056,128]{1,0:T(8,128)(2,1)S(1)}, u32[]{:S(2)}, u32[]{:S(2)}) collective-permute-start(bf16[1056,128]{1,0:T(8,128)(2,1)S(1)} %fusion.3), channel_id=1, source_target_pairs={{0,248},{4,244},{8,0},{12,252},{16,8},{20,4},{24,16},{28,12},{32,2... | collective-permute-start | bytes 811016 | tf_op jit(solution)/shard_map/ppermute | solution.py:173
  46.3 9.6 %collective-permute-done.7 = bf16[1056,128]{1,0:T(8,128)(2,1)S(1)} collective-permute-done((bf16[1056,128]{1,0:T(8,128)(2,1)S(1)}, bf16[1056,128]{1,0:T(8,128)(2,1)S(1)}, u32[]{:S(2)}, u32[]{:S(2)}) %collective-permute-start.7) | collective-permute-done | bytes 270368 | tf_op jit(solution)/shard_map/ppermute | solution.py:173
  55.9 0.5 slice.49
  57.8 0.3 collective-permute-start.8
  59.3 3.6 %back_kernel.1 = (bf16[256,1024]{1,0:T(8,128)(2,1)}, bf16[256,1024]{1,0:T(8,128)(2,1)}, f32[256,1024]{1,0:T(8,128)S(1)}, f32[256,1024]{1,0:T(8,128)S(1)}) custom-call(s32[1,256]{1,0:T(1,128)S(1)} %bitcast.12, f32[2,256]{1,0:T(2,128)S(1)} %get-tuple-element.19.s0, f32[2,256]{1,0:T(2,128)S(1)} %collective-permute-done.3.s1, ...), custom_call_target="tpu_custom_call" | custom-call | flops 671088640 | bytes 9184256 | tf_op jit(solution)/shard_map/back_kernel/pallas_call | solution.py:145
  62.9 0.0 collective-permute-done.8
  62.9 0.2 fusion.5.after_ref
  63.1 1.6 %finish_kernel.1 = (bf16[256,1024]{1,0:T(8,128)(2,1)}, bf16[256,1024]{1,0:T(8,128)(2,1)}) custom-call(s32[1,256]{1,0:T(1,128)S(1)} %bitcast.13, bf16[256,1024]{1,0:T(8,128)(2,1)S(1)} %copy-done.1, bf16[256,1024]{1,0:T(8,128)(2,1)S(1)} %copy-done.3, bf16[1024,128]{1,0:T(8,128)(2,1)S(1)} %fusion.5.after_ref, f32[256,1024]{1,0:T(8,128)S(1)} %get-tuple-element.25.key_part_ref, ...), custom_call_target="tpu_custom_call" | custom-call | flops 134217728 | bytes 4457472 | tf_op jit(solution)/shard_map/finish_kernel/pallas_call | solution.py:145
  (5 shorter events, 0.1 us)
Async XLA Ops:
  0.6 0.7 %copy-start.7 = (s32[256]{0:T(256)S(1)}, s32[256]{0:T(256)}, u32[]{:S(2)}) copy-start(s32[256]{0:T(256)} %param.11) | copy-start | bytes 3076
  1.3 1.0 %copy-start = (bf16[256,1024]{1,0:T(8,128)(2,1)S(1)}, bf16[256,1024]{1,0:T(8,128)(2,1)}, u32[]{:S(2)}) copy-start(bf16[256,1024]{1,0:T(8,128)(2,1)} %k_ref.7) | copy-start | bytes 1572868
  2.4 1.0 %copy-start.2 = (bf16[256,1024]{1,0:T(8,128)(2,1)S(1)}, bf16[256,1024]{1,0:T(8,128)(2,1)}, u32[]{:S(2)}) copy-start(bf16[256,1024]{1,0:T(8,128)(2,1)} %v_ref.7) | copy-start | bytes 1572868
  3.4 25.6 %copy-start.6 = (bf16[256,1024]{1,0:T(8,128)(2,1)S(1)}, bf16[256,1024]{1,0:T(8,128)(2,1)}, u32[]{:S(2)}) copy-start(bf16[256,1024]{1,0:T(8,128)(2,1)} %c_ref.1) | copy-start | bytes 1572868
  3.9 4.5 %collective-permute-start = (bf16[1056,128]{1,0:T(8,128)(2,1)S(1)}, bf16[1056,128]{1,0:T(8,128)(2,1)S(1)}, u32[]{:S(2)}, u32[]{:S(2)}) collective-permute-start(bf16[1056,128]{1,0:T(8,128)(2,1)S(1)} %tail_kernel.1), channel_id=1, source_target_pairs={{0,4},{4,0},{8,12},{12,8},{16,20},{20,16},{24,28},{28,24},{32,36},... | collective-permute-start | bytes 811016 | tf_op jit(solution)/shard_map/ppermute | solution.py:169
  8.4 20.6 %copy-start.4 = (bf16[256,1024]{1,0:T(8,128)(2,1)S(1)}, bf16[256,1024]{1,0:T(8,128)(2,1)}, u32[]{:S(2)}) copy-start(bf16[256,1024]{1,0:T(8,128)(2,1)} %q_ref.7) | copy-start | bytes 1572868
  8.4 20.6 %copy-start.5 = (bf16[256,1024]{1,0:T(8,128)(2,1)S(1)}, bf16[256,1024]{1,0:T(8,128)(2,1)}, u32[]{:S(2)}) copy-start(bf16[256,1024]{1,0:T(8,128)(2,1)} %g_ref.3) | copy-start | bytes 1572868
  10.3 18.7 %copy-start.1 = (bf16[256,1024]{1,0:T(8,128)(2,1)S(1)}, bf16[256,1024]{1,0:T(8,128)(2,1)}, u32[]{:S(2)}) copy-start(bf16[256,1024]{1,0:T(8,128)(2,1)} %k_ref.7) | copy-start | bytes 1572868
  10.3 18.7 %copy-start.3 = (bf16[256,1024]{1,0:T(8,128)(2,1)S(1)}, bf16[256,1024]{1,0:T(8,128)(2,1)}, u32[]{:S(2)}) copy-start(bf16[256,1024]{1,0:T(8,128)(2,1)} %v_ref.7) | copy-start | bytes 1572868
  10.5 13.2 %collective-permute-start.1 = (bf16[1056,128]{1,0:T(8,128)(2,1)S(1)}, bf16[1056,128]{1,0:T(8,128)(2,1)S(1)}, u32[]{:S(2)}, u32[]{:S(2)}) collective-permute-start(bf16[1056,128]{1,0:T(8,128)(2,1)S(1)} %fusion.2), channel_id=1, source_target_pairs={{0,8},{4,20},{8,16},{12,28},{16,24},{20,36},{24,32},{28,44},{32,40... | collective-permute-start | bytes 811016 | tf_op jit(solution)/shard_map/ppermute | solution.py:173
  25.6 7.0 %collective-permute-start.2 = (bf16[1024,128]{1,0:T(8,128)(2,1)S(1)}, bf16[1024,128]{1,0:T(8,128)(2,1)S(1)}, u32[]{:S(2)}, u32[]{:S(2)}) collective-permute-start(bf16[1024,128]{1,0:T(8,128)(2,1)S(1)} %slice_select_fusion.2), channel_id=1, source_target_pairs={{0,4},{4,0},{8,12},{12,8},{16,20},{20,16},{24,28},{28,24},{32,36},... | collective-permute-start | bytes 786440 | tf_op jit(solution)/shard_map/ppermute | solution.py:169
  33.4 5.7 %collective-permute-start.3 = (f32[2,256]{1,0:T(2,128)S(1)}, f32[2,256]{1,0:T(2,128)S(1)}, u32[]{:S(2)}, u32[]{:S(2)}) collective-permute-start(f32[2,256]{1,0:T(2,128)S(1)} %get-tuple-element.19.s0), channel_id=1, source_target_pairs={{0,2},{1,3},{2,0},{3,1},{4,6},{5,7},{6,4},{7,5},{8,10},{9,11},{10,... | collective-permute-start | bytes 6152 | tf_op jit(solution)/shard_map/ppermute | solution.py:210
  36.4 3.6 %collective-permute-start.4 = (f32[2,256]{1,0:T(2,128)S(1)}, f32[2,256]{1,0:T(2,128)S(1)}, u32[]{:S(2)}, u32[]{:S(2)}) collective-permute-start(f32[2,256]{1,0:T(2,128)S(1)} %get-tuple-element.19.s0), channel_id=1, source_target_pairs={{0,1},{1,2},{2,3},{3,0},{4,5},{5,6},{6,7},{7,4},{8,9},{9,10},{10,1... | collective-permute-start | bytes 6152 | tf_op jit(solution)/shard_map/ppermute | solution.py:210
  36.8 3.3 %collective-permute-start.5 = (f32[2,256]{1,0:T(2,128)S(1)}, f32[2,256]{1,0:T(2,128)S(1)}, u32[]{:S(2)}, u32[]{:S(2)}) collective-permute-start(f32[2,256]{1,0:T(2,128)S(1)} %get-tuple-element.19.s0), channel_id=1, source_target_pairs={{0,3},{1,0},{2,1},{3,2},{4,7},{5,4},{6,5},{7,6},{8,11},{9,8},{10,9... | collective-permute-start | bytes 6152 | tf_op jit(solution)/shard_map/ppermute | solution.py:210
  40.7 2.9 %collective-permute-start.6 = (bf16[1056,128]{1,0:T(8,128)(2,1)S(1)}, bf16[1056,128]{1,0:T(8,128)(2,1)S(1)}, u32[]{:S(2)}, u32[]{:S(2)}) collective-permute-start(bf16[1056,128]{1,0:T(8,128)(2,1)S(1)} %get-tuple-element.24), channel_id=1, source_target_pairs={{0,4},{4,0},{8,12},{12,8},{16,20},{20,16},{24,28},{28,24},{32,36},... | collective-permute-start | bytes 811016 | tf_op jit(solution)/shard_map/ppermute | solution.py:169
  43.9 12.1 %collective-permute-start.7 = (bf16[1056,128]{1,0:T(8,128)(2,1)S(1)}, bf16[1056,128]{1,0:T(8,128)(2,1)S(1)}, u32[]{:S(2)}, u32[]{:S(2)}) collective-permute-start(bf16[1056,128]{1,0:T(8,128)(2,1)S(1)} %fusion.3), channel_id=1, source_target_pairs={{0,248},{4,244},{8,0},{12,252},{16,8},{20,4},{24,16},{28,12},{32,2... | collective-permute-start | bytes 811016 | tf_op jit(solution)/shard_map/ppermute | solution.py:173
  57.8 5.2 %collective-permute-start.8 = (bf16[1024,128]{1,0:T(8,128)(2,1)S(1)}, bf16[1024,128]{1,0:T(8,128)(2,1)S(1)}, u32[]{:S(2)}, u32[]{:S(2)}) collective-permute-start(bf16[1024,128]{1,0:T(8,128)(2,1)S(1)} %slice_select_fusion.1), channel_id=1, source_target_pairs={{0,4},{4,0},{8,12},{12,8},{16,20},{20,16},{24,28},{28,24},{32,36},... | collective-permute-start | bytes 786440 | tf_op jit(solution)/shard_map/ppermute | solution.py:169

commit v2 on v1

--- a/solution.py
+++ b/solution.py
@@ -41,14 +41,70 @@
     out_ref[states + IDS :, :] = first.astype(F32).astype(BF)
 
 
-def tail_kernel(ids_ref, k_ref, v_ref, out_ref):
-    ids = ids_ref[...]
+def last_of(message_ref):
+    states = message_ref.shape[0] - 2 * IDS
+    return message_ref[states : states + IDS, :].astype(F32)[:1]
+
+
+def first_of(message_ref):
+    states = message_ref.shape[0] - 2 * IDS
+    return message_ref[states + IDS :, :].astype(F32)[:1]
+
+
+def tail_kernel(ids_hbm, k_hbm, v_hbm, out_ref, ids_ref, k_ref, v_ref, ids_sem, k_sem, v_sem):
     states = k_ref.shape[1]
+    heads = range(states // HEAD)
+    ids_copy = pltpu.make_async_copy(ids_hbm, ids_ref, ids_sem)
+    k_copies = [pltpu.make_async_copy(k_hbm.at[:, head(h)], k_ref.at[:, head(h)], k_sem.at[h]) for h in heads]
+    v_copies = [pltpu.make_async_copy(v_hbm.at[:, head(h)], v_ref.at[:, head(h)], v_sem.at[h]) for h in heads]
+    ids_copy.start()
+    for h in heads:
+        k_copies[h].start()
+        v_copies[h].start()
+    ids_copy.wait()
+    ids = ids_ref[...]
     hit = (column(ids, HEAD) == ids[:, -1:]).astype(F32).astype(BF)
-    for h in range(states // HEAD):
+    put_ids(ids, out_ref, states)
+    for h in heads:
+        k_copies[h].wait()
+        v_copies[h].wait()
         state = dot(k_ref[:, head(h)] * hit, v_ref[:, head(h)], TN)
         out_ref[head(h), :] = state.astype(BF)
-    put_ids(ids, out_ref, states)
+
+
+def chip_kernel(backward, odd_ref, mine_ref, theirs_ref, out_ref):
+    states = out_ref.shape[0] - 2 * IDS
+    odd = odd_ref[...] > 0
+    kept = ~odd if backward else odd
+    part = first_of if backward else last_of
+    both = part(mine_ref) == part(theirs_ref)
+    for rows in (*(head(h) for h in range(states // HEAD)), slice(states, states + 2 * IDS)):
+        mine, theirs = mine_ref[rows, :].astype(F32), theirs_ref[rows, :].astype(F32)
+        chosen = jnp.where(kept, mine, theirs)
+        if rows.start < states:
+            chosen = jnp.where(both, mine + theirs, chosen)
+        out_ref[rows, :] = chosen.astype(BF)
+
+
+def joined(backward, odd_ref, mine_ref, theirs_ref, came_ref, other_ref):
+    odd = odd_ref[...] > 0
+    part = first_of if backward else last_of
+    far = last_of if backward else first_of
+    inner = ~odd if backward else odd
+    mine_near, mine_far = part(mine_ref), far(mine_ref)
+    theirs_near, theirs_far = part(theirs_ref), far(theirs_ref)
+    edge = jnp.where(inner, theirs_far, mine_far)
+    take_came, take_other = part(came_ref) == edge, part(other_ref) == edge
+    take_theirs = inner & (theirs_near == mine_far)
+    take_outer = ~inner | (take_theirs & (theirs_near == theirs_far))
+
+    def rows_of(rows):
+        outer = jnp.where(take_came, came_ref[rows, :].astype(F32), 0.0)
+        outer = outer + jnp.where(take_other, other_ref[rows, :].astype(F32), 0.0)
+        own = jnp.where(take_theirs, theirs_ref[rows, :].astype(F32), 0.0)
+        return (own + jnp.where(take_outer, outer, 0.0)).astype(BF)
+
+    return rows_of
 
 
 def local_kernel(ids_ref, q_ref, k_ref, v_ref, g_ref, c_ref, scores_ref, local_ref, up_ref):
@@ -66,14 +122,20 @@
         up_ref[:, head(h)] = c_ref[:, head(h)].astype(F32) * gate
 
 
-def attend_kernel(ids_ref, q_ref, before_ref, local_ref, up_ref, attended_ref, sums_ref):
+def attend_kernel(
+    ids_ref, odd_ref, mine_ref, theirs_ref, came_ref, other_ref, q_ref, local_ref, up_ref,
+    before_ref, attended_ref, sums_ref,
+):
     ids = ids_ref[...]
     length = ids.shape[1]
+    entering = joined(False, odd_ref, mine_ref, theirs_ref, came_ref, other_ref)
     hit = (column(ids, HEAD) == ids[:, :1]).astype(F32).astype(BF)
     square = jnp.zeros((length, HEAD), F32)
     cross = jnp.zeros((length, HEAD), F32)
     for h in range(q_ref.shape[1] // HEAD):
-        attended = local_ref[:, head(h)] + dot(q_ref[:, head(h)] * hit, before_ref[head(h), :], NN)
+        before = entering(head(h))
+        before_ref[head(h), :] = before
+        attended = local_ref[:, head(h)] + dot(q_ref[:, head(h)] * hit, before, NN)
         attended_ref[:, head(h)] = attended
         square = square + attended * attended
         cross = cross + up_ref[:, head(h)] * attended
@@ -128,42 +190,60 @@
         gate_grad_ref[:, head(h)] = gate_grad.astype(BF)
 
 
-def finish_kernel(ids_ref, k_ref, v_ref, after_ref, key_part_ref, value_part_ref, key_grad_ref, value_grad_ref):
-    ids = ids_ref[...]
+def finish_kernel(
+    ids_ref, odd_ref, mine_ref, theirs_ref, came_ref, other_ref, k_ref, v_ref, key_part_ref, value_part_ref,
+    key_grad_hbm, value_grad_hbm, key_grad_ref, value_grad_ref, key_sem, value_sem,
+):
+    ids = ids_ref[...]
+    leaving = joined(True, odd_ref, mine_ref, theirs_ref, came_ref, other_ref)
     hit = (column(ids, HEAD) == ids[:, -1:]).astype(F32).astype(BF)
+    copies = []
     for h in range(k_ref.shape[1] // HEAD):
-        after = after_ref[head(h), :]
+        after = leaving(head(h))
         key_grad = key_part_ref[:, head(h)] + dot(v_ref[:, head(h)] * hit, after, NT)
         key_grad_ref[:, head(h)] = key_grad.astype(BF)
+        copies.append(pltpu.make_async_copy(key_grad_ref.at[:, head(h)], key_grad_hbm.at[:, head(h)], key_sem.at[h]))
+        copies[-1].start()
         value_grad = value_part_ref[:, head(h)] + dot(k_ref[:, head(h)] * hit, after, NN)
         value_grad_ref[:, head(h)] = value_grad.astype(BF)
-
-
-def call(kernel, outs, flops, *args):
-    whole = pl.BlockSpec(memory_space=pltpu.VMEM)
+        copies.append(
+            pltpu.make_async_copy(value_grad_ref.at[:, head(h)], value_grad_hbm.at[:, head(h)], value_sem.at[h])
+        )
+        copies[-1].start()
+    for copy in copies:
+        copy.wait()
+
+
+VMEM = pl.BlockSpec(memory_space=pltpu.VMEM)
+HBM = pl.BlockSpec(memory_space=pltpu.HBM)
+
+
+def call(kernel, outs, flops, *args, name=None, in_specs=None, out_specs=None, scratch=(), vmem=24 * MIB):
     size = sum(a.size * a.dtype.itemsize for a in (*args, *outs))
     return pl.pallas_call(
         kernel,
         out_shape=outs,
-        in_specs=[whole] * len(args),
-        out_specs=[whole] * len(outs),
-        compiler_params=pltpu.CompilerParams(vmem_limit_bytes=24 * MIB),
+        in_specs=in_specs or [VMEM] * len(args),
+        out_specs=out_specs or [VMEM] * len(outs),
+        scratch_shapes=scratch,
+        compiler_params=pltpu.CompilerParams(vmem_limit_bytes=vmem),
         cost_estimate=pl.CostEstimate(flops=flops, bytes_accessed=size, transcendentals=0),
-        name=kernel.__name__,
+        name=name or kernel.__name__,
     )(*args)
 
 
 def body(queries, keys, values, gates, cotangent, doc_ids):
     length, states = queries.shape
-    count = lax.axis_size("ctx")
+    count, ranks = lax.axis_size("ctx"), lax.axis_size("tp")
     heads = states // HEAD
     shape = jax.ShapeDtypeStruct
     ids = doc_ids.reshape(1, length)
-    odd = lax.rem(lax.axis_index("ctx"), 2) == 1
+    odd = jnp.broadcast_to(lax.rem(lax.axis_index("ctx"), 2), (1, HEAD))
     message = shape((states + 2 * IDS, HEAD), BF)
     wide = shape((length, states), F32)
     narrow = shape((length, states), BF)
     unit = 2 * length * length * states
+    buffer, sems = pltpu.VMEM((length, states), BF), pltpu.SemaphoreType.DMA((heads,))
 
     def swap(x):
         return lax.ppermute(x, "ctx", [(i, i ^ 1) for i in range(count)])
@@ -172,65 +252,42 @@
         pairs = [(i, (i + way * (2 if i % 2 == 0 else 4)) % count) for i in range(count)]
         return lax.ppermute(x, "ctx", pairs)
 
-    def add(a, b):
-        return (a.astype(F32) + b.astype(F32)).astype(BF)
-
-    is_state = lax.broadcasted_iota(jnp.int32, message.shape, 0) < states
-
-    def last_of(m):
-        return m[states, 0]
-
-    def first_of(m):
-        return m[states + IDS, 0]
-
-    (mine,) = call(tail_kernel, [message], unit // 2, ids, keys, values)
-    theirs = swap(mine)
-    even_part, odd_part = jnp.where(odd, theirs, mine), jnp.where(odd, mine, theirs)
-    first_even, last_even = first_of(even_part), last_of(even_part)
-    first_odd, last_odd = first_of(odd_part), last_of(odd_part)
-    chip = jnp.where(is_state & (last_even == last_odd), add(mine, theirs), odd_part)
+    (tail,) = call(
+        tail_kernel, [message], unit // 2, ids, keys, values, in_specs=[HBM] * 3,
+        scratch=[pltpu.VMEM((1, length), jnp.int32), buffer, buffer, pltpu.SemaphoreType.DMA, sems, sems], vmem=int(53.5 * MIB),
+    )
+    tail_other = swap(tail)
+    (chip,) = call(functools.partial(chip_kernel, False), [message], 0, odd, tail, tail_other, name="chip_tail")
     came = spread(chip, 1)
+    ids, _ = lax.optimization_barrier((ids, chip))
     scores, local, up = call(
         local_kernel, [shape((heads, length, length), BF), wide, wide], 2 * unit, ids, queries, keys, values, gates, cotangent
     )
-    came = jnp.where(last_of(came) == first_even, came[:states], 0)
-    entering = add(came, swap(came))
-    before = jnp.where(
-        odd,
-        jnp.where(
-            first_odd == last_even,
-            jnp.where(first_even == last_even, add(even_part[:states], entering), even_part[:states]),
-            0,
-        ),
-        entering,
-    )
-    attended, sums = call(attend_kernel, [wide, shape((2, length), F32)], unit // 2, ids, queries, before, local, up)
-    ranks = lax.axis_size("tp")
+    came, local = lax.optimization_barrier((came, local))
+    other = swap(came)
+    before, attended, sums = call(
+        attend_kernel, [shape((states, HEAD), BF), wide, shape((2, length), F32)], unit // 2,
+        ids, odd, tail, tail_other, came, other, queries, local, up,
+    )
     parts = [sums] + [
         lax.ppermute(sums, "tp", [(i, (i + step) % ranks) for i in range(ranks)]) for step in (2, 1, 3)
     ]
     grad, lead = call(lead_kernel, [narrow, message], unit // 2, ids, *parts, queries, attended, up)
 
-    other = swap(lead)
-    lead_even, lead_odd = jnp.where(odd, other, lead), jnp.where(odd, lead, other)
-    chip = jnp.where(is_state & (first_even == first_odd), add(lead, other), lead_even)
+    lead_other = swap(lead)
+    (chip,) = call(functools.partial(chip_kernel, True), [message], 0, odd, lead, lead_other, name="chip_lead")
     came = spread(chip, -1)
+    ids, _ = lax.optimization_barrier((ids, chip))
     query_grad, gate_grad, key_part, value_part = call(
         back_kernel, [narrow, narrow, wide, wide], 5 * unit, ids, *parts, queries, keys, values, gates, scores, attended,
         up, grad, before,
     )
-    came = jnp.where(first_of(came) == last_odd, came[:states], 0)
-    leaving = add(came, swap(came))
-    after = jnp.where(
-        odd,
-        leaving,
-        jnp.where(
-            first_odd == last_even,
-            jnp.where(first_odd == last_odd, add(lead_odd[:states], leaving), lead_odd[:states]),
-            0,
-        ),
-    )
-    key_grad, value_grad = call(finish_kernel, [narrow, narrow], unit, ids, keys, values, after, key_part, value_part)
+    came, key_part = lax.optimization_barrier((came, key_part))
+    other = swap(came)
+    key_grad, value_grad = call(
+        finish_kernel, [narrow, narrow], unit, ids, odd, lead, lead_other, came, other, keys, values, key_part, value_part,
+        out_specs=[HBM] * 2, scratch=[buffer, buffer, sems, sems],
+    )
     return query_grad, key_grad, value_grad, gate_grad
 
 

time: 65.1 us -> 52.8 us (0.81)
  between operations: 9.87 us -> 0.7 us
  local copies, waits for them, and re-layouts: 4.39 us -> 1.73 us
  Pallas kernels: 7.89 us -> 10.4 us
  other arithmetic: 1 us -> 0 us
  starting transfers between devices: 17.9 us -> 16.9 us
  waiting for transfers between devices: 23.6 us -> 22.9 us
    ppermute x2, waiting for transfers between devices: 21.5 us -> 15.7 us  [spread(): return lax.ppermute(x, 'ctx', pairs)]
    ppermute x4, waiting for transfers between devices: 1.18 us -> 4.94 us  [swap(): return lax.ppermute(x, 'ctx', [(i, i ^ 1) for i in range(count)])]
    pallas_call x6 -> x8, Pallas kernels: 7.89 us -> 10.4 us  [call(): pl.pallas_call(kernel, out_shape=outs, in_specs=in_specs or [VMEM] * len(...]
    slice x3 -> x0, local copies, waits for them, and re-layouts: 1.61 us -> none  [the longest x2 1.04 us: first_of(): return m[states + IDS, 0]]
    ppermute x3, waiting for transfers between devices: 0.97 us -> 2.3 us  [body(): lax.ppermute(sums, 'tp', [(i, (i + step) % ranks) for i in range(ranks)])]
    ppermute x3, starting transfers between devices: 5.67 us -> 4.46 us  [body(): lax.ppermute(sums, 'tp', [(i, (i + step) % ranks) for i in range(ranks)])]
    unnamed x16 -> x12, local copies, waits for them, and re-layouts: 2.78 us -> 1.73 us
    select_n x7 -> x0, other arithmetic: 0.98 us -> none  [the longest x1 0.26 us: body(): jnp.where(is_state & (last_even == last_odd), add(mine, theirs), odd_part)]
  transfers between devices with their start and end apart: 9 -> 9, of which waited for: 4 -> 8; matrix products, arithmetic and copies ran while one was open for 0% -> 0% of each run, Pallas kernels for 7% -> 9%
where the time goes in v2:
time: 52.8 us; the launch traced here: 52.6 us
  waiting for transfers between devices  22.9 us (43%)
  starting transfers between devices  16.9 us (32%)
  Pallas kernels  10.4 us (20%)
  local copies, waits for them, and re-layouts  1.73 us (3%)
  between operations  0.7 us (1%)
    ppermute x2, waiting for transfers between devices, spread(): return lax.ppermute(x, 'ctx', pairs)  15.7 us
    pallas_call x8, Pallas kernels, call(): pl.pallas_call(kernel, out_shape=outs, in_specs=in_specs or [VMEM] * len(...  10.4 us
    ppermute x4, starting transfers between devices, swap(): return lax.ppermute(x, 'ctx', [(i, i ^ 1) for i in range(count)])  8.63 us
    ppermute x4, waiting for transfers between devices, swap(): return lax.ppermute(x, 'ctx', [(i, i ^ 1) for i in range(count)])  4.94 us
    ppermute x3, starting transfers between devices, body(): lax.ppermute(sums, 'tp', [(i, (i + step) % ranks) for i in range(ranks)])  4.46 us
    ppermute x2, starting transfers between devices, spread(): return lax.ppermute(x, 'ctx', pairs)  3.77 us
    ppermute x3, waiting for transfers between devices, body(): lax.ppermute(sums, 'tp', [(i, (i + step) % ranks) for i in range(ranks)])  2.3 us
    unnamed x12, local copies, waits for them, and re-layouts  1.73 us
  transfers between devices with their start and end apart: 9, of which 8 were waited for; matrix products, arithmetic and copies ran while one was open for 0% of the time, Pallas kernels for 9%

profile of v2, /device:TPU:1, one launch (start us, length us, event | category | flops | bytes accessed | tf_op | source)
XLA Modules:
  0.0 52.6 jit_solution(11962453009686444598)
XLA Ops:
  0.6 0.0 copy-start.5
  0.6 0.7 %copy-done.5 = s32[256]{0:T(256)S(1)} copy-done((s32[256]{0:T(256)S(1)}, s32[256]{0:T(256)}, u32[]{:S(2)}) %copy-start.5) | copy-done | bytes 1048
  1.3 0.0 copy-start.1
  1.3 0.0 copy-start.2
  1.3 0.0 copy-start.3
  1.3 2.9 %tail_kernel.1.mine_ref = bf16[1056,128]{1,0:T(8,128)(2,1)S(1)} custom-call(s32[1,256]{1,0:T(1,128)S(1)} %bitcast.1, bf16[256,1024]{1,0:T(8,128)(2,1)} %k_ref.5, bf16[256,1024]{1,0:T(8,128)(2,1)} %v_ref.5), custom_call_target="tpu_custom_call" | custom-call | flops 67108864 | bytes 1319936 | tf_op jit(solution)/shard_map/tail_kernel/pallas_call | solution.py:223
  4.2 0.0 copy-start
  4.2 3.3 %collective-permute-start = (bf16[1056,128]{1,0:T(8,128)(2,1)S(1)}, bf16[1056,128]{1,0:T(8,128)(2,1)S(1)}, u32[]{:S(2)}, u32[]{:S(2)}) collective-permute-start(bf16[1056,128]{1,0:T(8,128)(2,1)S(1)} %tail_kernel.1.mine_ref), channel_id=1, source_target_pairs={{0,4},{4,0},{8,12},{12,8},{16,20},{20,16},{24,28},{28,24},{32,36},... | collective-permute-start | bytes 811016 | tf_op jit(solution)/shard_map/ppermute | solution.py:249
  7.6 1.2 %collective-permute-done.theirs_ref = bf16[1056,128]{1,0:T(8,128)(2,1)S(1)} collective-permute-done((bf16[1056,128]{1,0:T(8,128)(2,1)S(1)}, bf16[1056,128]{1,0:T(8,128)(2,1)S(1)}, u32[]{:S(2)}, u32[]{:S(2)}) %collective-permute-start) | collective-permute-done | bytes 270368 | tf_op jit(solution)/shard_map/ppermute | solution.py:249
  8.7 0.1 chip_tail.1
  8.8 1.3 %collective-permute-start.1 = (bf16[1056,128]{1,0:T(8,128)(2,1)S(1)}, bf16[1056,128]{1,0:T(8,128)(2,1)S(1)}, u32[]{:S(2)}, u32[]{:S(2)}) collective-permute-start(bf16[1056,128]{1,0:T(8,128)(2,1)S(1)} %chip_tail.1), channel_id=1, source_target_pairs={{0,8},{4,20},{8,16},{12,28},{16,24},{20,36},{24,32},{28,44},{32,40... | collective-permute-start | bytes 811016 | tf_op jit(solution)/shard_map/ppermute | solution.py:253
  10.2 0.0 copy-done.1
  10.2 0.0 copy-done.2
  10.2 0.0 copy-done.3
  10.2 0.0 copy-done
  10.2 0.0 copy-start.4
  10.2 1.0 %copy-done.4 = bf16[256,1024]{1,0:T(8,128)(2,1)S(1)} copy-done((bf16[256,1024]{1,0:T(8,128)(2,1)S(1)}, bf16[256,1024]{1,0:T(8,128)(2,1)}, u32[]{:S(2)}) %copy-start.4) | copy-done | bytes 524312
  11.2 1.1 %local_kernel.1 = (bf16[8,256,256]{2,1,0:T(8,128)(2,1)S(1)}, f32[256,1024]{1,0:T(8,128)S(1)}, f32[256,1024]{1,0:T(8,128)S(1)}) custom-call(s32[1,256]{1,0:T(1,128)S(1)} %bitcast.2, bf16[256,1024]{1,0:T(8,128)(2,1)S(1)} %copy-done.2, bf16[256,1024]{1,0:T(8,128)(2,1)S(1)} %copy-done, bf16[256,1024]{1,0:T(8,128)(2,1)S(1)} %copy-done.1, ...), custom_call_target="tpu_custom_call" | custom-call | flops 268435456 | bytes 5768192 | tf_op jit(solution)/shard_map/local_kernel/pallas_call | solution.py:223
  12.3 9.7 %collective-permute-done.1.came_ref = bf16[1056,128]{1,0:T(8,128)(2,1)S(1)} collective-permute-done((bf16[1056,128]{1,0:T(8,128)(2,1)S(1)}, bf16[1056,128]{1,0:T(8,128)(2,1)S(1)}, u32[]{:S(2)}, u32[]{:S(2)}) %collective-permute-start.1) | collective-permute-done | bytes 270368 | tf_op jit(solution)/shard_map/ppermute | solution.py:253
  22.0 3.3 %collective-permute-start.2 = (bf16[1056,128]{1,0:T(8,128)(2,1)S(1)}, bf16[1056,128]{1,0:T(8,128)(2,1)S(1)}, u32[]{:S(2)}, u32[]{:S(2)}) collective-permute-start(bf16[1056,128]{1,0:T(8,128)(2,1)S(1)} %collective-permute-done.1.came_ref), channel_id=1, source_target_pairs={{0,4},{4,0},{8,12},{12,8},{16,20},{20,16},{24,28},{28,24},{32,36},... | collective-permute-start | bytes 811016 | tf_op jit(solution)/shard_map/ppermute | solution.py:249
  25.3 1.2 %collective-permute-done.2.other_ref = bf16[1056,128]{1,0:T(8,128)(2,1)S(1)} collective-permute-done((bf16[1056,128]{1,0:T(8,128)(2,1)S(1)}, bf16[1056,128]{1,0:T(8,128)(2,1)S(1)}, u32[]{:S(2)}, u32[]{:S(2)}) %collective-permute-start.2) | collective-permute-done | bytes 270368 | tf_op jit(solution)/shard_map/ppermute | solution.py:249
  26.5 0.6 %attend_kernel.1 = (bf16[1024,128]{1,0:T(8,128)(2,1)S(1)}, f32[256,1024]{1,0:T(8,128)S(1)}, f32[2,256]{1,0:T(2,128)S(1)}) custom-call(s32[1,256]{1,0:T(1,128)S(1)} %bitcast.3, s32[1,128]{1,0:T(1,128)S(1)} %broadcast_in_dim.3.odd_ref, bf16[1056,128]{1,0:T(8,128)(2,1)S(1)} %tail_kernel.1.mine_ref, bf16[1056,128]{1,0:T(8,128)(2,1)S(1)} %collective-permute-done.theirs_ref, ...), custom_call_target="tpu_custom_call" | custom-call | flops 67108864 | bytes 5017088 | tf_op jit(solution)/shard_map/attend_kernel/pallas_call | solution.py:223
  27.1 2.8 %collective-permute-start.5 = (f32[2,256]{1,0:T(2,128)S(1)}, f32[2,256]{1,0:T(2,128)S(1)}, u32[]{:S(2)}, u32[]{:S(2)}) collective-permute-start(f32[2,256]{1,0:T(2,128)S(1)} %get-tuple-element.29.s0), channel_id=1, source_target_pairs={{0,3},{1,0},{2,1},{3,2},{4,7},{5,4},{6,5},{7,6},{8,11},{9,8},{10,9... | collective-permute-start | bytes 6152 | tf_op jit(solution)/shard_map/ppermute | solution.py:273
  29.9 0.0 collective-permute-start.4
  29.9 1.6 %collective-permute-start.3 = (f32[2,256]{1,0:T(2,128)S(1)}, f32[2,256]{1,0:T(2,128)S(1)}, u32[]{:S(2)}, u32[]{:S(2)}) collective-permute-start(f32[2,256]{1,0:T(2,128)S(1)} %get-tuple-element.29.s0), channel_id=1, source_target_pairs={{0,2},{1,3},{2,0},{3,1},{4,6},{5,7},{6,4},{7,5},{8,10},{9,11},{10,... | collective-permute-start | bytes 6152 | tf_op jit(solution)/shard_map/ppermute | solution.py:273
  31.6 0.0 collective-permute-done.5.s3
  31.6 2.0 %collective-permute-done.4.s2 = f32[2,256]{1,0:T(2,128)S(1)} collective-permute-done((f32[2,256]{1,0:T(2,128)S(1)}, f32[2,256]{1,0:T(2,128)S(1)}, u32[]{:S(2)}, u32[]{:S(2)}) %collective-permute-start.4) | collective-permute-done | bytes 2080 | tf_op jit(solution)/shard_map/ppermute | solution.py:273
  33.6 0.3 collective-permute-done.3.s1
  33.8 0.6 %lead_kernel.1 = (bf16[256,1024]{1,0:T(8,128)(2,1)S(1)}, bf16[1056,128]{1,0:T(8,128)(2,1)S(1)}) custom-call(s32[1,256]{1,0:T(1,128)S(1)} %bitcast.4, f32[2,256]{1,0:T(2,128)S(1)} %get-tuple-element.29.s0, f32[2,256]{1,0:T(2,128)S(1)} %collective-permute-done.3.s1, f32[2,256]{1,0:T(2,128)S(1)} %collective-permute-done.4.s2, ...), custom_call_target="tpu_custom_call" | custom-call | flops 67108864 | bytes 3425280 | tf_op jit(solution)/shard_map/lead_kernel/pallas_call | solution.py:223
  34.5 1.9 %collective-permute-start.6 = (bf16[1056,128]{1,0:T(8,128)(2,1)S(1)}, bf16[1056,128]{1,0:T(8,128)(2,1)S(1)}, u32[]{:S(2)}, u32[]{:S(2)}) collective-permute-start(bf16[1056,128]{1,0:T(8,128)(2,1)S(1)} %get-tuple-element.31.mine_ref), channel_id=1, source_target_pairs={{0,4},{4,0},{8,12},{12,8},{16,20},{20,16},{24,28},{28,24},{32,36},... | collective-permute-start | bytes 811016 | tf_op jit(solution)/shard_map/ppermute | solution.py:249
  36.3 1.2 %collective-permute-done.6.theirs_ref = bf16[1056,128]{1,0:T(8,128)(2,1)S(1)} collective-permute-done((bf16[1056,128]{1,0:T(8,128)(2,1)S(1)}, bf16[1056,128]{1,0:T(8,128)(2,1)S(1)}, u32[]{:S(2)}, u32[]{:S(2)}) %collective-permute-start.6) | collective-permute-done | bytes 270368 | tf_op jit(solution)/shard_map/ppermute | solution.py:249
  37.5 0.1 chip_lead.1
  37.6 2.4 %collective-permute-start.7 = (bf16[1056,128]{1,0:T(8,128)(2,1)S(1)}, bf16[1056,128]{1,0:T(8,128)(2,1)S(1)}, u32[]{:S(2)}, u32[]{:S(2)}) collective-permute-start(bf16[1056,128]{1,0:T(8,128)(2,1)S(1)} %chip_lead.1), channel_id=1, source_target_pairs={{0,248},{4,244},{8,0},{12,252},{16,8},{20,4},{24,16},{28,12},{32,2... | collective-permute-start | bytes 811016 | tf_op jit(solution)/shard_map/ppermute | solution.py:253
  40.1 3.6 %back_kernel.1 = (bf16[256,1024]{1,0:T(8,128)(2,1)}, bf16[256,1024]{1,0:T(8,128)(2,1)}, f32[256,1024]{1,0:T(8,128)S(1)}, f32[256,1024]{1,0:T(8,128)S(1)}) custom-call(s32[1,256]{1,0:T(1,128)S(1)} %bitcast.5, f32[2,256]{1,0:T(2,128)S(1)} %get-tuple-element.29.s0, f32[2,256]{1,0:T(2,128)S(1)} %collective-permute-done.3.s1, ...), custom_call_target="tpu_custom_call" | custom-call | flops 671088640 | bytes 9184256 | tf_op jit(solution)/shard_map/back_kernel/pallas_call | solution.py:223
  43.6 6.0 %collective-permute-done.7.came_ref = bf16[1056,128]{1,0:T(8,128)(2,1)S(1)} collective-permute-done((bf16[1056,128]{1,0:T(8,128)(2,1)S(1)}, bf16[1056,128]{1,0:T(8,128)(2,1)S(1)}, u32[]{:S(2)}, u32[]{:S(2)}) %collective-permute-start.7) | collective-permute-done | bytes 270368 | tf_op jit(solution)/shard_map/ppermute | solution.py:253
  49.6 0.1 collective-permute-start.8
  49.8 1.4 %collective-permute-done.8.other_ref = bf16[1056,128]{1,0:T(8,128)(2,1)S(1)} collective-permute-done((bf16[1056,128]{1,0:T(8,128)(2,1)S(1)}, bf16[1056,128]{1,0:T(8,128)(2,1)S(1)}, u32[]{:S(2)}, u32[]{:S(2)}) %collective-permute-start.8) | collective-permute-done | bytes 270368 | tf_op jit(solution)/shard_map/ppermute | solution.py:249
  51.2 1.5 %finish_kernel.1 = (bf16[256,1024]{1,0:T(8,128)(2,1)}, bf16[256,1024]{1,0:T(8,128)(2,1)}) custom-call(s32[1,256]{1,0:T(1,128)S(1)} %bitcast.6, s32[1,128]{1,0:T(1,128)S(1)} %broadcast_in_dim.3.odd_ref, bf16[1056,128]{1,0:T(8,128)(2,1)S(1)} %get-tuple-element.31.mine_ref, bf16[1056,128]{1,0:T(8,128)(2,1)S(1)} %collective-permute-done.6.theirs_ref, ...), custom_call_target="tpu_custom_call" | custom-call | flops 134217728 | bytes 5277184 | tf_op jit(solution)/shard_map/finish_kernel/pallas_call | solution.py:223
  (1 shorter events, 0.0 us)
Async XLA Ops:
  0.6 0.7 %copy-start.5 = (s32[256]{0:T(256)S(1)}, s32[256]{0:T(256)}, u32[]{:S(2)}) copy-start(s32[256]{0:T(256)} %param.11) | copy-start | bytes 3076
  1.3 8.9 %copy-start.1 = (bf16[256,1024]{1,0:T(8,128)(2,1)S(1)}, bf16[256,1024]{1,0:T(8,128)(2,1)}, u32[]{:S(2)}) copy-start(bf16[256,1024]{1,0:T(8,128)(2,1)} %v_ref.5) | copy-start | bytes 1572868
  1.3 8.9 %copy-start.2 = (bf16[256,1024]{1,0:T(8,128)(2,1)S(1)}, bf16[256,1024]{1,0:T(8,128)(2,1)}, u32[]{:S(2)}) copy-start(bf16[256,1024]{1,0:T(8,128)(2,1)} %q_ref.7) | copy-start | bytes 1572868
  1.3 8.9 %copy-start.3 = (bf16[256,1024]{1,0:T(8,128)(2,1)S(1)}, bf16[256,1024]{1,0:T(8,128)(2,1)}, u32[]{:S(2)}) copy-start(bf16[256,1024]{1,0:T(8,128)(2,1)} %g_ref.3) | copy-start | bytes 1572868
  4.2 6.0 %copy-start = (bf16[256,1024]{1,0:T(8,128)(2,1)S(1)}, bf16[256,1024]{1,0:T(8,128)(2,1)}, u32[]{:S(2)}) copy-start(bf16[256,1024]{1,0:T(8,128)(2,1)} %k_ref.5) | copy-start | bytes 1572868
  4.2 4.5 %collective-permute-start = (bf16[1056,128]{1,0:T(8,128)(2,1)S(1)}, bf16[1056,128]{1,0:T(8,128)(2,1)S(1)}, u32[]{:S(2)}, u32[]{:S(2)}) collective-permute-start(bf16[1056,128]{1,0:T(8,128)(2,1)S(1)} %tail_kernel.1.mine_ref), channel_id=1, source_target_pairs={{0,4},{4,0},{8,12},{12,8},{16,20},{20,16},{24,28},{28,24},{32,36},... | collective-permute-start | bytes 811016 | tf_op jit(solution)/shard_map/ppermute | solution.py:249
  8.8 13.2 %collective-permute-start.1 = (bf16[1056,128]{1,0:T(8,128)(2,1)S(1)}, bf16[1056,128]{1,0:T(8,128)(2,1)S(1)}, u32[]{:S(2)}, u32[]{:S(2)}) collective-permute-start(bf16[1056,128]{1,0:T(8,128)(2,1)S(1)} %chip_tail.1), channel_id=1, source_target_pairs={{0,8},{4,20},{8,16},{12,28},{16,24},{20,36},{24,32},{28,44},{32,40... | collective-permute-start | bytes 811016 | tf_op jit(solution)/shard_map/ppermute | solution.py:253
  10.2 1.0 %copy-start.4 = (bf16[256,1024]{1,0:T(8,128)(2,1)S(1)}, bf16[256,1024]{1,0:T(8,128)(2,1)}, u32[]{:S(2)}) copy-start(bf16[256,1024]{1,0:T(8,128)(2,1)} %c_ref.1) | copy-start | bytes 1572868
  22.0 4.5 %collective-permute-start.2 = (bf16[1056,128]{1,0:T(8,128)(2,1)S(1)}, bf16[1056,128]{1,0:T(8,128)(2,1)S(1)}, u32[]{:S(2)}, u32[]{:S(2)}) collective-permute-start(bf16[1056,128]{1,0:T(8,128)(2,1)S(1)} %collective-permute-done.1.came_ref), channel_id=1, source_target_pairs={{0,4},{4,0},{8,12},{12,8},{16,20},{20,16},{24,28},{28,24},{32,36},... | collective-permute-start | bytes 811016 | tf_op jit(solution)/shard_map/ppermute | solution.py:249
  27.1 4.5 %collective-permute-start.5 = (f32[2,256]{1,0:T(2,128)S(1)}, f32[2,256]{1,0:T(2,128)S(1)}, u32[]{:S(2)}, u32[]{:S(2)}) collective-permute-start(f32[2,256]{1,0:T(2,128)S(1)} %get-tuple-element.29.s0), channel_id=1, source_target_pairs={{0,3},{1,0},{2,1},{3,2},{4,7},{5,4},{6,5},{7,6},{8,11},{9,8},{10,9... | collective-permute-start | bytes 6152 | tf_op jit(solution)/shard_map/ppermute | solution.py:273
  29.9 3.6 %collective-permute-start.4 = (f32[2,256]{1,0:T(2,128)S(1)}, f32[2,256]{1,0:T(2,128)S(1)}, u32[]{:S(2)}, u32[]{:S(2)}) collective-permute-start(f32[2,256]{1,0:T(2,128)S(1)} %get-tuple-element.29.s0), channel_id=1, source_target_pairs={{0,1},{1,2},{2,3},{3,0},{4,5},{5,6},{6,7},{7,4},{8,9},{9,10},{10,1... | collective-permute-start | bytes 6152 | tf_op jit(solution)/shard_map/ppermute | solution.py:273
  29.9 3.9 %collective-permute-start.3 = (f32[2,256]{1,0:T(2,128)S(1)}, f32[2,256]{1,0:T(2,128)S(1)}, u32[]{:S(2)}, u32[]{:S(2)}) collective-permute-start(f32[2,256]{1,0:T(2,128)S(1)} %get-tuple-element.29.s0), channel_id=1, source_target_pairs={{0,2},{1,3},{2,0},{3,1},{4,6},{5,7},{6,4},{7,5},{8,10},{9,11},{10,... | collective-permute-start | bytes 6152 | tf_op jit(solution)/shard_map/ppermute | solution.py:273
  34.5 3.1 %collective-permute-start.6 = (bf16[1056,128]{1,0:T(8,128)(2,1)S(1)}, bf16[1056,128]{1,0:T(8,128)(2,1)S(1)}, u32[]{:S(2)}, u32[]{:S(2)}) collective-permute-start(bf16[1056,128]{1,0:T(8,128)(2,1)S(1)} %get-tuple-element.31.mine_ref), channel_id=1, source_target_pairs={{0,4},{4,0},{8,12},{12,8},{16,20},{20,16},{24,28},{28,24},{32,36},... | collective-permute-start | bytes 811016 | tf_op jit(solution)/shard_map/ppermute | solution.py:249
  37.6 12.0 %collective-permute-start.7 = (bf16[1056,128]{1,0:T(8,128)(2,1)S(1)}, bf16[1056,128]{1,0:T(8,128)(2,1)S(1)}, u32[]{:S(2)}, u32[]{:S(2)}) collective-permute-start(bf16[1056,128]{1,0:T(8,128)(2,1)S(1)} %chip_lead.1), channel_id=1, source_target_pairs={{0,248},{4,244},{8,0},{12,252},{16,8},{20,4},{24,16},{28,12},{32,2... | collective-permute-start | bytes 811016 | tf_op jit(solution)/shard_map/ppermute | solution.py:253
  49.6 1.5 %collective-permute-start.8 = (bf16[1056,128]{1,0:T(8,128)(2,1)S(1)}, bf16[1056,128]{1,0:T(8,128)(2,1)S(1)}, u32[]{:S(2)}, u32[]{:S(2)}) collective-permute-start(bf16[1056,128]{1,0:T(8,128)(2,1)S(1)} %collective-permute-done.7.came_ref), channel_id=1, source_target_pairs={{0,4},{4,0},{8,12},{12,8},{16,20},{20,16},{24,28},{28,24},{32,36},... | collective-permute-start | bytes 811016 | tf_op jit(solution)/shard_map/ppermute | solution.py:249

commit v3 on v2

v3 whole, which is shorter than its diff:
```python
import functools

import jax
import jax.numpy as jnp
from jax import lax
from jax.experimental import pallas as pl
from jax.experimental.pallas import tpu as pltpu
from jax.sharding import PartitionSpec as P

HEADS = 32
HEAD = 128
EPSILON = 1e-06
FEATURES = HEADS * HEAD
BF = jnp.bfloat16
F32 = jnp.float32
IDS = 8
MIB = 1 << 20


def dot(a, b, dims):
    return lax.dot_general(a, b, (dims, ((), ())), preferred_element_type=F32)


NN = ((1,), (0,))
NT = ((1,), (1,))
TN = ((0,), (0,))


def head(h):
    return slice(h * HEAD, (h + 1) * HEAD)


def column(row, lanes):
    return jnp.broadcast_to(row, (lanes, row.shape[1])).T


def put_ids(ids, out_ref):
    last = jnp.broadcast_to(ids[:, -1:], (IDS, HEAD))
    first = jnp.broadcast_to(ids[:, :1], (IDS, HEAD))
    out_ref[-2 * IDS :, :] = jnp.concatenate([last, first]).astype(F32).astype(BF)


def get_ids(message_ref):
    ids = message_ref[-2 * IDS :, :].astype(F32)
    return ids[:1], ids[IDS : IDS + 1]


def load_kernel(k_hbm, v_hbm, k_ref, v_ref, sems):
    k_copy = pltpu.make_async_copy(k_hbm, k_ref, sems.at[0])
    v_copy = pltpu.make_async_copy(v_hbm, v_ref, sems.at[1])
    k_copy.start()
    v_copy.start()
    k_copy.wait()
    v_copy.wait()


def split(states, odd, keep_ref, send_ref):
    half = len(states) // 2
    for h in range(half):
        keep_ref[head(h), :] = jnp.where(odd, states[half + h], states[h]).astype(BF)
        send_ref[head(h), :] = jnp.where(odd, states[h], states[half + h]).astype(BF)


def tail_kernel(ids_ref, odd_ref, k_ref, v_ref, keep_ref, send_ref):
    ids = ids_ref[...]
    hit = (column(ids, HEAD) == ids[:, -1:]).astype(F32).astype(BF)
    put_ids(ids, send_ref)
    heads = range(k_ref.shape[1] // HEAD)
    states = [dot(k_ref[:, head(h)] * hit, v_ref[:, head(h)], TN) for h in heads]
    split(states, odd_ref[...] > 0, keep_ref, send_ref)


def chip_kernel(backward, odd_ref, keep_ref, send_ref, theirs_ref, out_ref):
    odd = odd_ref[...] > 0
    mine_kept = ~odd if backward else odd
    which = 1 if backward else 0
    both = get_ids(send_ref)[which] == get_ids(theirs_ref)[which]
    for h in range(keep_ref.shape[0] // HEAD):
        mine, theirs = keep_ref[head(h), :].astype(F32), theirs_ref[head(h), :].astype(F32)
        state = jnp.where(both, mine + theirs, jnp.where(mine_kept, mine, theirs))
        out_ref[head(h), :] = state.astype(BF)
    mine, theirs = send_ref[-2 * IDS :, :].astype(F32), theirs_ref[-2 * IDS :, :].astype(F32)
    out_ref[-2 * IDS :, :] = jnp.where(mine_kept, mine, theirs).astype(BF)


def edge_kernel(backward, odd_ref, keep_ref, send_ref, theirs_ref, near_ref, far_ref, mine_ref, other_ref):
    odd = odd_ref[...] > 0
    inner = ~odd if backward else odd
    which, opposite = (1, 0) if backward else (0, 1)
    ours, others = get_ids(send_ref), get_ids(theirs_ref)
    outer_part = jnp.where(inner, others[which], ours[which])
    outer_edge = jnp.where(inner, others[opposite], ours[opposite])
    inner_edge = jnp.where(inner, ours[opposite], others[opposite])
    take_near = get_ids(near_ref)[which] == outer_edge
    take_far = get_ids(far_ref)[which] == outer_edge
    take_part = inner_edge == outer_part
    take_outer = take_part & (outer_part == outer_edge)
    for h in range(keep_ref.shape[0] // HEAD):
        outer = jnp.where(take_near, near_ref[head(h), :].astype(F32), 0.0)
        outer = outer + jnp.where(take_far, far_ref[head(h), :].astype(F32), 0.0)
        part = jnp.where(inner, theirs_ref[head(h), :].astype(F32), keep_ref[head(h), :].astype(F32))
        joined = jnp.where(take_part, part, 0.0) + jnp.where(take_outer, outer, 0.0)
        mine_ref[head(h), :] = jnp.where(inner, joined, outer).astype(BF)
        other_ref[head(h), :] = jnp.where(inner, outer, joined).astype(BF)


def merged(odd_ref, mine_ref, other_ref):
    odd = odd_ref[...] > 0
    half = mine_ref.shape[0] // HEAD

    def state(h):
        mine, other = mine_ref[head(h % half), :].astype(F32), other_ref[head(h % half), :].astype(F32)
        return (jnp.where(odd, other, mine) if h < half else jnp.where(odd, mine, other)).astype(BF)

    return state


def local_kernel(
    ids_ref, q_ref, k_ref, v_ref, g_ref, c_ref, scores_ref, local_ref, up_ref, lead_q_ref, lead_qt_ref
):
    ids = ids_ref[...]
    length = ids.shape[1]
    at = lax.broadcasted_iota(jnp.int32, (length, length), 0)
    of = lax.broadcasted_iota(jnp.int32, (length, length), 1)
    causal = (of <= at) & (column(ids, length) == ids)
    hit = (column(ids, HEAD) == ids[:, :1]).astype(F32)
    for h in range(q_ref.shape[1] // HEAD):
        scores = dot(q_ref[:, head(h)], k_ref[:, head(h)], NT)
        scores = jnp.where(causal, scores, 0.0).astype(BF)
        scores_ref[h] = scores
        local_ref[:, head(h)] = dot(scores, v_ref[:, head(h)], NN)
        gate = jax.nn.sigmoid(g_ref[:, head(h)].astype(F32))
        up_ref[:, head(h)] = c_ref[:, head(h)].astype(F32) * gate
        lead_q = q_ref[:, head(h)].astype(F32) * hit
        lead_q_ref[:, head(h)] = lead_q.astype(BF)
        lead_qt_ref[head(h), :] = lead_q.T.astype(BF)


def attend_kernel(odd_ref, mine_ref, other_ref, lead_q_ref, local_ref, up_ref, before_ref, attended_ref, sums_ref):
    length, states = lead_q_ref.shape
    entering = merged(odd_ref, mine_ref, other_ref)
    square = jnp.zeros((length, HEAD), F32)
    cross = jnp.zeros((length, HEAD), F32)
    for h in range(states // HEAD):
        before = entering(h)
        before_ref[head(h), :] = before
        attended = local_ref[:, head(h)] + dot(lead_q_ref[:, head(h)], before, NN)
        attended_ref[:, head(h)] = attended
        square = square + attended * attended
        cross = cross + up_ref[:, head(h)] * attended
    sums_ref[0:1, :] = jnp.sum(square.T, axis=0, keepdims=True)
    sums_ref[1:2, :] = jnp.sum(cross.T, axis=0, keepdims=True)


def scales(parts):
    total = parts[0][...]
    for part in parts[1:]:
        total = total + part[...]
    inverse = lax.rsqrt(total[0:1, :] / FEATURES + EPSILON)
    factor = inverse * inverse * inverse * total[1:2, :] / FEATURES
    return inverse, factor


def lead_kernel(ids_ref, odd_ref, s0, s1, s2, s3, lead_qt_ref, attended_ref, up_ref, grad_ref, keep_ref, send_ref):
    inverse, factor = scales((s0, s1, s2, s3))
    inverse, factor = column(inverse, HEAD), column(factor, HEAD)
    put_ids(ids_ref[...], send_ref)
    states = []
    for h in range(up_ref.shape[1] // HEAD):
        grad = up_ref[:, head(h)] * inverse - attended_ref[:, head(h)] * factor
        grad = grad.astype(BF)
        grad_ref[:, head(h)] = grad
        states.append(dot(lead_qt_ref[head(h), :], grad, NN))
    split(states, odd_ref[...] > 0, keep_ref, send_ref)


def back_kernel(
    ids_ref, s0, s1, s2, s3, q_ref, k_ref, v_ref, g_ref, scores_ref, attended_ref, up_ref, grad_ref, before_ref,
    query_grad_ref, gate_grad_ref, key_part_ref, value_part_ref, tail_k_ref, tail_v_ref,
):
    ids = ids_ref[...]
    length = ids.shape[1]
    inverse, _ = scales((s0, s1, s2, s3))
    inverse = column(inverse, HEAD)
    hit = (column(ids, HEAD) == ids[:, :1]).astype(F32).astype(BF)
    tail_hit = (column(ids, HEAD) == ids[:, -1:]).astype(F32).astype(BF)
    at = lax.broadcasted_iota(jnp.int32, (length, length), 0)
    of = lax.broadcasted_iota(jnp.int32, (length, length), 1)
    causal = (of <= at) & (column(ids, length) == ids)
    for h in range(q_ref.shape[1] // HEAD):
        grad = grad_ref[:, head(h)]
        back = jnp.where(causal, dot(grad, v_ref[:, head(h)], NT), 0.0).astype(BF)
        query_grad = dot(back, k_ref[:, head(h)], NN) + dot(grad * hit, before_ref[head(h), :], NT)
        query_grad_ref[:, head(h)] = query_grad.astype(BF)
        key_part_ref[:, head(h)] = dot(back, q_ref[:, head(h)], TN)
        value_part_ref[:, head(h)] = dot(scores_ref[h], grad, TN)
        gate = jax.nn.sigmoid(g_ref[:, head(h)].astype(F32))
        gate_grad = up_ref[:, head(h)] * attended_ref[:, head(h)] * inverse * (1.0 - gate)
        gate_grad_ref[:, head(h)] = gate_grad.astype(BF)
        tail_k_ref[:, head(h)] = k_ref[:, head(h)] * tail_hit
        tail_v_ref[:, head(h)] = v_ref[:, head(h)] * tail_hit


def finish_kernel(
    odd_ref, mine_ref, other_ref, tail_k_ref, tail_v_ref, key_part_ref, value_part_ref,
    key_grad_hbm, value_grad_hbm, key_grad_ref, value_grad_ref, key_sem, value_sem,
):
    leaving = merged(odd_ref, mine_ref, other_ref)
    copies = []

    def send(ref, hbm, sem, h):
        copies.append(pltpu.make_async_copy(ref.at[:, head(h)], hbm.at[:, head(h)], sem.at[h]))
        copies[-1].start()

    for h in range(tail_k_ref.shape[1] // HEAD):
        after = leaving(h)
        key_grad = key_part_ref[:, head(h)] + dot(tail_v_ref[:, head(h)], after, NT)
        key_grad_ref[:, head(h)] = key_grad.astype(BF)
        send(key_grad_ref, key_grad_hbm, key_sem, h)
        value_grad = value_part_ref[:, head(h)] + dot(tail_k_ref[:, head(h)], after, NN)
        value_grad_ref[:, head(h)] = value_grad.astype(BF)
        send(value_grad_ref, value_grad_hbm, value_sem, h)
    for copy in copies:
        copy.wait()


VMEM = pl.BlockSpec(memory_space=pltpu.VMEM)
HBM = pl.BlockSpec(memory_space=pltpu.HBM)


def call(kernel, outs, flops, *args, name=None, in_specs=None, out_specs=None, scratch=(), vmem=24 * MIB):
    size = sum(a.size * a.dtype.itemsize for a in (*args, *outs))
    return pl.pallas_call(
        kernel,
        out_shape=outs,
        in_specs=in_specs or [VMEM] * len(args),
        out_specs=out_specs or [VMEM] * len(outs),
        scratch_shapes=scratch,
        compiler_params=pltpu.CompilerParams(vmem_limit_bytes=vmem),
        cost_estimate=pl.CostEstimate(flops=flops, bytes_accessed=size, transcendentals=0),
        name=name or kernel.__name__,
    )(*args)


def body(queries, keys, values, gates, cotangent, doc_ids):
    length, states = queries.shape
    count, ranks = lax.axis_size("ctx"), lax.axis_size("tp")
    heads = states // HEAD
    shape = jax.ShapeDtypeStruct
    ids = doc_ids.reshape(1, length)
    odd = jnp.broadcast_to(lax.rem(lax.axis_index("ctx"), 2), (1, HEAD))
    half = shape((states // 2, HEAD), BF)
    message = shape((states // 2 + 2 * IDS, HEAD), BF)
    wide = shape((length, states), F32)
    narrow = shape((length, states), BF)
    unit = 2 * length * length * states
    buffer, sems = pltpu.VMEM((length, states), BF), pltpu.SemaphoreType.DMA((heads,))

    def swap(x):
        return lax.ppermute(x, "ctx", [(i, i ^ 1) for i in range(count)])

    def shift(x, blocks, wrap=True):
        pairs = [(i, (i + blocks) % count) for i in range(count) if wrap or 0 <= i + blocks < count]
        return lax.ppermute(x, "ctx", pairs)

    def chip(backward, *parts):
        name = "chip_lead" if backward else "chip_tail"
        return call(functools.partial(chip_kernel, backward), [message], 0, odd, *parts, name=name)[0]

    def edge(backward, *parts):
        name = "edge_lead" if backward else "edge_tail"
        return call(functools.partial(edge_kernel, backward), [half, half], 0, odd, *parts, name=name)

    keys, values = call(
        load_kernel, [narrow, narrow], 1, keys, values, in_specs=[HBM] * 2, scratch=[pltpu.SemaphoreType.DMA((2,))],
        vmem=52 * MIB + 768 * 1024,
    )
    tail, tail_sent = call(tail_kernel, [half, message], unit // 2, ids, odd, keys, values)
    tail_theirs = swap(tail_sent)
    state = chip(False, tail, tail_sent, tail_theirs)
    near, far = shift(state, 2, False), shift(state, 4)
    ids, _ = lax.optimization_barrier((ids, state))
    scores, local, up, lead_q, lead_qt = call(
        local_kernel, [shape((heads, length, length), BF), wide, wide, narrow, shape((states, length), BF)], 2 * unit,
        ids, queries, keys, values, gates, cotangent,
    )
    near, far, local = lax.optimization_barrier((near, far, local))
    mine, given = edge(False, tail, tail_sent, tail_theirs, near, far)
    before, attended, sums = call(
        attend_kernel, [shape((states, HEAD), BF), wide, shape((2, length), F32)], unit // 2,
        odd, mine, swap(given), lead_q, local, up,
    )
    parts = [sums] + [lax.ppermute(sums, "tp", [(i, i ^ step) for i in range(ranks)]) for step in (1, 3, 2)]
    grad, lead, lead_sent = call(
        lead_kernel, [narrow, half, message], unit // 2, ids, odd, *parts, lead_qt, attended, up
    )

    lead_theirs = swap(lead_sent)
    state = chip(True, lead, lead_sent, lead_theirs)
    near, far = shift(state, -2), shift(state, -4)
    ids, _ = lax.optimization_barrier((ids, state))
    query_grad, gate_grad, key_part, value_part, tail_k, tail_v = call(
        back_kernel, [narrow, narrow, wide, wide, narrow, narrow], 5 * unit,
        ids, *parts, queries, keys, values, gates, scores, attended, up, grad, before,
    )
    near, far, key_part = lax.optimization_barrier((near, far, key_part))
    mine, given = edge(True, lead, lead_sent, lead_theirs, near, far)
    key_grad, value_grad = call(
        finish_kernel, [narrow, narrow], unit, odd, mine, swap(given), tail_k, tail_v, key_part, value_part,
        out_specs=[HBM] * 2, scratch=[buffer, buffer, sems, sems],
    )
    return query_grad, key_grad, value_grad, gate_grad


def solution(mesh):
    return jax.shard_map(
        body,
        mesh=mesh,
        in_specs=(P("ctx", "tp"),) * 5 + (P("ctx"),),
        out_specs=(P("ctx", "tp"),) * 4,
        check_vma=False,
    )
```

time: 52.8 us -> 49.7 us (0.941)
  waiting for transfers between devices: 22.9 us -> 14.7 us
  starting transfers between devices: 16.9 us -> 24 us
  Pallas kernels: 10.4 us -> 9.36 us
  local copies, waits for them, and re-layouts: 1.73 us -> 0.69 us
    ppermute x5 -> x7, starting transfers between devices: 8.23 us -> 16.1 us  [the longest x4 12.3 us: shift(): return lax.ppermute(x, 'ctx', pairs)]
    ppermute x5 -> x7, waiting for transfers between devices: 18 us -> 10.8 us  [the longest x4 7.92 us: shift(): return lax.ppermute(x, 'ctx', pairs)]
    pallas_call x8 -> x11, Pallas kernels: 10.4 us -> 9.36 us  [call(): pl.pallas_call(kernel, out_shape=outs, in_specs=in_specs or [VMEM] * len(...]
    unnamed x12 -> x8, local copies, waits for them, and re-layouts: 1.73 us -> 0.69 us
    ppermute x4, waiting for transfers between devices: 4.94 us -> 3.96 us  [swap(): return lax.ppermute(x, 'ctx', [(i, i ^ 1) for i in range(count)])]
    ppermute x4, starting transfers between devices: 8.63 us -> 7.92 us  [swap(): return lax.ppermute(x, 'ctx', [(i, i ^ 1) for i in range(count)])]
  transfers between devices with their start and end apart: 9 -> 11, of which waited for: 8 -> 9; matrix products, arithmetic and copies ran while one was open for 0% -> 0% of each run, Pallas kernels for 9% -> 10%
where the time goes in v3:
time: 49.7 us; the launch traced here: 49.6 us
  starting transfers between devices  24 us (48%)
  waiting for transfers between devices  14.7 us (30%)
  Pallas kernels  9.36 us (19%)
  between operations  0.75 us (2%)
  local copies, waits for them, and re-layouts  0.69 us (1%)
    ppermute x4, starting transfers between devices, shift(): return lax.ppermute(x, 'ctx', pairs)  12.3 us
    pallas_call x11, Pallas kernels, call(): pl.pallas_call(kernel, out_shape=outs, in_specs=in_specs or [VMEM] * len(...  9.36 us
    ppermute x4, waiting for transfers between devices, shift(): return lax.ppermute(x, 'ctx', pairs)  7.92 us
    ppermute x4, starting transfers between devices, swap(): return lax.ppermute(x, 'ctx', [(i, i ^ 1) for i in range(count)])  7.92 us
    ppermute x4, waiting for transfers between devices, swap(): return lax.ppermute(x, 'ctx', [(i, i ^ 1) for i in range(count)])  3.96 us
    ppermute x3, starting transfers between devices, body(): lax.ppermute(sums, 'tp', [(i, i ^ step) for i in range(ranks)])  3.78 us
    ppermute x3, waiting for transfers between devices, body(): lax.ppermute(sums, 'tp', [(i, i ^ step) for i in range(ranks)])  2.88 us
  transfers between devices with their start and end apart: 11, of which 9 were waited for; matrix products, arithmetic and copies ran while one was open for 0% of the time, Pallas kernels for 10%

profile of v3, /device:TPU:1, one launch (start us, length us, event | category | flops | bytes accessed | tf_op | source)
XLA Modules:
  0.0 49.6 jit_solution(14849235884747673904)
XLA Ops:
  0.6 1.2 %load_kernel.1 = (bf16[256,1024]{1,0:T(8,128)(2,1)S(1)}, bf16[256,1024]{1,0:T(8,128)(2,1)S(1)}) custom-call(bf16[256,1024]{1,0:T(8,128)(2,1)} %k_hbm.1, bf16[256,1024]{1,0:T(8,128)(2,1)} %v_hbm.1), custom_call_target="tpu_custom_call" | custom-call | flops 1 | bytes 2097152 | tf_op jit(solution)/shard_map/load_kernel/pallas_call | solution.py:233
  1.9 0.0 copy-start.3
  1.9 0.7 %copy-done.3 = s32[256]{0:T(256)S(1)} copy-done((s32[256]{0:T(256)S(1)}, s32[256]{0:T(256)}, u32[]{:S(2)}) %copy-start.3) | copy-done | bytes 1048
  2.6 0.0 copy-start.1
  2.6 0.0 copy-start.2
  2.6 0.5 tail_kernel.1
  3.0 0.0 copy-start
  3.0 3.3 %collective-permute-start = (bf16[528,128]{1,0:T(8,128)(2,1)S(1)}, bf16[528,128]{1,0:T(8,128)(2,1)S(1)}, u32[]{:S(2)}, u32[]{:S(2)}) collective-permute-start(bf16[528,128]{1,0:T(8,128)(2,1)S(1)} %get-tuple-element.42.send_ref), channel_id=1, source_target_pairs={{0,4},{4,0},{8,12},{12,8},{16,20},{20,16},{24,28},{28,24},{32,36},... | collective-permute-start | bytes 405512 | tf_op jit(solution)/shard_map/ppermute | solution.py:260
  6.4 1.0 %collective-permute-done.theirs_ref = bf16[528,128]{1,0:T(8,128)(2,1)S(1)} collective-permute-done((bf16[528,128]{1,0:T(8,128)(2,1)S(1)}, bf16[528,128]{1,0:T(8,128)(2,1)S(1)}, u32[]{:S(2)}, u32[]{:S(2)}) %collective-permute-start) | collective-permute-done | bytes 135200 | tf_op jit(solution)/shard_map/ppermute | solution.py:260
  7.4 0.1 chip_tail.1
  7.4 1.3 %collective-permute-start.2 = (bf16[528,128]{1,0:T(8,128)(2,1)S(1)}, bf16[528,128]{1,0:T(8,128)(2,1)S(1)}, u32[]{:S(2)}, u32[]{:S(2)}) collective-permute-start(bf16[528,128]{1,0:T(8,128)(2,1)S(1)} %chip_tail.1), channel_id=1, source_target_pairs={{0,16},{4,20},{8,24},{12,28},{16,32},{20,36},{24,40},{28,44},{32,4... | collective-permute-start | bytes 405512 | tf_op jit(solution)/shard_map/ppermute | solution.py:264
  8.8 3.5 %collective-permute-start.1 = (bf16[528,128]{1,0:T(8,128)(2,1)S(1)}, bf16[528,128]{1,0:T(8,128)(2,1)S(1)}, u32[]{:S(2)}, u32[]{:S(2)}) collective-permute-start(bf16[528,128]{1,0:T(8,128)(2,1)S(1)} %chip_tail.1), channel_id=1, source_target_pairs={{0,8},{4,12},{8,16},{12,20},{16,24},{20,28},{24,32},{28,36},{32,40... | collective-permute-start | bytes 405512 | tf_op jit(solution)/shard_map/ppermute | solution.py:264
  12.3 0.0 copy-done.1
  12.3 0.0 copy-done.2
  12.3 0.0 copy-done
  12.3 1.2 %local_kernel.1 = (bf16[8,256,256]{2,1,0:T(8,128)(2,1)S(1)}, f32[256,1024]{1,0:T(8,128)S(1)}, f32[256,1024]{1,0:T(8,128)S(1)}, bf16[256,1024]{1,0:T(8,128)(2,1)S(1)}, bf16[1024,256]{1,0:T(8,128)(2,1)S(1)}) custom-call(s32[1,256]{1,0:T(1,128)S(1)} %bitcast.2, bf16[256,1024]{1,0:T(8,128)(2,1)S(1)} %copy-done, bf16[256,1024]{1,0:T(8,128)(2,1)S(1)} %get-tuple-element.39.k_ref, ...), custom_call_target="tpu_custom_call" | custom-call | flops 268435456 | bytes 6816768 | tf_op jit(solution)/shard_map/local_kernel/pallas_call | solution.py:233
  13.5 4.7 %collective-permute-done.2.far_ref = bf16[528,128]{1,0:T(8,128)(2,1)S(1)} collective-permute-done((bf16[528,128]{1,0:T(8,128)(2,1)S(1)}, bf16[528,128]{1,0:T(8,128)(2,1)S(1)}, u32[]{:S(2)}, u32[]{:S(2)}) %collective-permute-start.2) | collective-permute-done | bytes 135200 | tf_op jit(solution)/shard_map/ppermute | solution.py:264
  18.2 0.0 collective-permute-done.1.near_ref
  18.2 0.1 edge_tail.1
  18.4 1.4 %collective-permute-start.3 = (bf16[512,128]{1,0:T(8,128)(2,1)S(1)}, bf16[512,128]{1,0:T(8,128)(2,1)S(1)}, u32[]{:S(2)}, u32[]{:S(2)}) collective-permute-start(bf16[512,128]{1,0:T(8,128)(2,1)S(1)} %get-tuple-element.48), channel_id=1, source_target_pairs={{0,4},{4,0},{8,12},{12,8},{16,20},{20,16},{24,28},{28,24},{32,36},... | collective-permute-start | bytes 393224 | tf_op jit(solution)/shard_map/ppermute | solution.py:260
  19.8 1.0 %collective-permute-done.3.other_ref = bf16[512,128]{1,0:T(8,128)(2,1)S(1)} collective-permute-done((bf16[512,128]{1,0:T(8,128)(2,1)S(1)}, bf16[512,128]{1,0:T(8,128)(2,1)S(1)}, u32[]{:S(2)}, u32[]{:S(2)}) %collective-permute-start.3) | collective-permute-done | bytes 131104 | tf_op jit(solution)/shard_map/ppermute | solution.py:260
  20.8 0.5 attend_kernel.1
  21.3 3.0 %collective-permute-start.6 = (f32[2,256]{1,0:T(2,128)S(1)}, f32[2,256]{1,0:T(2,128)S(1)}, u32[]{:S(2)}, u32[]{:S(2)}) collective-permute-start(f32[2,256]{1,0:T(2,128)S(1)} %get-tuple-element.52.s0), channel_id=1, source_target_pairs={{0,2},{1,3},{2,0},{3,1},{4,6},{5,7},{6,4},{7,5},{8,10},{9,11},{10,... | collective-permute-start | bytes 6152 | tf_op jit(solution)/shard_map/ppermute | solution.py:293
  24.3 0.8 %collective-permute-start.5 = (f32[2,256]{1,0:T(2,128)S(1)}, f32[2,256]{1,0:T(2,128)S(1)}, u32[]{:S(2)}, u32[]{:S(2)}) collective-permute-start(f32[2,256]{1,0:T(2,128)S(1)} %get-tuple-element.52.s0), channel_id=1, source_target_pairs={{0,3},{1,2},{2,1},{3,0},{4,7},{5,6},{6,5},{7,4},{8,11},{9,10},{10,... | collective-permute-start | bytes 6152 | tf_op jit(solution)/shard_map/ppermute | solution.py:293
  25.1 0.0 collective-permute-start.4
  25.1 0.2 collective-permute-done.6.s3
  25.3 2.6 %collective-permute-done.5.s2 = f32[2,256]{1,0:T(2,128)S(1)} collective-permute-done((f32[2,256]{1,0:T(2,128)S(1)}, f32[2,256]{1,0:T(2,128)S(1)}, u32[]{:S(2)}, u32[]{:S(2)}) %collective-permute-start.5) | collective-permute-done | bytes 2080 | tf_op jit(solution)/shard_map/ppermute | solution.py:293
  27.9 0.0 collective-permute-done.4.s1
  27.9 0.5 lead_kernel.1
  28.4 1.9 %collective-permute-start.7 = (bf16[528,128]{1,0:T(8,128)(2,1)S(1)}, bf16[528,128]{1,0:T(8,128)(2,1)S(1)}, u32[]{:S(2)}, u32[]{:S(2)}) collective-permute-start(bf16[528,128]{1,0:T(8,128)(2,1)S(1)} %get-tuple-element.56.send_ref), channel_id=1, source_target_pairs={{0,4},{4,0},{8,12},{12,8},{16,20},{20,16},{24,28},{28,24},{32,36},... | collective-permute-start | bytes 405512 | tf_op jit(solution)/shard_map/ppermute | solution.py:260
  30.3 1.0 %collective-permute-done.7.theirs_ref = bf16[528,128]{1,0:T(8,128)(2,1)S(1)} collective-permute-done((bf16[528,128]{1,0:T(8,128)(2,1)S(1)}, bf16[528,128]{1,0:T(8,128)(2,1)S(1)}, u32[]{:S(2)}, u32[]{:S(2)}) %collective-permute-start.7) | collective-permute-done | bytes 135200 | tf_op jit(solution)/shard_map/ppermute | solution.py:260
  31.3 0.1 chip_lead.1
  31.4 6.7 %collective-permute-start.9 = (bf16[528,128]{1,0:T(8,128)(2,1)S(1)}, bf16[528,128]{1,0:T(8,128)(2,1)S(1)}, u32[]{:S(2)}, u32[]{:S(2)}) collective-permute-start(bf16[528,128]{1,0:T(8,128)(2,1)S(1)} %chip_lead.1), channel_id=1, source_target_pairs={{0,240},{4,244},{8,248},{12,252},{16,0},{20,4},{24,8},{28,12},{32,... | collective-permute-start | bytes 405512 | tf_op jit(solution)/shard_map/ppermute | solution.py:264
  38.1 0.8 %collective-permute-start.8 = (bf16[528,128]{1,0:T(8,128)(2,1)S(1)}, bf16[528,128]{1,0:T(8,128)(2,1)S(1)}, u32[]{:S(2)}, u32[]{:S(2)}) collective-permute-start(bf16[528,128]{1,0:T(8,128)(2,1)S(1)} %chip_lead.1), channel_id=1, source_target_pairs={{0,248},{4,252},{8,0},{12,4},{16,8},{20,12},{24,16},{28,20},{32,24... | collective-permute-start | bytes 405512 | tf_op jit(solution)/shard_map/ppermute | solution.py:264
  38.8 3.8 %back_kernel.1 = (bf16[256,1024]{1,0:T(8,128)(2,1)}, bf16[256,1024]{1,0:T(8,128)(2,1)}, f32[256,1024]{1,0:T(8,128)S(1)}, f32[256,1024]{1,0:T(8,128)S(1)}, bf16[2...) custom-call(s32[1,256]{1,0:T(1,128)S(1)} %bitcast.4, f32[2,256]{1,0:T(2,128)S(1)} %get-tuple-element.52.s0, ...), custom_call_target="tpu_custom_call" | custom-call | flops 671088640 | bytes 10232832 | tf_op jit(solution)/shard_map/back_kernel/pallas_call | solution.py:233
  42.7 0.2 collective-permute-done.9.far_ref
  42.9 3.0 %collective-permute-done.8.near_ref = bf16[528,128]{1,0:T(8,128)(2,1)S(1)} collective-permute-done((bf16[528,128]{1,0:T(8,128)(2,1)S(1)}, bf16[528,128]{1,0:T(8,128)(2,1)S(1)}, u32[]{:S(2)}, u32[]{:S(2)}) %collective-permute-start.8) | collective-permute-done | bytes 135200 | tf_op jit(solution)/shard_map/ppermute | solution.py:264
  45.9 0.1 edge_lead.1
  46.0 1.3 %collective-permute-start.10 = (bf16[512,128]{1,0:T(8,128)(2,1)S(1)}, bf16[512,128]{1,0:T(8,128)(2,1)S(1)}, u32[]{:S(2)}, u32[]{:S(2)}) collective-permute-start(bf16[512,128]{1,0:T(8,128)(2,1)S(1)} %get-tuple-element.66), channel_id=1, source_target_pairs={{0,4},{4,0},{8,12},{12,8},{16,20},{20,16},{24,28},{28,24},{32,36},... | collective-permute-start | bytes 393224 | tf_op jit(solution)/shard_map/ppermute | solution.py:260
  47.3 1.0 %collective-permute-done.10.other_ref = bf16[512,128]{1,0:T(8,128)(2,1)S(1)} collective-permute-done((bf16[512,128]{1,0:T(8,128)(2,1)S(1)}, bf16[512,128]{1,0:T(8,128)(2,1)S(1)}, u32[]{:S(2)}, u32[]{:S(2)}) %collective-permute-start.10) | collective-permute-done | bytes 131104 | tf_op jit(solution)/shard_map/ppermute | solution.py:260
  48.3 1.3 %finish_kernel.1 = (bf16[256,1024]{1,0:T(8,128)(2,1)}, bf16[256,1024]{1,0:T(8,128)(2,1)}) custom-call(s32[1,128]{1,0:T(1,128)S(1)} %broadcast_in_dim.3.odd_ref, bf16[512,128]{1,0:T(8,128)(2,1)S(1)} %get-tuple-element.65.mine_ref, bf16[512,128]{1,0:T(8,128)(2,1)S(1)} %collective-permute-done.10.other_ref, bf16[256,1024]{1,0:T(8,128)(2,1)S(1)} %get-tuple-element.67.tail_k_ref, ...), custom_call_target="tpu_custom_call" | custom-call | flops 134217728 | bytes 4456960 | tf_op jit(solution)/shard_map/finish_kernel/pallas_call | solution.py:233
  (1 shorter events, 0.0 us)
Async XLA Ops:
  1.9 0.7 %copy-start.3 = (s32[256]{0:T(256)S(1)}, s32[256]{0:T(256)}, u32[]{:S(2)}) copy-start(s32[256]{0:T(256)} %param.11) | copy-start | bytes 3076
  2.6 9.7 %copy-start.1 = (bf16[256,1024]{1,0:T(8,128)(2,1)S(1)}, bf16[256,1024]{1,0:T(8,128)(2,1)}, u32[]{:S(2)}) copy-start(bf16[256,1024]{1,0:T(8,128)(2,1)} %g_ref.3) | copy-start | bytes 1572868
  2.6 9.8 %copy-start.2 = (bf16[256,1024]{1,0:T(8,128)(2,1)S(1)}, bf16[256,1024]{1,0:T(8,128)(2,1)}, u32[]{:S(2)}) copy-start(bf16[256,1024]{1,0:T(8,128)(2,1)} %c_ref.1) | copy-start | bytes 1572868
  3.0 9.3 %copy-start = (bf16[256,1024]{1,0:T(8,128)(2,1)S(1)}, bf16[256,1024]{1,0:T(8,128)(2,1)}, u32[]{:S(2)}) copy-start(bf16[256,1024]{1,0:T(8,128)(2,1)} %q_ref.3) | copy-start | bytes 1572868
  3.0 4.3 %collective-permute-start = (bf16[528,128]{1,0:T(8,128)(2,1)S(1)}, bf16[528,128]{1,0:T(8,128)(2,1)S(1)}, u32[]{:S(2)}, u32[]{:S(2)}) collective-permute-start(bf16[528,128]{1,0:T(8,128)(2,1)S(1)} %get-tuple-element.42.send_ref), channel_id=1, source_target_pairs={{0,4},{4,0},{8,12},{12,8},{16,20},{20,16},{24,28},{28,24},{32,36},... | collective-permute-start | bytes 405512 | tf_op jit(solution)/shard_map/ppermute | solution.py:260
  7.4 10.8 %collective-permute-start.2 = (bf16[528,128]{1,0:T(8,128)(2,1)S(1)}, bf16[528,128]{1,0:T(8,128)(2,1)S(1)}, u32[]{:S(2)}, u32[]{:S(2)}) collective-permute-start(bf16[528,128]{1,0:T(8,128)(2,1)S(1)} %chip_tail.1), channel_id=1, source_target_pairs={{0,16},{4,20},{8,24},{12,28},{16,32},{20,36},{24,40},{28,44},{32,4... | collective-permute-start | bytes 405512 | tf_op jit(solution)/shard_map/ppermute | solution.py:264
  8.8 9.5 %collective-permute-start.1 = (bf16[528,128]{1,0:T(8,128)(2,1)S(1)}, bf16[528,128]{1,0:T(8,128)(2,1)S(1)}, u32[]{:S(2)}, u32[]{:S(2)}) collective-permute-start(bf16[528,128]{1,0:T(8,128)(2,1)S(1)} %chip_tail.1), channel_id=1, source_target_pairs={{0,8},{4,12},{8,16},{12,20},{16,24},{20,28},{24,32},{28,36},{32,40... | collective-permute-start | bytes 405512 | tf_op jit(solution)/shard_map/ppermute | solution.py:264
  18.4 2.4 %collective-permute-start.3 = (bf16[512,128]{1,0:T(8,128)(2,1)S(1)}, bf16[512,128]{1,0:T(8,128)(2,1)S(1)}, u32[]{:S(2)}, u32[]{:S(2)}) collective-permute-start(bf16[512,128]{1,0:T(8,128)(2,1)S(1)} %get-tuple-element.48), channel_id=1, source_target_pairs={{0,4},{4,0},{8,12},{12,8},{16,20},{20,16},{24,28},{28,24},{32,36},... | collective-permute-start | bytes 393224 | tf_op jit(solution)/shard_map/ppermute | solution.py:260
  21.3 4.0 %collective-permute-start.6 = (f32[2,256]{1,0:T(2,128)S(1)}, f32[2,256]{1,0:T(2,128)S(1)}, u32[]{:S(2)}, u32[]{:S(2)}) collective-permute-start(f32[2,256]{1,0:T(2,128)S(1)} %get-tuple-element.52.s0), channel_id=1, source_target_pairs={{0,2},{1,3},{2,0},{3,1},{4,6},{5,7},{6,4},{7,5},{8,10},{9,11},{10,... | collective-permute-start | bytes 6152 | tf_op jit(solution)/shard_map/ppermute | solution.py:293
  24.3 3.6 %collective-permute-start.5 = (f32[2,256]{1,0:T(2,128)S(1)}, f32[2,256]{1,0:T(2,128)S(1)}, u32[]{:S(2)}, u32[]{:S(2)}) collective-permute-start(f32[2,256]{1,0:T(2,128)S(1)} %get-tuple-element.52.s0), channel_id=1, source_target_pairs={{0,3},{1,2},{2,1},{3,0},{4,7},{5,6},{6,5},{7,4},{8,11},{9,10},{10,... | collective-permute-start | bytes 6152 | tf_op jit(solution)/shard_map/ppermute | solution.py:293
  25.1 2.9 %collective-permute-start.4 = (f32[2,256]{1,0:T(2,128)S(1)}, f32[2,256]{1,0:T(2,128)S(1)}, u32[]{:S(2)}, u32[]{:S(2)}) collective-permute-start(f32[2,256]{1,0:T(2,128)S(1)} %get-tuple-element.52.s0), channel_id=1, source_target_pairs={{0,1},{1,0},{2,3},{3,2},{4,5},{5,4},{6,7},{7,6},{8,9},{9,8},{10,11... | collective-permute-start | bytes 6152 | tf_op jit(solution)/shard_map/ppermute | solution.py:293
  28.4 2.9 %collective-permute-start.7 = (bf16[528,128]{1,0:T(8,128)(2,1)S(1)}, bf16[528,128]{1,0:T(8,128)(2,1)S(1)}, u32[]{:S(2)}, u32[]{:S(2)}) collective-permute-start(bf16[528,128]{1,0:T(8,128)(2,1)S(1)} %get-tuple-element.56.send_ref), channel_id=1, source_target_pairs={{0,4},{4,0},{8,12},{12,8},{16,20},{20,16},{24,28},{28,24},{32,36},... | collective-permute-start | bytes 405512 | tf_op jit(solution)/shard_map/ppermute | solution.py:260
  31.4 11.5 %collective-permute-start.9 = (bf16[528,128]{1,0:T(8,128)(2,1)S(1)}, bf16[528,128]{1,0:T(8,128)(2,1)S(1)}, u32[]{:S(2)}, u32[]{:S(2)}) collective-permute-start(bf16[528,128]{1,0:T(8,128)(2,1)S(1)} %chip_lead.1), channel_id=1, source_target_pairs={{0,240},{4,244},{8,248},{12,252},{16,0},{20,4},{24,8},{28,12},{32,... | collective-permute-start | bytes 405512 | tf_op jit(solution)/shard_map/ppermute | solution.py:264
  38.1 7.8 %collective-permute-start.8 = (bf16[528,128]{1,0:T(8,128)(2,1)S(1)}, bf16[528,128]{1,0:T(8,128)(2,1)S(1)}, u32[]{:S(2)}, u32[]{:S(2)}) collective-permute-start(bf16[528,128]{1,0:T(8,128)(2,1)S(1)} %chip_lead.1), channel_id=1, source_target_pairs={{0,248},{4,252},{8,0},{12,4},{16,8},{20,12},{24,16},{28,20},{32,24... | collective-permute-start | bytes 405512 | tf_op jit(solution)/shard_map/ppermute | solution.py:264
  46.0 2.3 %collective-permute-start.10 = (bf16[512,128]{1,0:T(8,128)(2,1)S(1)}, bf16[512,128]{1,0:T(8,128)(2,1)S(1)}, u32[]{:S(2)}, u32[]{:S(2)}) collective-permute-start(bf16[512,128]{1,0:T(8,128)(2,1)S(1)} %get-tuple-element.66), channel_id=1, source_target_pairs={{0,4},{4,0},{8,12},{12,8},{16,20},{20,16},{24,28},{28,24},{32,36},... | collective-permute-start | bytes 393224 | tf_op jit(solution)/shard_map/ppermute | solution.py:260

commit v4 on v3

--- a/solution.py
+++ b/solution.py
@@ -83,25 +83,22 @@
     out_ref[-2 * IDS :, :] = jnp.where(mine_kept, mine, theirs).astype(BF)
 
 
-def edge_kernel(backward, odd_ref, keep_ref, send_ref, theirs_ref, near_ref, far_ref, mine_ref, other_ref):
+def edge_kernel(odd_ref, keep_ref, send_ref, theirs_ref, near_ref, far_ref, mine_ref, other_ref):
     odd = odd_ref[...] > 0
-    inner = ~odd if backward else odd
-    which, opposite = (1, 0) if backward else (0, 1)
     ours, others = get_ids(send_ref), get_ids(theirs_ref)
-    outer_part = jnp.where(inner, others[which], ours[which])
-    outer_edge = jnp.where(inner, others[opposite], ours[opposite])
-    inner_edge = jnp.where(inner, ours[opposite], others[opposite])
-    take_near = get_ids(near_ref)[which] == outer_edge
-    take_far = get_ids(far_ref)[which] == outer_edge
-    take_part = inner_edge == outer_part
-    take_outer = take_part & (outer_part == outer_edge)
+    last_even = jnp.where(odd, others[0], ours[0])
+    first_even = jnp.where(odd, others[1], ours[1])
+    first_odd = jnp.where(odd, ours[1], others[1])
+    take_near, take_far = get_ids(near_ref)[0] == first_even, get_ids(far_ref)[0] == first_even
+    take_part = first_odd == last_even
+    take_outer = take_part & (last_even == first_even)
     for h in range(keep_ref.shape[0] // HEAD):
         outer = jnp.where(take_near, near_ref[head(h), :].astype(F32), 0.0)
         outer = outer + jnp.where(take_far, far_ref[head(h), :].astype(F32), 0.0)
-        part = jnp.where(inner, theirs_ref[head(h), :].astype(F32), keep_ref[head(h), :].astype(F32))
+        part = jnp.where(odd, theirs_ref[head(h), :].astype(F32), keep_ref[head(h), :].astype(F32))
         joined = jnp.where(take_part, part, 0.0) + jnp.where(take_outer, outer, 0.0)
-        mine_ref[head(h), :] = jnp.where(inner, joined, outer).astype(BF)
-        other_ref[head(h), :] = jnp.where(inner, outer, joined).astype(BF)
+        mine_ref[head(h), :] = jnp.where(odd, joined, outer).astype(BF)
+        other_ref[head(h), :] = jnp.where(odd, outer, joined).astype(BF)
 
 
 def merged(odd_ref, mine_ref, other_ref):
@@ -161,17 +158,15 @@
     return inverse, factor
 
 
-def lead_kernel(ids_ref, odd_ref, s0, s1, s2, s3, lead_qt_ref, attended_ref, up_ref, grad_ref, keep_ref, send_ref):
+def lead_kernel(ids_ref, s0, s1, s2, s3, lead_qt_ref, attended_ref, up_ref, grad_ref, out_ref):
     inverse, factor = scales((s0, s1, s2, s3))
     inverse, factor = column(inverse, HEAD), column(factor, HEAD)
-    put_ids(ids_ref[...], send_ref)
-    states = []
+    put_ids(ids_ref[...], out_ref)
     for h in range(up_ref.shape[1] // HEAD):
         grad = up_ref[:, head(h)] * inverse - attended_ref[:, head(h)] * factor
         grad = grad.astype(BF)
         grad_ref[:, head(h)] = grad
-        states.append(dot(lead_qt_ref[head(h), :], grad, NN))
-    split(states, odd_ref[...] > 0, keep_ref, send_ref)
+        out_ref[head(h), :] = dot(lead_qt_ref[head(h), :], grad, NN).astype(BF)
 
 
 def back_kernel(
@@ -202,10 +197,15 @@
 
 
 def finish_kernel(
-    odd_ref, mine_ref, other_ref, tail_k_ref, tail_v_ref, key_part_ref, value_part_ref,
+    odd_ref, mine_ref, theirs_ref, came_ref, other_ref, tail_k_ref, tail_v_ref, key_part_ref, value_part_ref,
     key_grad_hbm, value_grad_hbm, key_grad_ref, value_grad_ref, key_sem, value_sem,
 ):
-    leaving = merged(odd_ref, mine_ref, other_ref)
+    odd = odd_ref[...] > 0
+    (last, first), (their_last, their_first) = get_ids(mine_ref), get_ids(theirs_ref)
+    edge = jnp.where(odd, last, their_last)
+    take_came, take_other = get_ids(came_ref)[1] == edge, get_ids(other_ref)[1] == edge
+    take_theirs = ~odd & (their_first == last)
+    take_outer = odd | (take_theirs & (their_first == their_last))
     copies = []
 
     def send(ref, hbm, sem, h):
@@ -213,7 +213,10 @@
         copies[-1].start()
 
     for h in range(tail_k_ref.shape[1] // HEAD):
-        after = leaving(h)
+        outer = jnp.where(take_came, came_ref[head(h), :].astype(F32), 0.0)
+        outer = outer + jnp.where(take_other, other_ref[head(h), :].astype(F32), 0.0)
+        after = jnp.where(take_theirs, theirs_ref[head(h), :].astype(F32), 0.0)
+        after = (after + jnp.where(take_outer, outer, 0.0)).astype(BF)
         key_grad = key_part_ref[:, head(h)] + dot(tail_v_ref[:, head(h)], after, NT)
         key_grad_ref[:, head(h)] = key_grad.astype(BF)
         send(key_grad_ref, key_grad_hbm, key_sem, h)
@@ -251,6 +254,7 @@
     odd = jnp.broadcast_to(lax.rem(lax.axis_index("ctx"), 2), (1, HEAD))
     half = shape((states // 2, HEAD), BF)
     message = shape((states // 2 + 2 * IDS, HEAD), BF)
+    whole = shape((states + 2 * IDS, HEAD), BF)
     wide = shape((length, states), F32)
     narrow = shape((length, states), BF)
     unit = 2 * length * length * states
@@ -263,13 +267,9 @@
         pairs = [(i, (i + blocks) % count) for i in range(count) if wrap or 0 <= i + blocks < count]
         return lax.ppermute(x, "ctx", pairs)
 
-    def chip(backward, *parts):
+    def chip(backward, out, *parts):
         name = "chip_lead" if backward else "chip_tail"
-        return call(functools.partial(chip_kernel, backward), [message], 0, odd, *parts, name=name)[0]
-
-    def edge(backward, *parts):
-        name = "edge_lead" if backward else "edge_tail"
-        return call(functools.partial(edge_kernel, backward), [half, half], 0, odd, *parts, name=name)
+        return call(functools.partial(chip_kernel, backward), [out], 0, odd, *parts, name=name)[0]
 
     keys, values = call(
         load_kernel, [narrow, narrow], 1, keys, values, in_specs=[HBM] * 2, scratch=[pltpu.SemaphoreType.DMA((2,))],
@@ -277,36 +277,34 @@
     )
     tail, tail_sent = call(tail_kernel, [half, message], unit // 2, ids, odd, keys, values)
     tail_theirs = swap(tail_sent)
-    state = chip(False, tail, tail_sent, tail_theirs)
-    near, far = shift(state, 2, False), shift(state, 4)
+    state = chip(False, message, tail, tail_sent, tail_theirs)
+    far = shift(state, 4, False)
+    near = shift(state, 2)
     ids, _ = lax.optimization_barrier((ids, state))
     scores, local, up, lead_q, lead_qt = call(
         local_kernel, [shape((heads, length, length), BF), wide, wide, narrow, shape((states, length), BF)], 2 * unit,
         ids, queries, keys, values, gates, cotangent,
     )
-    near, far, local = lax.optimization_barrier((near, far, local))
-    mine, given = edge(False, tail, tail_sent, tail_theirs, near, far)
+    far, near, local = lax.optimization_barrier((far, near, local))
+    mine, given = call(edge_kernel, [half, half], 0, odd, tail, tail_sent, tail_theirs, far, near)
     before, attended, sums = call(
         attend_kernel, [shape((states, HEAD), BF), wide, shape((2, length), F32)], unit // 2,
         odd, mine, swap(given), lead_q, local, up,
     )
     parts = [sums] + [lax.ppermute(sums, "tp", [(i, i ^ step) for i in range(ranks)]) for step in (1, 3, 2)]
-    grad, lead, lead_sent = call(
-        lead_kernel, [narrow, half, message], unit // 2, ids, odd, *parts, lead_qt, attended, up
-    )
-
-    lead_theirs = swap(lead_sent)
-    state = chip(True, lead, lead_sent, lead_theirs)
-    near, far = shift(state, -2), shift(state, -4)
+    grad, lead = call(lead_kernel, [narrow, whole], unit // 2, ids, *parts, lead_qt, attended, up)
+
+    lead_theirs = swap(lead)
+    state = chip(True, whole, lead, lead, lead_theirs)
+    came = lax.ppermute(state, "ctx", [(i, (i - (2 if i % 2 == 0 else 4)) % count) for i in range(count)])
     ids, _ = lax.optimization_barrier((ids, state))
     query_grad, gate_grad, key_part, value_part, tail_k, tail_v = call(
         back_kernel, [narrow, narrow, wide, wide, narrow, narrow], 5 * unit,
         ids, *parts, queries, keys, values, gates, scores, attended, up, grad, before,
     )
-    near, far, key_part = lax.optimization_barrier((near, far, key_part))
-    mine, given = edge(True, lead, lead_sent, lead_theirs, near, far)
+    came, key_part = lax.optimization_barrier((came, key_part))
     key_grad, value_grad = call(
-        finish_kernel, [narrow, narrow], unit, odd, mine, swap(given), tail_k, tail_v, key_part, value_part,
+        finish_kernel, [narrow, narrow], unit, odd, lead, lead_theirs, came, swap(came), tail_k, tail_v, key_part, value_part,
         out_specs=[HBM] * 2, scratch=[buffer, buffer, sems, sems],
     )
     return query_grad, key_grad, value_grad, gate_grad

time: 49.7 us -> 48.4 us (0.974)
  starting transfers between devices: 24 us -> 23.4 us
  waiting for transfers between devices: 14.7 us -> 14.1 us
    ppermute x4 -> x2, starting transfers between devices: 12.3 us -> 4.86 us  [shift(): return lax.ppermute(x, 'ctx', pairs)]
    ppermute x0 -> x1, starting transfers between devices: none -> 6.16 us  [body(): lax.ppermute(state, 'ctx', [(i, (i - (2 if i % 2 == 0 else 4)) % count) f...]
    ppermute x4 -> x2, waiting for transfers between devices: 7.92 us -> 3.67 us  [shift(): return lax.ppermute(x, 'ctx', pairs)]
    ppermute x0 -> x1, waiting for transfers between devices: none -> 3.26 us  [body(): lax.ppermute(state, 'ctx', [(i, (i - (2 if i % 2 == 0 else 4)) % count) f...]
    ppermute x4, starting transfers between devices: 7.92 us -> 8.6 us  [swap(): return lax.ppermute(x, 'ctx', [(i, i ^ 1) for i in range(count)])]
    pallas_call x11 -> x10, Pallas kernels: 9.36 us -> 9.33 us  [call(): pl.pallas_call(kernel, out_shape=outs, in_specs=in_specs or [VMEM] * len(...]
  transfers between devices with their start and end apart: 11 -> 10, of which waited for: 9 -> 8; matrix products, arithmetic and copies ran while one was open for 0% -> 0% of each run, Pallas kernels for 10% -> 10%
where the time goes in v4:
time: 48.4 us; the launch traced here: 48.3 us
  starting transfers between devices  23.4 us (48%)
  waiting for transfers between devices  14.1 us (29%)
  Pallas kernels  9.33 us (19%)
  between operations  0.75 us (2%)
  local copies, waits for them, and re-layouts  0.69 us (1%)
    pallas_call x10, Pallas kernels, call(): pl.pallas_call(kernel, out_shape=outs, in_specs=in_specs or [VMEM] * len(...  9.33 us
    ppermute x4, starting transfers between devices, swap(): return lax.ppermute(x, 'ctx', [(i, i ^ 1) for i in range(count)])  8.6 us
    ppermute x1, starting transfers between devices, body(): lax.ppermute(state, 'ctx', [(i, (i - (2 if i % 2 == 0 else 4)) % count) f...  6.16 us
    ppermute x2, starting transfers between devices, shift(): return lax.ppermute(x, 'ctx', pairs)  4.86 us
    ppermute x4, waiting for transfers between devices, swap(): return lax.ppermute(x, 'ctx', [(i, i ^ 1) for i in range(count)])  4.31 us
    ppermute x3, starting transfers between devices, body(): lax.ppermute(sums, 'tp', [(i, i ^ step) for i in range(ranks)])  3.78 us
    ppermute x2, waiting for transfers between devices, shift(): return lax.ppermute(x, 'ctx', pairs)  3.67 us
    ppermute x1, waiting for transfers between devices, body(): lax.ppermute(state, 'ctx', [(i, (i - (2 if i % 2 == 0 else 4)) % count) f...  3.26 us
  transfers between devices with their start and end apart: 10, of which 8 were waited for; matrix products, arithmetic and copies ran while one was open for 0% of the time, Pallas kernels for 10%

profile of v4, /device:TPU:1, one launch (start us, length us, event | category | flops | bytes accessed | tf_op | source)
XLA Modules:
  0.0 48.3 jit_solution(6563764593213418623)
XLA Ops:
  0.6 1.2 %load_kernel.1 = (bf16[256,1024]{1,0:T(8,128)(2,1)S(1)}, bf16[256,1024]{1,0:T(8,128)(2,1)S(1)}) custom-call(bf16[256,1024]{1,0:T(8,128)(2,1)} %k_hbm.1, bf16[256,1024]{1,0:T(8,128)(2,1)} %v_hbm.1), custom_call_target="tpu_custom_call" | custom-call | flops 1 | bytes 2097152 | tf_op jit(solution)/shard_map/load_kernel/pallas_call | solution.py:236
  1.9 0.0 copy-start.3
  1.9 0.7 %copy-done.3 = s32[256]{0:T(256)S(1)} copy-done((s32[256]{0:T(256)S(1)}, s32[256]{0:T(256)}, u32[]{:S(2)}) %copy-start.3) | copy-done | bytes 1048
  2.6 0.0 copy-start.1
  2.6 0.0 copy-start.2
  2.6 0.5 tail_kernel.1
  3.0 0.0 copy-start
  3.0 3.3 %collective-permute-start = (bf16[528,128]{1,0:T(8,128)(2,1)S(1)}, bf16[528,128]{1,0:T(8,128)(2,1)S(1)}, u32[]{:S(2)}, u32[]{:S(2)}) collective-permute-start(bf16[528,128]{1,0:T(8,128)(2,1)S(1)} %get-tuple-element.38.send_ref), channel_id=1, source_target_pairs={{0,4},{4,0},{8,12},{12,8},{16,20},{20,16},{24,28},{28,24},{32,36},... | collective-permute-start | bytes 405512 | tf_op jit(solution)/shard_map/ppermute | solution.py:264
  6.4 1.0 %collective-permute-done.theirs_ref = bf16[528,128]{1,0:T(8,128)(2,1)S(1)} collective-permute-done((bf16[528,128]{1,0:T(8,128)(2,1)S(1)}, bf16[528,128]{1,0:T(8,128)(2,1)S(1)}, u32[]{:S(2)}, u32[]{:S(2)}) %collective-permute-start) | collective-permute-done | bytes 135200 | tf_op jit(solution)/shard_map/ppermute | solution.py:264
  7.4 0.1 chip_tail.1
  7.4 0.1 collective-permute-start.2
  7.5 4.8 %collective-permute-start.1 = (bf16[528,128]{1,0:T(8,128)(2,1)S(1)}, bf16[528,128]{1,0:T(8,128)(2,1)S(1)}, u32[]{:S(2)}, u32[]{:S(2)}) collective-permute-start(bf16[528,128]{1,0:T(8,128)(2,1)S(1)} %chip_tail.1), channel_id=1, source_target_pairs={{0,16},{4,20},{8,24},{12,28},{16,32},{20,36},{24,40},{28,44},{32,4... | collective-permute-start | bytes 405512 | tf_op jit(solution)/shard_map/ppermute | solution.py:268
  12.3 0.0 copy-done.1
  12.3 0.0 copy-done.2
  12.3 0.0 copy-done
  12.3 1.2 %local_kernel.1 = (bf16[8,256,256]{2,1,0:T(8,128)(2,1)S(1)}, f32[256,1024]{1,0:T(8,128)S(1)}, f32[256,1024]{1,0:T(8,128)S(1)}, bf16[256,1024]{1,0:T(8,128)(2,1)S(1)}, bf16[1024,256]{1,0:T(8,128)(2,1)S(1)}) custom-call(s32[1,256]{1,0:T(1,128)S(1)} %bitcast.2, bf16[256,1024]{1,0:T(8,128)(2,1)S(1)} %copy-done, bf16[256,1024]{1,0:T(8,128)(2,1)S(1)} %get-tuple-element.35.k_ref, ...), custom_call_target="tpu_custom_call" | custom-call | flops 268435456 | bytes 6816768 | tf_op jit(solution)/shard_map/local_kernel/pallas_call | solution.py:236
  13.5 3.7 %collective-permute-done.2.far_ref = bf16[528,128]{1,0:T(8,128)(2,1)S(1)} collective-permute-done((bf16[528,128]{1,0:T(8,128)(2,1)S(1)}, bf16[528,128]{1,0:T(8,128)(2,1)S(1)}, u32[]{:S(2)}, u32[]{:S(2)}) %collective-permute-start.2) | collective-permute-done | bytes 135200 | tf_op jit(solution)/shard_map/ppermute | solution.py:268
  17.2 0.0 collective-permute-done.1.near_ref
  17.2 0.1 edge_kernel.1
  17.3 1.0 %collective-permute-start.3 = (bf16[512,128]{1,0:T(8,128)(2,1)S(1)}, bf16[512,128]{1,0:T(8,128)(2,1)S(1)}, u32[]{:S(2)}, u32[]{:S(2)}) collective-permute-start(bf16[512,128]{1,0:T(8,128)(2,1)S(1)} %get-tuple-element.44), channel_id=1, source_target_pairs={{0,4},{4,0},{8,12},{12,8},{16,20},{20,16},{24,28},{28,24},{32,36},... | collective-permute-start | bytes 393224 | tf_op jit(solution)/shard_map/ppermute | solution.py:264
  18.3 1.0 %collective-permute-done.3.other_ref = bf16[512,128]{1,0:T(8,128)(2,1)S(1)} collective-permute-done((bf16[512,128]{1,0:T(8,128)(2,1)S(1)}, bf16[512,128]{1,0:T(8,128)(2,1)S(1)}, u32[]{:S(2)}, u32[]{:S(2)}) %collective-permute-start.3) | collective-permute-done | bytes 131104 | tf_op jit(solution)/shard_map/ppermute | solution.py:264
  19.3 0.5 %attend_kernel.1 = (bf16[1024,128]{1,0:T(8,128)(2,1)S(1)}, f32[256,1024]{1,0:T(8,128)S(1)}, f32[2,256]{1,0:T(2,128)S(1)}) custom-call(s32[1,128]{1,0:T(1,128)S(1)} %broadcast_in_dim.3.odd_ref, bf16[512,128]{1,0:T(8,128)(2,1)S(1)} %get-tuple-element.43.mine_ref, bf16[512,128]{1,0:T(8,128)(2,1)S(1)} %collective-permute-done.3.other_ref, ...), custom_call_target="tpu_custom_call" | custom-call | flops 67108864 | bytes 4196864 | tf_op jit(solution)/shard_map/attend_kernel/pallas_call | solution.py:236
  19.8 3.0 %collective-permute-start.6 = (f32[2,256]{1,0:T(2,128)S(1)}, f32[2,256]{1,0:T(2,128)S(1)}, u32[]{:S(2)}, u32[]{:S(2)}) collective-permute-start(f32[2,256]{1,0:T(2,128)S(1)} %get-tuple-element.48.s0), channel_id=1, source_target_pairs={{0,2},{1,3},{2,0},{3,1},{4,6},{5,7},{6,4},{7,5},{8,10},{9,11},{10,... | collective-permute-start | bytes 6152 | tf_op jit(solution)/shard_map/ppermute | solution.py:294
  22.8 0.8 %collective-permute-start.5 = (f32[2,256]{1,0:T(2,128)S(1)}, f32[2,256]{1,0:T(2,128)S(1)}, u32[]{:S(2)}, u32[]{:S(2)}) collective-permute-start(f32[2,256]{1,0:T(2,128)S(1)} %get-tuple-element.48.s0), channel_id=1, source_target_pairs={{0,3},{1,2},{2,1},{3,0},{4,7},{5,6},{6,5},{7,4},{8,11},{9,10},{10,... | collective-permute-start | bytes 6152 | tf_op jit(solution)/shard_map/ppermute | solution.py:294
  23.6 0.0 collective-permute-start.4
  23.6 0.2 collective-permute-done.6.s3
  23.8 2.6 %collective-permute-done.5.s2 = f32[2,256]{1,0:T(2,128)S(1)} collective-permute-done((f32[2,256]{1,0:T(2,128)S(1)}, f32[2,256]{1,0:T(2,128)S(1)}, u32[]{:S(2)}, u32[]{:S(2)}) %collective-permute-start.5) | collective-permute-done | bytes 2080 | tf_op jit(solution)/shard_map/ppermute | solution.py:294
  26.5 0.0 collective-permute-done.4.s1
  26.5 0.5 lead_kernel.1
  26.9 1.9 %collective-permute-start.7 = (bf16[1040,128]{1,0:T(8,128)(2,1)S(1)}, bf16[1040,128]{1,0:T(8,128)(2,1)S(1)}, u32[]{:S(2)}, u32[]{:S(2)}) collective-permute-start(bf16[1040,128]{1,0:T(8,128)(2,1)S(1)} %get-tuple-element.51.keep_ref.send_ref.mine_ref), channel_id=1, source_target_pairs={{0,4},{4,0},{8,12},{12,8},{16,20},{20,16},{24,28},{28,24},{32,36},... | collective-permute-start | bytes 798728 | tf_op jit(solution)/shard_map/ppermute | solution.py:264
  28.8 1.2 %collective-permute-done.7.theirs_ref = bf16[1040,128]{1,0:T(8,128)(2,1)S(1)} collective-permute-done((bf16[1040,128]{1,0:T(8,128)(2,1)S(1)}, bf16[1040,128]{1,0:T(8,128)(2,1)S(1)}, u32[]{:S(2)}, u32[]{:S(2)}) %collective-permute-start.7) | collective-permute-done | bytes 266272 | tf_op jit(solution)/shard_map/ppermute | solution.py:264
  30.0 0.1 chip_lead.1
  30.1 6.2 %collective-permute-start.8 = (bf16[1040,128]{1,0:T(8,128)(2,1)S(1)}, bf16[1040,128]{1,0:T(8,128)(2,1)S(1)}, u32[]{:S(2)}, u32[]{:S(2)}) collective-permute-start(bf16[1040,128]{1,0:T(8,128)(2,1)S(1)} %chip_lead.1), channel_id=1, source_target_pairs={{0,248},{4,244},{8,0},{12,252},{16,8},{20,4},{24,16},{28,12},{32,2... | collective-permute-start | bytes 798728 | tf_op jit(solution)/shard_map/ppermute | solution.py:299
  36.3 3.8 %back_kernel.1 = (bf16[256,1024]{1,0:T(8,128)(2,1)}, bf16[256,1024]{1,0:T(8,128)(2,1)}, f32[256,1024]{1,0:T(8,128)S(1)}, f32[256,1024]{1,0:T(8,128)S(1)}, bf16[2...) custom-call(s32[1,256]{1,0:T(1,128)S(1)} %bitcast.4, f32[2,256]{1,0:T(2,128)S(1)} %get-tuple-element.48.s0, ...), custom_call_target="tpu_custom_call" | custom-call | flops 671088640 | bytes 10232832 | tf_op jit(solution)/shard_map/back_kernel/pallas_call | solution.py:236
  40.1 3.3 %collective-permute-done.8.came_ref = bf16[1040,128]{1,0:T(8,128)(2,1)S(1)} collective-permute-done((bf16[1040,128]{1,0:T(8,128)(2,1)S(1)}, bf16[1040,128]{1,0:T(8,128)(2,1)S(1)}, u32[]{:S(2)}, u32[]{:S(2)}) %collective-permute-start.8) | collective-permute-done | bytes 266272 | tf_op jit(solution)/shard_map/ppermute | solution.py:299
  43.4 2.4 %collective-permute-start.9 = (bf16[1040,128]{1,0:T(8,128)(2,1)S(1)}, bf16[1040,128]{1,0:T(8,128)(2,1)S(1)}, u32[]{:S(2)}, u32[]{:S(2)}) collective-permute-start(bf16[1040,128]{1,0:T(8,128)(2,1)S(1)} %collective-permute-done.8.came_ref), channel_id=1, source_target_pairs={{0,4},{4,0},{8,12},{12,8},{16,20},{20,16},{24,28},{28,24},{32,36},... | collective-permute-start | bytes 798728 | tf_op jit(solution)/shard_map/ppermute | solution.py:264
  45.8 1.2 %collective-permute-done.9.other_ref = bf16[1040,128]{1,0:T(8,128)(2,1)S(1)} collective-permute-done((bf16[1040,128]{1,0:T(8,128)(2,1)S(1)}, bf16[1040,128]{1,0:T(8,128)(2,1)S(1)}, u32[]{:S(2)}, u32[]{:S(2)}) %collective-permute-start.9) | collective-permute-done | bytes 266272 | tf_op jit(solution)/shard_map/ppermute | solution.py:264
  46.9 1.4 %finish_kernel.1 = (bf16[256,1024]{1,0:T(8,128)(2,1)}, bf16[256,1024]{1,0:T(8,128)(2,1)}) custom-call(s32[1,128]{1,0:T(1,128)S(1)} %broadcast_in_dim.3.odd_ref, bf16[1040,128]{1,0:T(8,128)(2,1)S(1)} %get-tuple-element.51.keep_ref.send_ref.mine_ref, bf16[1040,128]{1,0:T(8,128)(2,1)S(1)} %collective-permute-done.7.theirs_ref, ...), custom_call_target="tpu_custom_call" | custom-call | flops 134217728 | bytes 5259776 | tf_op jit(solution)/shard_map/finish_kernel/pallas_call | solution.py:236
  (1 shorter events, 0.0 us)
Async XLA Ops:
  1.9 0.7 %copy-start.3 = (s32[256]{0:T(256)S(1)}, s32[256]{0:T(256)}, u32[]{:S(2)}) copy-start(s32[256]{0:T(256)} %param.11) | copy-start | bytes 3076
  2.6 9.7 %copy-start.1 = (bf16[256,1024]{1,0:T(8,128)(2,1)S(1)}, bf16[256,1024]{1,0:T(8,128)(2,1)}, u32[]{:S(2)}) copy-start(bf16[256,1024]{1,0:T(8,128)(2,1)} %g_ref.3) | copy-start | bytes 1572868
  2.6 9.8 %copy-start.2 = (bf16[256,1024]{1,0:T(8,128)(2,1)S(1)}, bf16[256,1024]{1,0:T(8,128)(2,1)}, u32[]{:S(2)}) copy-start(bf16[256,1024]{1,0:T(8,128)(2,1)} %c_ref.1) | copy-start | bytes 1572868
  3.0 9.3 %copy-start = (bf16[256,1024]{1,0:T(8,128)(2,1)S(1)}, bf16[256,1024]{1,0:T(8,128)(2,1)}, u32[]{:S(2)}) copy-start(bf16[256,1024]{1,0:T(8,128)(2,1)} %q_ref.3) | copy-start | bytes 1572868
  3.0 4.3 %collective-permute-start = (bf16[528,128]{1,0:T(8,128)(2,1)S(1)}, bf16[528,128]{1,0:T(8,128)(2,1)S(1)}, u32[]{:S(2)}, u32[]{:S(2)}) collective-permute-start(bf16[528,128]{1,0:T(8,128)(2,1)S(1)} %get-tuple-element.38.send_ref), channel_id=1, source_target_pairs={{0,4},{4,0},{8,12},{12,8},{16,20},{20,16},{24,28},{28,24},{32,36},... | collective-permute-start | bytes 405512 | tf_op jit(solution)/shard_map/ppermute | solution.py:264
  7.4 9.8 %collective-permute-start.2 = (bf16[528,128]{1,0:T(8,128)(2,1)S(1)}, bf16[528,128]{1,0:T(8,128)(2,1)S(1)}, u32[]{:S(2)}, u32[]{:S(2)}) collective-permute-start(bf16[528,128]{1,0:T(8,128)(2,1)S(1)} %chip_tail.1), channel_id=1, source_target_pairs={{0,8},{4,12},{8,16},{12,20},{16,24},{20,28},{24,32},{28,36},{32,40... | collective-permute-start | bytes 405512 | tf_op jit(solution)/shard_map/ppermute | solution.py:268
  7.5 9.7 %collective-permute-start.1 = (bf16[528,128]{1,0:T(8,128)(2,1)S(1)}, bf16[528,128]{1,0:T(8,128)(2,1)S(1)}, u32[]{:S(2)}, u32[]{:S(2)}) collective-permute-start(bf16[528,128]{1,0:T(8,128)(2,1)S(1)} %chip_tail.1), channel_id=1, source_target_pairs={{0,16},{4,20},{8,24},{12,28},{16,32},{20,36},{24,40},{28,44},{32,4... | collective-permute-start | bytes 405512 | tf_op jit(solution)/shard_map/ppermute | solution.py:268
  17.3 2.0 %collective-permute-start.3 = (bf16[512,128]{1,0:T(8,128)(2,1)S(1)}, bf16[512,128]{1,0:T(8,128)(2,1)S(1)}, u32[]{:S(2)}, u32[]{:S(2)}) collective-permute-start(bf16[512,128]{1,0:T(8,128)(2,1)S(1)} %get-tuple-element.44), channel_id=1, source_target_pairs={{0,4},{4,0},{8,12},{12,8},{16,20},{20,16},{24,28},{28,24},{32,36},... | collective-permute-start | bytes 393224 | tf_op jit(solution)/shard_map/ppermute | solution.py:264
  19.8 4.0 %collective-permute-start.6 = (f32[2,256]{1,0:T(2,128)S(1)}, f32[2,256]{1,0:T(2,128)S(1)}, u32[]{:S(2)}, u32[]{:S(2)}) collective-permute-start(f32[2,256]{1,0:T(2,128)S(1)} %get-tuple-element.48.s0), channel_id=1, source_target_pairs={{0,2},{1,3},{2,0},{3,1},{4,6},{5,7},{6,4},{7,5},{8,10},{9,11},{10,... | collective-permute-start | bytes 6152 | tf_op jit(solution)/shard_map/ppermute | solution.py:294
  22.8 3.6 %collective-permute-start.5 = (f32[2,256]{1,0:T(2,128)S(1)}, f32[2,256]{1,0:T(2,128)S(1)}, u32[]{:S(2)}, u32[]{:S(2)}) collective-permute-start(f32[2,256]{1,0:T(2,128)S(1)} %get-tuple-element.48.s0), channel_id=1, source_target_pairs={{0,3},{1,2},{2,1},{3,0},{4,7},{5,6},{6,5},{7,4},{8,11},{9,10},{10,... | collective-permute-start | bytes 6152 | tf_op jit(solution)/shard_map/ppermute | solution.py:294
  23.6 2.9 %collective-permute-start.4 = (f32[2,256]{1,0:T(2,128)S(1)}, f32[2,256]{1,0:T(2,128)S(1)}, u32[]{:S(2)}, u32[]{:S(2)}) collective-permute-start(f32[2,256]{1,0:T(2,128)S(1)} %get-tuple-element.48.s0), channel_id=1, source_target_pairs={{0,1},{1,0},{2,3},{3,2},{4,5},{5,4},{6,7},{7,6},{8,9},{9,8},{10,11... | collective-permute-start | bytes 6152 | tf_op jit(solution)/shard_map/ppermute | solution.py:294
  26.9 3.0 %collective-permute-start.7 = (bf16[1040,128]{1,0:T(8,128)(2,1)S(1)}, bf16[1040,128]{1,0:T(8,128)(2,1)S(1)}, u32[]{:S(2)}, u32[]{:S(2)}) collective-permute-start(bf16[1040,128]{1,0:T(8,128)(2,1)S(1)} %get-tuple-element.51.keep_ref.send_ref.mine_ref), channel_id=1, source_target_pairs={{0,4},{4,0},{8,12},{12,8},{16,20},{20,16},{24,28},{28,24},{32,36},... | collective-permute-start | bytes 798728 | tf_op jit(solution)/shard_map/ppermute | solution.py:264
  30.1 13.3 %collective-permute-start.8 = (bf16[1040,128]{1,0:T(8,128)(2,1)S(1)}, bf16[1040,128]{1,0:T(8,128)(2,1)S(1)}, u32[]{:S(2)}, u32[]{:S(2)}) collective-permute-start(bf16[1040,128]{1,0:T(8,128)(2,1)S(1)} %chip_lead.1), channel_id=1, source_target_pairs={{0,248},{4,244},{8,0},{12,252},{16,8},{20,4},{24,16},{28,12},{32,2... | collective-permute-start | bytes 798728 | tf_op jit(solution)/shard_map/ppermute | solution.py:299
  43.4 3.6 %collective-permute-start.9 = (bf16[1040,128]{1,0:T(8,128)(2,1)S(1)}, bf16[1040,128]{1,0:T(8,128)(2,1)S(1)}, u32[]{:S(2)}, u32[]{:S(2)}) collective-permute-start(bf16[1040,128]{1,0:T(8,128)(2,1)S(1)} %collective-permute-done.8.came_ref), channel_id=1, source_target_pairs={{0,4},{4,0},{8,12},{12,8},{16,20},{20,16},{24,28},{28,24},{32,36},... | collective-permute-start | bytes 798728 | tf_op jit(solution)/shard_map/ppermute | solution.py:264

commit v5 on v4

--- a/solution.py
+++ b/solution.py
@@ -1,4 +1,5 @@
 import functools
+import math
 
 import jax
 import jax.numpy as jnp
@@ -45,15 +46,6 @@
     return ids[:1], ids[IDS : IDS + 1]
 
 
-def load_kernel(k_hbm, v_hbm, k_ref, v_ref, sems):
-    k_copy = pltpu.make_async_copy(k_hbm, k_ref, sems.at[0])
-    v_copy = pltpu.make_async_copy(v_hbm, v_ref, sems.at[1])
-    k_copy.start()
-    v_copy.start()
-    k_copy.wait()
-    v_copy.wait()
-
-
 def split(states, odd, keep_ref, send_ref):
     half = len(states) // 2
     for h in range(half):
@@ -61,12 +53,21 @@
         send_ref[head(h), :] = jnp.where(odd, states[h], states[half + h]).astype(BF)
 
 
-def tail_kernel(ids_ref, odd_ref, k_ref, v_ref, keep_ref, send_ref):
+def tail_kernel(ids_hbm, k_hbm, v_hbm, odd_ref, ids_ref, k_ref, v_ref, keep_ref, send_ref, kt_ref, sems):
+    loads = ((ids_hbm, ids_ref), (k_hbm, k_ref), (v_hbm, v_ref))
+    copies = [pltpu.make_async_copy(hbm, ref, sems.at[i]) for i, (hbm, ref) in enumerate(loads)]
+    for copy in copies:
+        copy.start()
+    heads = range(k_ref.shape[1] // HEAD)
+    copies[0].wait()
     ids = ids_ref[...]
-    hit = (column(ids, HEAD) == ids[:, -1:]).astype(F32).astype(BF)
     put_ids(ids, send_ref)
-    heads = range(k_ref.shape[1] // HEAD)
-    states = [dot(k_ref[:, head(h)] * hit, v_ref[:, head(h)], TN) for h in heads]
+    hit = jnp.broadcast_to((ids == ids[:, -1:]).astype(F32).astype(BF), (HEAD, ids.shape[1]))
+    copies[1].wait()
+    for h in heads:
+        kt_ref[head(h), :] = k_ref[:, head(h)].T * hit
+    copies[2].wait()
+    states = [dot(kt_ref[head(h), :], v_ref[:, head(h)], NN) for h in heads]
     split(states, odd_ref[...] > 0, keep_ref, send_ref)
 
 
@@ -113,14 +114,21 @@
 
 
 def local_kernel(
-    ids_ref, q_ref, k_ref, v_ref, g_ref, c_ref, scores_ref, local_ref, up_ref, lead_q_ref, lead_qt_ref
+    ids_ref, q_hbm, k_ref, v_ref, g_hbm, c_hbm, scores_ref, local_ref, up_ref, lead_q_ref, lead_qt_ref,
+    q_ref, g_ref, c_ref, sems,
 ):
+    loads = ((q_hbm, q_ref), (g_hbm, g_ref), (c_hbm, c_ref))
+    copies = [pltpu.make_async_copy(hbm, ref, sems.at[i]) for i, (hbm, ref) in enumerate(loads)]
+    for copy in copies:
+        copy.start()
     ids = ids_ref[...]
     length = ids.shape[1]
     at = lax.broadcasted_iota(jnp.int32, (length, length), 0)
     of = lax.broadcasted_iota(jnp.int32, (length, length), 1)
     causal = (of <= at) & (column(ids, length) == ids)
     hit = (column(ids, HEAD) == ids[:, :1]).astype(F32)
+    for copy in copies:
+        copy.wait()
     for h in range(q_ref.shape[1] // HEAD):
         scores = dot(q_ref[:, head(h)], k_ref[:, head(h)], NT)
         scores = jnp.where(causal, scores, 0.0).astype(BF)
@@ -231,8 +239,12 @@
 HBM = pl.BlockSpec(memory_space=pltpu.HBM)
 
 
+def in_hbm(x):
+    return pltpu.with_memory_space_constraint(x, pltpu.HBM)
+
+
 def call(kernel, outs, flops, *args, name=None, in_specs=None, out_specs=None, scratch=(), vmem=24 * MIB):
-    size = sum(a.size * a.dtype.itemsize for a in (*args, *outs))
+    size = sum(math.prod(a.shape) * jnp.dtype(a.dtype).itemsize for a in (*args, *outs))
     return pl.pallas_call(
         kernel,
         out_shape=outs,
@@ -271,11 +283,12 @@
         name = "chip_lead" if backward else "chip_tail"
         return call(functools.partial(chip_kernel, backward), [out], 0, odd, *parts, name=name)[0]
 
-    keys, values = call(
-        load_kernel, [narrow, narrow], 1, keys, values, in_specs=[HBM] * 2, scratch=[pltpu.SemaphoreType.DMA((2,))],
-        vmem=52 * MIB + 768 * 1024,
-    )
-    tail, tail_sent = call(tail_kernel, [half, message], unit // 2, ids, odd, keys, values)
+    ids, keys, values, tail, tail_sent = call(
+        tail_kernel,
+        [pltpu.VMEM(ids.shape, ids.dtype)] + [pltpu.VMEM(a.shape, a.dtype) for a in (narrow, narrow, half, message)],
+        unit // 2, in_hbm(ids), in_hbm(keys), in_hbm(values), odd,
+        in_specs=[HBM] * 3 + [VMEM], scratch=[pltpu.VMEM((states, length), BF), pltpu.SemaphoreType.DMA((3,))],
+    )
     tail_theirs = swap(tail_sent)
     state = chip(False, message, tail, tail_sent, tail_theirs)
     far = shift(state, 4, False)
@@ -283,7 +296,8 @@
     ids, _ = lax.optimization_barrier((ids, state))
     scores, local, up, lead_q, lead_qt = call(
         local_kernel, [shape((heads, length, length), BF), wide, wide, narrow, shape((states, length), BF)], 2 * unit,
-        ids, queries, keys, values, gates, cotangent,
+        ids, in_hbm(queries), keys, values, in_hbm(gates), in_hbm(cotangent),
+        in_specs=[VMEM, HBM, VMEM, VMEM, HBM, HBM], scratch=[buffer] * 3 + [pltpu.SemaphoreType.DMA((3,))],
     )
     far, near, local = lax.optimization_barrier((far, near, local))
     mine, given = call(edge_kernel, [half, half], 0, odd, tail, tail_sent, tail_theirs, far, near)

time: 48.4 us -> 47.7 us (0.986)
  waiting for transfers between devices: 14.1 us -> 12.8 us
  Pallas kernels: 9.33 us -> 10.6 us
  local copies, waits for them, and re-layouts: 0.69 us -> 0.02 us
    ppermute x2, waiting for transfers between devices: 3.67 us -> 2.37 us  [shift(): return lax.ppermute(x, 'ctx', pairs)]
    pallas_call x10 -> x9, Pallas kernels: 9.33 us -> 10.6 us  [call(): pl.pallas_call(kernel, out_shape=outs, in_specs=in_specs or [VMEM] * len(...]
    unnamed x8 -> x4, local copies, waits for them, and re-layouts: 0.69 us -> 0.01 us
  transfers between devices with their start and end apart: 10 -> 10, of which waited for: 8 -> 8; matrix products, arithmetic and copies ran while one was open for 0% -> 0% of each run, Pallas kernels for 10% -> 13%
where the time goes in v5:
time: 47.7 us; the launch traced here: 47.5 us
  starting transfers between devices  23.4 us (49%)
  waiting for transfers between devices  12.8 us (27%)
  Pallas kernels  10.6 us (22%)
  between operations  0.72 us (2%)
    pallas_call x9, Pallas kernels, call(): pl.pallas_call(kernel, out_shape=outs, in_specs=in_specs or [VMEM] * len(...  10.6 us
    ppermute x4, starting transfers between devices, swap(): return lax.ppermute(x, 'ctx', [(i, i ^ 1) for i in range(count)])  8.6 us
    ppermute x1, starting transfers between devices, body(): lax.ppermute(state, 'ctx', [(i, (i - (2 if i % 2 == 0 else 4)) % count) f...  6.16 us
    ppermute x2, starting transfers between devices, shift(): return lax.ppermute(x, 'ctx', pairs)  4.86 us
    ppermute x4, waiting for transfers between devices, swap(): return lax.ppermute(x, 'ctx', [(i, i ^ 1) for i in range(count)])  4.31 us
    ppermute x3, starting transfers between devices, body(): lax.ppermute(sums, 'tp', [(i, i ^ step) for i in range(ranks)])  3.77 us
    ppermute x1, waiting for transfers between devices, body(): lax.ppermute(state, 'ctx', [(i, (i - (2 if i % 2 == 0 else 4)) % count) f...  3.22 us
    ppermute x3, waiting for transfers between devices, body(): lax.ppermute(sums, 'tp', [(i, i ^ step) for i in range(ranks)])  2.87 us
  transfers between devices with their start and end apart: 10, of which 8 were waited for; matrix products, arithmetic and copies ran while one was open for 0% of the time, Pallas kernels for 13%

profile of v5, /device:TPU:1, one launch (start us, length us, event | category | flops | bytes accessed | tf_op | source)
XLA Modules:
  0.0 47.5 jit_solution(9832863784983043078)
XLA Ops:
  0.6 1.6 %tail_kernel.1 = (s32[1,256]{1,0:T(1,128)S(1)}, bf16[256,1024]{1,0:T(8,128)(2,1)S(1)}, bf16[256,1024]{1,0:T(8,128)(2,1)S(1)}, bf16[512,128]{1,0:T(8,128)(2,1)S(1)}, bf16[528,128]{1,0:T(8,128)(2,1)S(1)}) custom-call(s32[1,256]{1,0:T(1,128)} %bitcast.1, bf16[256,1024]{1,0:T(8,128)(2,1)} %k_hbm.1, bf16[256,1024]{1,0:T(8,128)(2,1)} %v_hbm.1, ...), custom_call_target="tpu_custom_call" | custom-call | flops 67108864 | bytes 2365952 | tf_op jit(solution)/shard_map/tail_kernel/pallas_call | solution.py:248
  2.2 3.3 %collective-permute-start = (bf16[528,128]{1,0:T(8,128)(2,1)S(1)}, bf16[528,128]{1,0:T(8,128)(2,1)S(1)}, u32[]{:S(2)}, u32[]{:S(2)}) collective-permute-start(bf16[528,128]{1,0:T(8,128)(2,1)S(1)} %get-tuple-element.38.send_ref), channel_id=1, source_target_pairs={{0,4},{4,0},{8,12},{12,8},{16,20},{20,16},{24,28},{28,24},{32,36},... | collective-permute-start | bytes 405512 | tf_op jit(solution)/shard_map/ppermute | solution.py:276
  5.6 1.0 %collective-permute-done.theirs_ref = bf16[528,128]{1,0:T(8,128)(2,1)S(1)} collective-permute-done((bf16[528,128]{1,0:T(8,128)(2,1)S(1)}, bf16[528,128]{1,0:T(8,128)(2,1)S(1)}, u32[]{:S(2)}, u32[]{:S(2)}) %collective-permute-start) | collective-permute-done | bytes 135200 | tf_op jit(solution)/shard_map/ppermute | solution.py:276
  6.5 0.1 chip_tail.1
  6.6 0.1 collective-permute-start.2
  6.7 4.8 %collective-permute-start.1 = (bf16[528,128]{1,0:T(8,128)(2,1)S(1)}, bf16[528,128]{1,0:T(8,128)(2,1)S(1)}, u32[]{:S(2)}, u32[]{:S(2)}) collective-permute-start(bf16[528,128]{1,0:T(8,128)(2,1)S(1)} %chip_tail.1), channel_id=1, source_target_pairs={{0,16},{4,20},{8,24},{12,28},{16,32},{20,36},{24,40},{28,44},{32,4... | collective-permute-start | bytes 405512 | tf_op jit(solution)/shard_map/ppermute | solution.py:280
  11.5 2.5 %local_kernel.1 = (bf16[8,256,256]{2,1,0:T(8,128)(2,1)S(1)}, f32[256,1024]{1,0:T(8,128)S(1)}, f32[256,1024]{1,0:T(8,128)S(1)}, bf16[256,1024]{1,0:T(8,128)(2,1)S(1)}, bf16[1024,256]{1,0:T(8,128)(2,1)S(1)}) custom-call(s32[1,256]{1,0:T(1,128)S(1)} %get-tuple-element.54.ids_ref, bf16[256,1024]{1,0:T(8,128)(2,1)} %q_ref.1, ...), custom_call_target="tpu_custom_call" | custom-call | flops 268435456 | bytes 6816768 | tf_op jit(solution)/shard_map/local_kernel/pallas_call | solution.py:248
  14.0 2.4 %collective-permute-done.2.far_ref = bf16[528,128]{1,0:T(8,128)(2,1)S(1)} collective-permute-done((bf16[528,128]{1,0:T(8,128)(2,1)S(1)}, bf16[528,128]{1,0:T(8,128)(2,1)S(1)}, u32[]{:S(2)}, u32[]{:S(2)}) %collective-permute-start.2) | collective-permute-done | bytes 135200 | tf_op jit(solution)/shard_map/ppermute | solution.py:280
  16.4 0.0 collective-permute-done.1.near_ref
  16.4 0.1 edge_kernel.1
  16.5 1.0 %collective-permute-start.3 = (bf16[512,128]{1,0:T(8,128)(2,1)S(1)}, bf16[512,128]{1,0:T(8,128)(2,1)S(1)}, u32[]{:S(2)}, u32[]{:S(2)}) collective-permute-start(bf16[512,128]{1,0:T(8,128)(2,1)S(1)} %get-tuple-element.46), channel_id=1, source_target_pairs={{0,4},{4,0},{8,12},{12,8},{16,20},{20,16},{24,28},{28,24},{32,36},... | collective-permute-start | bytes 393224 | tf_op jit(solution)/shard_map/ppermute | solution.py:276
  17.5 1.0 %collective-permute-done.3.other_ref = bf16[512,128]{1,0:T(8,128)(2,1)S(1)} collective-permute-done((bf16[512,128]{1,0:T(8,128)(2,1)S(1)}, bf16[512,128]{1,0:T(8,128)(2,1)S(1)}, u32[]{:S(2)}, u32[]{:S(2)}) %collective-permute-start.3) | collective-permute-done | bytes 131104 | tf_op jit(solution)/shard_map/ppermute | solution.py:276
  18.5 0.5 %attend_kernel.1 = (bf16[1024,128]{1,0:T(8,128)(2,1)S(1)}, f32[256,1024]{1,0:T(8,128)S(1)}, f32[2,256]{1,0:T(2,128)S(1)}) custom-call(s32[1,128]{1,0:T(1,128)S(1)} %broadcast_in_dim.3.odd_ref, bf16[512,128]{1,0:T(8,128)(2,1)S(1)} %get-tuple-element.45.mine_ref, bf16[512,128]{1,0:T(8,128)(2,1)S(1)} %collective-permute-done.3.other_ref, ...), custom_call_target="tpu_custom_call" | custom-call | flops 67108864 | bytes 4196864 | tf_op jit(solution)/shard_map/attend_kernel/pallas_call | solution.py:248
  19.0 3.0 %collective-permute-start.6 = (f32[2,256]{1,0:T(2,128)S(1)}, f32[2,256]{1,0:T(2,128)S(1)}, u32[]{:S(2)}, u32[]{:S(2)}) collective-permute-start(f32[2,256]{1,0:T(2,128)S(1)} %get-tuple-element.50.s0), channel_id=1, source_target_pairs={{0,2},{1,3},{2,0},{3,1},{4,6},{5,7},{6,4},{7,5},{8,10},{9,11},{10,... | collective-permute-start | bytes 6152 | tf_op jit(solution)/shard_map/ppermute | solution.py:308
  22.0 0.8 %collective-permute-start.5 = (f32[2,256]{1,0:T(2,128)S(1)}, f32[2,256]{1,0:T(2,128)S(1)}, u32[]{:S(2)}, u32[]{:S(2)}) collective-permute-start(f32[2,256]{1,0:T(2,128)S(1)} %get-tuple-element.50.s0), channel_id=1, source_target_pairs={{0,3},{1,2},{2,1},{3,0},{4,7},{5,6},{6,5},{7,4},{8,11},{9,10},{10,... | collective-permute-start | bytes 6152 | tf_op jit(solution)/shard_map/ppermute | solution.py:308
  22.8 0.0 collective-permute-start.4
  22.8 0.2 collective-permute-done.6.s3
  23.0 2.6 %collective-permute-done.5.s2 = f32[2,256]{1,0:T(2,128)S(1)} collective-permute-done((f32[2,256]{1,0:T(2,128)S(1)}, f32[2,256]{1,0:T(2,128)S(1)}, u32[]{:S(2)}, u32[]{:S(2)}) %collective-permute-start.5) | collective-permute-done | bytes 2080 | tf_op jit(solution)/shard_map/ppermute | solution.py:308
  25.7 0.0 collective-permute-done.4.s1
  25.7 0.5 %lead_kernel.1 = (bf16[256,1024]{1,0:T(8,128)(2,1)S(1)}, bf16[1040,128]{1,0:T(8,128)(2,1)S(1)}) custom-call(s32[1,256]{1,0:T(1,128)S(1)} %get-tuple-element.54.ids_ref, f32[2,256]{1,0:T(2,128)S(1)} %get-tuple-element.50.s0, f32[2,256]{1,0:T(2,128)S(1)} %collective-permute-done.4.s1, f32[2,256]{1,0:T(2,128)S(1)} %collective-permute-done.5.s2, ...), custom_call_target="tpu_custom_call" | custom-call | flops 67108864 | bytes 3421184 | tf_op jit(solution)/shard_map/lead_kernel/pallas_call | solution.py:248
  26.2 0.0 copy-start
  26.2 0.0 copy-start.1
  26.2 1.9 %collective-permute-start.7 = (bf16[1040,128]{1,0:T(8,128)(2,1)S(1)}, bf16[1040,128]{1,0:T(8,128)(2,1)S(1)}, u32[]{:S(2)}, u32[]{:S(2)}) collective-permute-start(bf16[1040,128]{1,0:T(8,128)(2,1)S(1)} %get-tuple-element.53.keep_ref.send_ref.mine_ref), channel_id=1, source_target_pairs={{0,4},{4,0},{8,12},{12,8},{16,20},{20,16},{24,28},{28,24},{32,36},... | collective-permute-start | bytes 798728 | tf_op jit(solution)/shard_map/ppermute | solution.py:276
  28.1 1.2 %collective-permute-done.7.theirs_ref = bf16[1040,128]{1,0:T(8,128)(2,1)S(1)} collective-permute-done((bf16[1040,128]{1,0:T(8,128)(2,1)S(1)}, bf16[1040,128]{1,0:T(8,128)(2,1)S(1)}, u32[]{:S(2)}, u32[]{:S(2)}) %collective-permute-start.7) | collective-permute-done | bytes 266272 | tf_op jit(solution)/shard_map/ppermute | solution.py:276
  29.2 0.1 chip_lead.1
  29.3 6.2 %collective-permute-start.8 = (bf16[1040,128]{1,0:T(8,128)(2,1)S(1)}, bf16[1040,128]{1,0:T(8,128)(2,1)S(1)}, u32[]{:S(2)}, u32[]{:S(2)}) collective-permute-start(bf16[1040,128]{1,0:T(8,128)(2,1)S(1)} %chip_lead.1), channel_id=1, source_target_pairs={{0,248},{4,244},{8,0},{12,252},{16,8},{20,4},{24,16},{28,12},{32,2... | collective-permute-start | bytes 798728 | tf_op jit(solution)/shard_map/ppermute | solution.py:313
  35.5 0.0 copy-done
  35.5 0.0 copy-done.1
  35.5 3.9 %back_kernel.1 = (bf16[256,1024]{1,0:T(8,128)(2,1)}, bf16[256,1024]{1,0:T(8,128)(2,1)}, f32[256,1024]{1,0:T(8,128)S(1)}, f32[256,1024]{1,0:T(8,128)S(1)}, bf16[2...) custom-call(s32[1,256]{1,0:T(1,128)S(1)} %get-tuple-element.54.ids_ref, f32[2,256]{1,0:T(2,128)S(1)} %get-tuple-element.50.s0, ...), custom_call_target="tpu_custom_call" | custom-call | flops 671088640 | bytes 10232832 | tf_op jit(solution)/shard_map/back_kernel/pallas_call | solution.py:248
  39.4 3.2 %collective-permute-done.8.came_ref = bf16[1040,128]{1,0:T(8,128)(2,1)S(1)} collective-permute-done((bf16[1040,128]{1,0:T(8,128)(2,1)S(1)}, bf16[1040,128]{1,0:T(8,128)(2,1)S(1)}, u32[]{:S(2)}, u32[]{:S(2)}) %collective-permute-start.8) | collective-permute-done | bytes 266272 | tf_op jit(solution)/shard_map/ppermute | solution.py:313
  42.6 2.4 %collective-permute-start.9 = (bf16[1040,128]{1,0:T(8,128)(2,1)S(1)}, bf16[1040,128]{1,0:T(8,128)(2,1)S(1)}, u32[]{:S(2)}, u32[]{:S(2)}) collective-permute-start(bf16[1040,128]{1,0:T(8,128)(2,1)S(1)} %collective-permute-done.8.came_ref), channel_id=1, source_target_pairs={{0,4},{4,0},{8,12},{12,8},{16,20},{20,16},{24,28},{28,24},{32,36},... | collective-permute-start | bytes 798728 | tf_op jit(solution)/shard_map/ppermute | solution.py:276
  45.0 1.2 %collective-permute-done.9.other_ref = bf16[1040,128]{1,0:T(8,128)(2,1)S(1)} collective-permute-done((bf16[1040,128]{1,0:T(8,128)(2,1)S(1)}, bf16[1040,128]{1,0:T(8,128)(2,1)S(1)}, u32[]{:S(2)}, u32[]{:S(2)}) %collective-permute-start.9) | collective-permute-done | bytes 266272 | tf_op jit(solution)/shard_map/ppermute | solution.py:276
  46.2 1.4 %finish_kernel.1 = (bf16[256,1024]{1,0:T(8,128)(2,1)}, bf16[256,1024]{1,0:T(8,128)(2,1)}) custom-call(s32[1,128]{1,0:T(1,128)S(1)} %broadcast_in_dim.3.odd_ref, bf16[1040,128]{1,0:T(8,128)(2,1)S(1)} %get-tuple-element.53.keep_ref.send_ref.mine_ref, bf16[1040,128]{1,0:T(8,128)(2,1)S(1)} %collective-permute-done.7.theirs_ref, ...), custom_call_target="tpu_custom_call" | custom-call | flops 134217728 | bytes 5259776 | tf_op jit(solution)/shard_map/finish_kernel/pallas_call | solution.py:248
  (1 shorter events, 0.0 us)
Async XLA Ops:
  2.2 4.3 %collective-permute-start = (bf16[528,128]{1,0:T(8,128)(2,1)S(1)}, bf16[528,128]{1,0:T(8,128)(2,1)S(1)}, u32[]{:S(2)}, u32[]{:S(2)}) collective-permute-start(bf16[528,128]{1,0:T(8,128)(2,1)S(1)} %get-tuple-element.38.send_ref), channel_id=1, source_target_pairs={{0,4},{4,0},{8,12},{12,8},{16,20},{20,16},{24,28},{28,24},{32,36},... | collective-permute-start | bytes 405512 | tf_op jit(solution)/shard_map/ppermute | solution.py:276
  6.6 9.8 %collective-permute-start.2 = (bf16[528,128]{1,0:T(8,128)(2,1)S(1)}, bf16[528,128]{1,0:T(8,128)(2,1)S(1)}, u32[]{:S(2)}, u32[]{:S(2)}) collective-permute-start(bf16[528,128]{1,0:T(8,128)(2,1)S(1)} %chip_tail.1), channel_id=1, source_target_pairs={{0,8},{4,12},{8,16},{12,20},{16,24},{20,28},{24,32},{28,36},{32,40... | collective-permute-start | bytes 405512 | tf_op jit(solution)/shard_map/ppermute | solution.py:280
  6.7 9.7 %collective-permute-start.1 = (bf16[528,128]{1,0:T(8,128)(2,1)S(1)}, bf16[528,128]{1,0:T(8,128)(2,1)S(1)}, u32[]{:S(2)}, u32[]{:S(2)}) collective-permute-start(bf16[528,128]{1,0:T(8,128)(2,1)S(1)} %chip_tail.1), channel_id=1, source_target_pairs={{0,16},{4,20},{8,24},{12,28},{16,32},{20,36},{24,40},{28,44},{32,4... | collective-permute-start | bytes 405512 | tf_op jit(solution)/shard_map/ppermute | solution.py:280
  16.5 2.0 %collective-permute-start.3 = (bf16[512,128]{1,0:T(8,128)(2,1)S(1)}, bf16[512,128]{1,0:T(8,128)(2,1)S(1)}, u32[]{:S(2)}, u32[]{:S(2)}) collective-permute-start(bf16[512,128]{1,0:T(8,128)(2,1)S(1)} %get-tuple-element.46), channel_id=1, source_target_pairs={{0,4},{4,0},{8,12},{12,8},{16,20},{20,16},{24,28},{28,24},{32,36},... | collective-permute-start | bytes 393224 | tf_op jit(solution)/shard_map/ppermute | solution.py:276
  19.0 4.0 %collective-permute-start.6 = (f32[2,256]{1,0:T(2,128)S(1)}, f32[2,256]{1,0:T(2,128)S(1)}, u32[]{:S(2)}, u32[]{:S(2)}) collective-permute-start(f32[2,256]{1,0:T(2,128)S(1)} %get-tuple-element.50.s0), channel_id=1, source_target_pairs={{0,2},{1,3},{2,0},{3,1},{4,6},{5,7},{6,4},{7,5},{8,10},{9,11},{10,... | collective-permute-start | bytes 6152 | tf_op jit(solution)/shard_map/ppermute | solution.py:308
  22.0 3.6 %collective-permute-start.5 = (f32[2,256]{1,0:T(2,128)S(1)}, f32[2,256]{1,0:T(2,128)S(1)}, u32[]{:S(2)}, u32[]{:S(2)}) collective-permute-start(f32[2,256]{1,0:T(2,128)S(1)} %get-tuple-element.50.s0), channel_id=1, source_target_pairs={{0,3},{1,2},{2,1},{3,0},{4,7},{5,6},{6,5},{7,4},{8,11},{9,10},{10,... | collective-permute-start | bytes 6152 | tf_op jit(solution)/shard_map/ppermute | solution.py:308
  22.8 2.9 %collective-permute-start.4 = (f32[2,256]{1,0:T(2,128)S(1)}, f32[2,256]{1,0:T(2,128)S(1)}, u32[]{:S(2)}, u32[]{:S(2)}) collective-permute-start(f32[2,256]{1,0:T(2,128)S(1)} %get-tuple-element.50.s0), channel_id=1, source_target_pairs={{0,1},{1,0},{2,3},{3,2},{4,5},{5,4},{6,7},{7,6},{8,9},{9,8},{10,11... | collective-permute-start | bytes 6152 | tf_op jit(solution)/shard_map/ppermute | solution.py:308
  26.2 9.3 %copy-start = (bf16[256,1024]{1,0:T(8,128)(2,1)S(1)}, bf16[256,1024]{1,0:T(8,128)(2,1)}, u32[]{:S(2)}) copy-start(bf16[256,1024]{1,0:T(8,128)(2,1)} %q_ref.1) | copy-start | bytes 1572868
  26.2 9.3 %copy-start.1 = (bf16[256,1024]{1,0:T(8,128)(2,1)S(1)}, bf16[256,1024]{1,0:T(8,128)(2,1)}, u32[]{:S(2)}) copy-start(bf16[256,1024]{1,0:T(8,128)(2,1)} %g_ref.1) | copy-start | bytes 1572868
  26.2 3.0 %collective-permute-start.7 = (bf16[1040,128]{1,0:T(8,128)(2,1)S(1)}, bf16[1040,128]{1,0:T(8,128)(2,1)S(1)}, u32[]{:S(2)}, u32[]{:S(2)}) collective-permute-start(bf16[1040,128]{1,0:T(8,128)(2,1)S(1)} %get-tuple-element.53.keep_ref.send_ref.mine_ref), channel_id=1, source_target_pairs={{0,4},{4,0},{8,12},{12,8},{16,20},{20,16},{24,28},{28,24},{32,36},... | collective-permute-start | bytes 798728 | tf_op jit(solution)/shard_map/ppermute | solution.py:276
  29.3 13.3 %collective-permute-start.8 = (bf16[1040,128]{1,0:T(8,128)(2,1)S(1)}, bf16[1040,128]{1,0:T(8,128)(2,1)S(1)}, u32[]{:S(2)}, u32[]{:S(2)}) collective-permute-start(bf16[1040,128]{1,0:T(8,128)(2,1)S(1)} %chip_lead.1), channel_id=1, source_target_pairs={{0,248},{4,244},{8,0},{12,252},{16,8},{20,4},{24,16},{28,12},{32,2... | collective-permute-start | bytes 798728 | tf_op jit(solution)/shard_map/ppermute | solution.py:313
  42.6 3.6 %collective-permute-start.9 = (bf16[1040,128]{1,0:T(8,128)(2,1)S(1)}, bf16[1040,128]{1,0:T(8,128)(2,1)S(1)}, u32[]{:S(2)}, u32[]{:S(2)}) collective-permute-start(bf16[1040,128]{1,0:T(8,128)(2,1)S(1)} %collective-permute-done.8.came_ref), channel_id=1, source_target_pairs={{0,4},{4,0},{8,12},{12,8},{16,20},{20,16},{24,28},{28,24},{32,36},... | collective-permute-start | bytes 798728 | tf_op jit(solution)/shard_map/ppermute | solution.py:276

commit v6 on v5

--- a/solution.py
+++ b/solution.py
@@ -71,20 +71,24 @@
     split(states, odd_ref[...] > 0, keep_ref, send_ref)
 
 
-def chip_kernel(backward, odd_ref, keep_ref, send_ref, theirs_ref, out_ref):
+def chip_kernel(backward, starts, odd_ref, keep_ref, send_ref, theirs_ref, *out_refs):
     odd = odd_ref[...] > 0
     mine_kept = ~odd if backward else odd
     which = 1 if backward else 0
     both = get_ids(send_ref)[which] == get_ids(theirs_ref)[which]
     for h in range(keep_ref.shape[0] // HEAD):
         mine, theirs = keep_ref[head(h), :].astype(F32), theirs_ref[head(h), :].astype(F32)
-        state = jnp.where(both, mine + theirs, jnp.where(mine_kept, mine, theirs))
-        out_ref[head(h), :] = state.astype(BF)
+        state = jnp.where(both, mine + theirs, jnp.where(mine_kept, mine, theirs)).astype(BF)
+        for start, ref in zip(starts, out_refs):
+            if start <= h < start + ref.shape[0] // HEAD:
+                ref[head(h - start), :] = state
     mine, theirs = send_ref[-2 * IDS :, :].astype(F32), theirs_ref[-2 * IDS :, :].astype(F32)
-    out_ref[-2 * IDS :, :] = jnp.where(mine_kept, mine, theirs).astype(BF)
-
-
-def edge_kernel(odd_ref, keep_ref, send_ref, theirs_ref, near_ref, far_ref, mine_ref, other_ref):
+    for ref in out_refs:
+        if ref.shape[0] % HEAD:
+            ref[-2 * IDS :, :] = jnp.where(mine_kept, mine, theirs).astype(BF)
+
+
+def edge_kernel(odd_ref, keep_ref, send_ref, theirs_ref, far_rear_ref, far_ref, near_ref, mine_ref, other_ref):
     odd = odd_ref[...] > 0
     ours, others = get_ids(send_ref), get_ids(theirs_ref)
     last_even = jnp.where(odd, others[0], ours[0])
@@ -93,9 +97,11 @@
     take_near, take_far = get_ids(near_ref)[0] == first_even, get_ids(far_ref)[0] == first_even
     take_part = first_odd == last_even
     take_outer = take_part & (last_even == first_even)
+    front = far_ref.shape[0] // HEAD
     for h in range(keep_ref.shape[0] // HEAD):
+        far = far_ref[head(h), :] if h < front else far_rear_ref[head(h - front), :]
         outer = jnp.where(take_near, near_ref[head(h), :].astype(F32), 0.0)
-        outer = outer + jnp.where(take_far, far_ref[head(h), :].astype(F32), 0.0)
+        outer = outer + jnp.where(take_far, far.astype(F32), 0.0)
         part = jnp.where(odd, theirs_ref[head(h), :].astype(F32), keep_ref[head(h), :].astype(F32))
         joined = jnp.where(take_part, part, 0.0) + jnp.where(take_outer, outer, 0.0)
         mine_ref[head(h), :] = jnp.where(odd, joined, outer).astype(BF)
@@ -205,24 +211,26 @@
 
 
 def finish_kernel(
-    odd_ref, mine_ref, theirs_ref, came_ref, other_ref, tail_k_ref, tail_v_ref, key_part_ref, value_part_ref,
-    key_grad_hbm, value_grad_hbm, key_grad_ref, value_grad_ref, key_sem, value_sem,
+    odd_ref, mine_ref, theirs_ref, front_ref, front_other_ref, rear_ref, rear_other_ref, tail_k_ref, tail_v_ref,
+    key_part_ref, value_part_ref, key_grad_hbm, value_grad_hbm, key_grad_ref, value_grad_ref, key_sem, value_sem,
 ):
     odd = odd_ref[...] > 0
     (last, first), (their_last, their_first) = get_ids(mine_ref), get_ids(theirs_ref)
     edge = jnp.where(odd, last, their_last)
-    take_came, take_other = get_ids(came_ref)[1] == edge, get_ids(other_ref)[1] == edge
+    take_came, take_other = get_ids(front_ref)[1] == edge, get_ids(front_other_ref)[1] == edge
     take_theirs = ~odd & (their_first == last)
     take_outer = odd | (take_theirs & (their_first == their_last))
+    came = [(front_ref, front_other_ref, h) for h in range(front_ref.shape[0] // HEAD)]
+    came += [(rear_ref, rear_other_ref, h) for h in range(rear_ref.shape[0] // HEAD)]
     copies = []
 
     def send(ref, hbm, sem, h):
         copies.append(pltpu.make_async_copy(ref.at[:, head(h)], hbm.at[:, head(h)], sem.at[h]))
         copies[-1].start()
 
-    for h in range(tail_k_ref.shape[1] // HEAD):
-        outer = jnp.where(take_came, came_ref[head(h), :].astype(F32), 0.0)
-        outer = outer + jnp.where(take_other, other_ref[head(h), :].astype(F32), 0.0)
+    for h, (came_ref, other_ref, at) in enumerate(came):
+        outer = jnp.where(take_came, came_ref[head(at), :].astype(F32), 0.0)
+        outer = outer + jnp.where(take_other, other_ref[head(at), :].astype(F32), 0.0)
         after = jnp.where(take_theirs, theirs_ref[head(h), :].astype(F32), 0.0)
         after = (after + jnp.where(take_outer, outer, 0.0)).astype(BF)
         key_grad = key_part_ref[:, head(h)] + dot(tail_v_ref[:, head(h)], after, NT)
@@ -243,7 +251,7 @@
     return pltpu.with_memory_space_constraint(x, pltpu.HBM)
 
 
-def call(kernel, outs, flops, *args, name=None, in_specs=None, out_specs=None, scratch=(), vmem=24 * MIB):
+def call(kernel, outs, flops, *args, name=None, in_specs=None, out_specs=None, scratch=()):
     size = sum(math.prod(a.shape) * jnp.dtype(a.dtype).itemsize for a in (*args, *outs))
     return pl.pallas_call(
         kernel,
@@ -251,7 +259,7 @@
         in_specs=in_specs or [VMEM] * len(args),
         out_specs=out_specs or [VMEM] * len(outs),
         scratch_shapes=scratch,
-        compiler_params=pltpu.CompilerParams(vmem_limit_bytes=vmem),
+        compiler_params=pltpu.CompilerParams(vmem_limit_bytes=24 * MIB),
         cost_estimate=pl.CostEstimate(flops=flops, bytes_accessed=size, transcendentals=0),
         name=name or kernel.__name__,
     )(*args)
@@ -279,9 +287,9 @@
         pairs = [(i, (i + blocks) % count) for i in range(count) if wrap or 0 <= i + blocks < count]
         return lax.ppermute(x, "ctx", pairs)
 
-    def chip(backward, out, *parts):
+    def chip(backward, starts, outs, *parts):
         name = "chip_lead" if backward else "chip_tail"
-        return call(functools.partial(chip_kernel, backward), [out], 0, odd, *parts, name=name)[0]
+        return call(functools.partial(chip_kernel, backward, starts), outs, 0, odd, *parts, name=name)
 
     ids, keys, values, tail, tail_sent = call(
         tail_kernel,
@@ -290,17 +298,17 @@
         in_specs=[HBM] * 3 + [VMEM], scratch=[pltpu.VMEM((states, length), BF), pltpu.SemaphoreType.DMA((3,))],
     )
     tail_theirs = swap(tail_sent)
-    state = chip(False, message, tail, tail_sent, tail_theirs)
-    far = shift(state, 4, False)
-    near = shift(state, 2)
+    outs = [message, shape((2 * HEAD + 2 * IDS, HEAD), BF), shape(((heads // 2 - 2) * HEAD, HEAD), BF)]
+    state, front, rear = chip(False, (0, 0, 2), outs, tail, tail_sent, tail_theirs)
+    near, far, far_rear = shift(state, 2), shift(front, 4), shift(rear, 4, False)
     ids, _ = lax.optimization_barrier((ids, state))
     scores, local, up, lead_q, lead_qt = call(
         local_kernel, [shape((heads, length, length), BF), wide, wide, narrow, shape((states, length), BF)], 2 * unit,
         ids, in_hbm(queries), keys, values, in_hbm(gates), in_hbm(cotangent),
         in_specs=[VMEM, HBM, VMEM, VMEM, HBM, HBM], scratch=[buffer] * 3 + [pltpu.SemaphoreType.DMA((3,))],
     )
-    far, near, local = lax.optimization_barrier((far, near, local))
-    mine, given = call(edge_kernel, [half, half], 0, odd, tail, tail_sent, tail_theirs, far, near)
+    far_rear, far, near, local = lax.optimization_barrier((far_rear, far, near, local))
+    mine, given = call(edge_kernel, [half, half], 0, odd, tail, tail_sent, tail_theirs, far_rear, far, near)
     before, attended, sums = call(
         attend_kernel, [shape((states, HEAD), BF), wide, shape((2, length), F32)], unit // 2,
         odd, mine, swap(given), lead_q, local, up,
@@ -308,18 +316,24 @@
     parts = [sums] + [lax.ppermute(sums, "tp", [(i, i ^ step) for i in range(ranks)]) for step in (1, 3, 2)]
     grad, lead = call(lead_kernel, [narrow, whole], unit // 2, ids, *parts, lead_qt, attended, up)
 
+    def spread(x, wrap):
+        pairs = [(i, i - (2 if i % 2 == 0 else 4)) for i in range(count)]
+        return lax.ppermute(x, "ctx", [(i, j % count) for i, j in pairs if wrap or j >= 0])
+
     lead_theirs = swap(lead)
-    state = chip(True, whole, lead, lead, lead_theirs)
-    came = lax.ppermute(state, "ctx", [(i, (i - (2 if i % 2 == 0 else 4)) % count) for i in range(count)])
-    ids, _ = lax.optimization_barrier((ids, state))
+    cut = 6 * heads // 8
+    outs = [shape((cut * HEAD + 2 * IDS, HEAD), BF), shape(((heads - cut) * HEAD, HEAD), BF)]
+    front, rear = chip(True, (0, cut), outs, lead, lead, lead_theirs)
+    front_came, rear_came = spread(front, True), spread(rear, False)
+    ids, _ = lax.optimization_barrier((ids, front))
     query_grad, gate_grad, key_part, value_part, tail_k, tail_v = call(
         back_kernel, [narrow, narrow, wide, wide, narrow, narrow], 5 * unit,
         ids, *parts, queries, keys, values, gates, scores, attended, up, grad, before,
     )
-    came, key_part = lax.optimization_barrier((came, key_part))
+    rear_came, front_came, key_part = lax.optimization_barrier((rear_came, front_came, key_part))
     key_grad, value_grad = call(
-        finish_kernel, [narrow, narrow], unit, odd, lead, lead_theirs, came, swap(came), tail_k, tail_v, key_part, value_part,
-        out_specs=[HBM] * 2, scratch=[buffer, buffer, sems, sems],
+        finish_kernel, [narrow, narrow], unit, odd, lead, lead_theirs, front_came, swap(front_came), rear_came,
+        swap(rear_came), tail_k, tail_v, key_part, value_part, out_specs=[HBM] * 2, scratch=[buffer, buffer, sems, sems],
     )
     return query_grad, key_grad, value_grad, gate_grad
 

time: 47.7 us -> 47.3 us (level)
  waiting for transfers between devices: 12.8 us -> 12.3 us
    ppermute x2 -> x3, starting transfers between devices: 4.86 us -> 8.16 us  [shift(): return lax.ppermute(x, 'ctx', pairs)]
    ppermute x1 -> x2, starting transfers between devices: 6.16 us -> 3.81 us  [spread(): lax.ppermute(x, 'ctx', [(i, j % count) for i, j in pairs if wrap or j >= 0])]
    ppermute x4 -> x5, starting transfers between devices: 8.6 us -> 7.69 us  [swap(): return lax.ppermute(x, 'ctx', [(i, i ^ 1) for i in range(count)])]
    ppermute x2 -> x3, waiting for transfers between devices: 2.37 us -> 1.61 us  [shift(): return lax.ppermute(x, 'ctx', pairs)]
    ppermute x1 -> x2, waiting for transfers between devices: 3.22 us -> 3.41 us  [spread(): lax.ppermute(x, 'ctx', [(i, j % count) for i, j in pairs if wrap or j >= 0])]
    ppermute x4 -> x5, waiting for transfers between devices: 4.31 us -> 4.4 us  [swap(): return lax.ppermute(x, 'ctx', [(i, i ^ 1) for i in range(count)])]
  transfers between devices with their start and end apart: 10 -> 13, of which waited for: 8 -> 8; matrix products, arithmetic and copies ran while one was open for 0% -> 0% of each run, Pallas kernels for 13% -> 14%
where the time goes in v6:
time: 47.3 us; the launch traced here: 47.1 us
  starting transfers between devices  23.4 us (49%)
  waiting for transfers between devices  12.3 us (26%)
  Pallas kernels  10.6 us (22%)
  between operations  0.75 us (2%)
    pallas_call x9, Pallas kernels, call(): pl.pallas_call(kernel, out_shape=outs, in_specs=in_specs or [VMEM] * len(...  10.6 us
    ppermute x3, starting transfers between devices, shift(): return lax.ppermute(x, 'ctx', pairs)  8.16 us
    ppermute x5, starting transfers between devices, swap(): return lax.ppermute(x, 'ctx', [(i, i ^ 1) for i in range(count)])  7.69 us
    ppermute x5, waiting for transfers between devices, swap(): return lax.ppermute(x, 'ctx', [(i, i ^ 1) for i in range(count)])  4.4 us
    ppermute x2, starting transfers between devices, spread(): lax.ppermute(x, 'ctx', [(i, j % count) for i, j in pairs if wrap or j >= 0])  3.81 us
    ppermute x3, starting transfers between devices, body(): lax.ppermute(sums, 'tp', [(i, i ^ step) for i in range(ranks)])  3.78 us
    ppermute x2, waiting for transfers between devices, spread(): lax.ppermute(x, 'ctx', [(i, j % count) for i, j in pairs if wrap or j >= 0])  3.41 us
    ppermute x3, waiting for transfers between devices, body(): lax.ppermute(sums, 'tp', [(i, i ^ step) for i in range(ranks)])  2.87 us
  transfers between devices with their start and end apart: 13, of which 8 were waited for; matrix products, arithmetic and copies ran while one was open for 0% of the time, Pallas kernels for 14%

profile of v6, /device:TPU:1, one launch (start us, length us, event | category | flops | bytes accessed | tf_op | source)
XLA Modules:
  0.0 47.1 jit_solution(10808958864464984120)
XLA Ops:
  0.6 1.6 %tail_kernel.1 = (s32[1,256]{1,0:T(1,128)S(1)}, bf16[256,1024]{1,0:T(8,128)(2,1)S(1)}, bf16[256,1024]{1,0:T(8,128)(2,1)S(1)}, bf16[512,128]{1,0:T(8,128)(2,1)S(1)}, bf16[528,128]{1,0:T(8,128)(2,1)S(1)}) custom-call(s32[1,256]{1,0:T(1,128)} %bitcast.1, bf16[256,1024]{1,0:T(8,128)(2,1)} %k_hbm.1, bf16[256,1024]{1,0:T(8,128)(2,1)} %v_hbm.1, ...), custom_call_target="tpu_custom_call" | custom-call | flops 67108864 | bytes 2365952 | tf_op jit(solution)/shard_map/tail_kernel/pallas_call | solution.py:256
  2.2 3.3 %collective-permute-start = (bf16[528,128]{1,0:T(8,128)(2,1)S(1)}, bf16[528,128]{1,0:T(8,128)(2,1)S(1)}, u32[]{:S(2)}, u32[]{:S(2)}) collective-permute-start(bf16[528,128]{1,0:T(8,128)(2,1)S(1)} %get-tuple-element.45.send_ref), channel_id=1, source_target_pairs={{0,4},{4,0},{8,12},{12,8},{16,20},{20,16},{24,28},{28,24},{32,36},... | collective-permute-start | bytes 405512 | tf_op jit(solution)/shard_map/ppermute | solution.py:284
  5.6 1.0 %collective-permute-done.theirs_ref = bf16[528,128]{1,0:T(8,128)(2,1)S(1)} collective-permute-done((bf16[528,128]{1,0:T(8,128)(2,1)S(1)}, bf16[528,128]{1,0:T(8,128)(2,1)S(1)}, u32[]{:S(2)}, u32[]{:S(2)}) %collective-permute-start) | collective-permute-done | bytes 135200 | tf_op jit(solution)/shard_map/ppermute | solution.py:284
  6.5 0.1 chip_tail.1
  6.6 0.1 collective-permute-start.3
  6.7 2.9 %collective-permute-start.2 = (bf16[272,128]{1,0:T(8,128)(2,1)S(1)}, bf16[272,128]{1,0:T(8,128)(2,1)S(1)}, u32[]{:S(2)}, u32[]{:S(2)}) collective-permute-start(bf16[272,128]{1,0:T(8,128)(2,1)S(1)} %get-tuple-element.49), channel_id=1, source_target_pairs={{0,16},{4,20},{8,24},{12,28},{16,32},{20,36},{24,40},{28,44},{32,4... | collective-permute-start | bytes 208904 | tf_op jit(solution)/shard_map/ppermute | solution.py:288
  9.6 5.2 %collective-permute-start.1 = (bf16[256,128]{1,0:T(8,128)(2,1)S(1)}, bf16[256,128]{1,0:T(8,128)(2,1)S(1)}, u32[]{:S(2)}, u32[]{:S(2)}) collective-permute-start(bf16[256,128]{1,0:T(8,128)(2,1)S(1)} %get-tuple-element.48), channel_id=1, source_target_pairs={{0,16},{4,20},{8,24},{12,28},{16,32},{20,36},{24,40},{28,44},{32,4... | collective-permute-start | bytes 196616 | tf_op jit(solution)/shard_map/ppermute | solution.py:288
  14.8 2.5 %local_kernel.1 = (bf16[8,256,256]{2,1,0:T(8,128)(2,1)S(1)}, f32[256,1024]{1,0:T(8,128)S(1)}, f32[256,1024]{1,0:T(8,128)S(1)}, bf16[256,1024]{1,0:T(8,128)(2,1)S(1)}, bf16[1024,256]{1,0:T(8,128)(2,1)S(1)}) custom-call(s32[1,256]{1,0:T(1,128)S(1)} %get-tuple-element.66.ids_ref, bf16[256,1024]{1,0:T(8,128)(2,1)} %q_ref.1, ...), custom_call_target="tpu_custom_call" | custom-call | flops 268435456 | bytes 6816768 | tf_op jit(solution)/shard_map/local_kernel/pallas_call | solution.py:256
  17.3 0.0 collective-permute-done.1.far_rear_ref
  17.3 1.6 %collective-permute-done.2.far_ref = bf16[272,128]{1,0:T(8,128)(2,1)S(1)} collective-permute-done((bf16[272,128]{1,0:T(8,128)(2,1)S(1)}, bf16[272,128]{1,0:T(8,128)(2,1)S(1)}, u32[]{:S(2)}, u32[]{:S(2)}) %collective-permute-start.2) | collective-permute-done | bytes 69664 | tf_op jit(solution)/shard_map/ppermute | solution.py:288
  18.9 0.0 collective-permute-done.3.near_ref
  18.9 0.1 edge_kernel.1
  19.1 1.7 %collective-permute-start.4 = (bf16[512,128]{1,0:T(8,128)(2,1)S(1)}, bf16[512,128]{1,0:T(8,128)(2,1)S(1)}, u32[]{:S(2)}, u32[]{:S(2)}) collective-permute-start(bf16[512,128]{1,0:T(8,128)(2,1)S(1)} %get-tuple-element.57), channel_id=1, source_target_pairs={{0,4},{4,0},{8,12},{12,8},{16,20},{20,16},{24,28},{28,24},{32,36},... | collective-permute-start | bytes 393224 | tf_op jit(solution)/shard_map/ppermute | solution.py:284
  20.8 1.0 %collective-permute-done.4.other_ref = bf16[512,128]{1,0:T(8,128)(2,1)S(1)} collective-permute-done((bf16[512,128]{1,0:T(8,128)(2,1)S(1)}, bf16[512,128]{1,0:T(8,128)(2,1)S(1)}, u32[]{:S(2)}, u32[]{:S(2)}) %collective-permute-start.4) | collective-permute-done | bytes 131104 | tf_op jit(solution)/shard_map/ppermute | solution.py:284
  21.8 0.5 %attend_kernel.1 = (bf16[1024,128]{1,0:T(8,128)(2,1)S(1)}, f32[256,1024]{1,0:T(8,128)S(1)}, f32[2,256]{1,0:T(2,128)S(1)}) custom-call(s32[1,128]{1,0:T(1,128)S(1)} %broadcast_in_dim.3.odd_ref, bf16[512,128]{1,0:T(8,128)(2,1)S(1)} %get-tuple-element.56.mine_ref, bf16[512,128]{1,0:T(8,128)(2,1)S(1)} %collective-permute-done.4.other_ref, ...), custom_call_target="tpu_custom_call" | custom-call | flops 67108864 | bytes 4196864 | tf_op jit(solution)/shard_map/attend_kernel/pallas_call | solution.py:256
  22.3 3.0 %collective-permute-start.7 = (f32[2,256]{1,0:T(2,128)S(1)}, f32[2,256]{1,0:T(2,128)S(1)}, u32[]{:S(2)}, u32[]{:S(2)}) collective-permute-start(f32[2,256]{1,0:T(2,128)S(1)} %get-tuple-element.61.s0), channel_id=1, source_target_pairs={{0,2},{1,3},{2,0},{3,1},{4,6},{5,7},{6,4},{7,5},{8,10},{9,11},{10,... | collective-permute-start | bytes 6152 | tf_op jit(solution)/shard_map/ppermute | solution.py:316
  25.3 0.8 %collective-permute-start.6 = (f32[2,256]{1,0:T(2,128)S(1)}, f32[2,256]{1,0:T(2,128)S(1)}, u32[]{:S(2)}, u32[]{:S(2)}) collective-permute-start(f32[2,256]{1,0:T(2,128)S(1)} %get-tuple-element.61.s0), channel_id=1, source_target_pairs={{0,3},{1,2},{2,1},{3,0},{4,7},{5,6},{6,5},{7,4},{8,11},{9,10},{10,... | collective-permute-start | bytes 6152 | tf_op jit(solution)/shard_map/ppermute | solution.py:316
  26.1 0.0 collective-permute-start.5
  26.1 0.2 collective-permute-done.7.s3
  26.3 2.6 %collective-permute-done.6.s2 = f32[2,256]{1,0:T(2,128)S(1)} collective-permute-done((f32[2,256]{1,0:T(2,128)S(1)}, f32[2,256]{1,0:T(2,128)S(1)}, u32[]{:S(2)}, u32[]{:S(2)}) %collective-permute-start.6) | collective-permute-done | bytes 2080 | tf_op jit(solution)/shard_map/ppermute | solution.py:316
  29.0 0.0 collective-permute-done.5.s1
  29.0 0.0 copy-start.1
  29.0 0.5 %lead_kernel.1 = (bf16[256,1024]{1,0:T(8,128)(2,1)S(1)}, bf16[1040,128]{1,0:T(8,128)(2,1)S(1)}) custom-call(s32[1,256]{1,0:T(1,128)S(1)} %get-tuple-element.66.ids_ref, f32[2,256]{1,0:T(2,128)S(1)} %get-tuple-element.61.s0, f32[2,256]{1,0:T(2,128)S(1)} %collective-permute-done.5.s1, f32[2,256]{1,0:T(2,128)S(1)} %collective-permute-done.6.s2, ...), custom_call_target="tpu_custom_call" | custom-call | flops 67108864 | bytes 3421184 | tf_op jit(solution)/shard_map/lead_kernel/pallas_call | solution.py:256
  29.5 0.0 copy-start
  29.5 1.9 %collective-permute-start.8 = (bf16[1040,128]{1,0:T(8,128)(2,1)S(1)}, bf16[1040,128]{1,0:T(8,128)(2,1)S(1)}, u32[]{:S(2)}, u32[]{:S(2)}) collective-permute-start(bf16[1040,128]{1,0:T(8,128)(2,1)S(1)} %get-tuple-element.64.keep_ref.send_ref.mine_ref), channel_id=1, source_target_pairs={{0,4},{4,0},{8,12},{12,8},{16,20},{20,16},{24,28},{28,24},{32,36},... | collective-permute-start | bytes 798728 | tf_op jit(solution)/shard_map/ppermute | solution.py:284
  31.4 1.2 %collective-permute-done.8.theirs_ref = bf16[1040,128]{1,0:T(8,128)(2,1)S(1)} collective-permute-done((bf16[1040,128]{1,0:T(8,128)(2,1)S(1)}, bf16[1040,128]{1,0:T(8,128)(2,1)S(1)}, u32[]{:S(2)}, u32[]{:S(2)}) %collective-permute-start.8) | collective-permute-done | bytes 266272 | tf_op jit(solution)/shard_map/ppermute | solution.py:284
  32.5 0.1 chip_lead.1
  32.6 2.5 %collective-permute-start.10 = (bf16[784,128]{1,0:T(8,128)(2,1)S(1)}, bf16[784,128]{1,0:T(8,128)(2,1)S(1)}, u32[]{:S(2)}, u32[]{:S(2)}) collective-permute-start(bf16[784,128]{1,0:T(8,128)(2,1)S(1)} %get-tuple-element.65), channel_id=1, source_target_pairs={{0,248},{4,244},{8,0},{12,252},{16,8},{20,4},{24,16},{28,12},{32,2... | collective-permute-start | bytes 602120 | tf_op jit(solution)/shard_map/ppermute | solution.py:321
  35.2 1.3 %collective-permute-start.9 = (bf16[256,128]{1,0:T(8,128)(2,1)S(1)}, bf16[256,128]{1,0:T(8,128)(2,1)S(1)}, u32[]{:S(2)}, u32[]{:S(2)}) collective-permute-start(bf16[256,128]{1,0:T(8,128)(2,1)S(1)} %get-tuple-element.71), channel_id=1, source_target_pairs={{8,0},{16,8},{20,4},{24,16},{28,12},{32,24},{36,20},{40,32},{44,28... | collective-permute-start | bytes 196616 | tf_op jit(solution)/shard_map/ppermute | solution.py:321
  36.4 0.0 copy-done.1
  36.5 0.0 copy-done
  36.5 3.9 %back_kernel.1 = (bf16[256,1024]{1,0:T(8,128)(2,1)}, bf16[256,1024]{1,0:T(8,128)(2,1)}, f32[256,1024]{1,0:T(8,128)S(1)}, f32[256,1024]{1,0:T(8,128)S(1)}, bf16[2...) custom-call(s32[1,256]{1,0:T(1,128)S(1)} %get-tuple-element.66.ids_ref, f32[2,256]{1,0:T(2,128)S(1)} %get-tuple-element.61.s0, ...), custom_call_target="tpu_custom_call" | custom-call | flops 671088640 | bytes 10232832 | tf_op jit(solution)/shard_map/back_kernel/pallas_call | solution.py:256
  40.3 3.4 %collective-permute-done.9.rear_ref = bf16[256,128]{1,0:T(8,128)(2,1)S(1)} collective-permute-done((bf16[256,128]{1,0:T(8,128)(2,1)S(1)}, bf16[256,128]{1,0:T(8,128)(2,1)S(1)}, u32[]{:S(2)}, u32[]{:S(2)}) %collective-permute-start.9) | collective-permute-done | bytes 65568 | tf_op jit(solution)/shard_map/ppermute | solution.py:321
  43.8 0.0 collective-permute-done.10.front_ref
  43.8 0.7 %collective-permute-start.11 = (bf16[784,128]{1,0:T(8,128)(2,1)S(1)}, bf16[784,128]{1,0:T(8,128)(2,1)S(1)}, u32[]{:S(2)}, u32[]{:S(2)}) collective-permute-start(bf16[784,128]{1,0:T(8,128)(2,1)S(1)} %collective-permute-done.10.front_ref), channel_id=1, source_target_pairs={{0,4},{4,0},{8,12},{12,8},{16,20},{20,16},{24,28},{28,24},{32,36},... | collective-permute-start | bytes 602120 | tf_op jit(solution)/shard_map/ppermute | solution.py:284
  44.5 0.0 collective-permute-start.12
  44.5 1.3 %collective-permute-done.12.rear_other_ref = bf16[256,128]{1,0:T(8,128)(2,1)S(1)} collective-permute-done((bf16[256,128]{1,0:T(8,128)(2,1)S(1)}, bf16[256,128]{1,0:T(8,128)(2,1)S(1)}, u32[]{:S(2)}, u32[]{:S(2)}) %collective-permute-start.12) | collective-permute-done | bytes 65568 | tf_op jit(solution)/shard_map/ppermute | solution.py:284
  45.8 0.0 collective-permute-done.11.front_other_ref
  45.8 1.4 %finish_kernel.1 = (bf16[256,1024]{1,0:T(8,128)(2,1)}, bf16[256,1024]{1,0:T(8,128)(2,1)}) custom-call(s32[1,128]{1,0:T(1,128)S(1)} %broadcast_in_dim.3.odd_ref, bf16[1040,128]{1,0:T(8,128)(2,1)S(1)} %get-tuple-element.64.keep_ref.send_ref.mine_ref, bf16[1040,128]{1,0:T(8,128)(2,1)S(1)} %collective-permute-done.8.theirs_ref, ...), custom_call_target="tpu_custom_call" | custom-call | flops 134217728 | bytes 5259776 | tf_op jit(solution)/shard_map/finish_kernel/pallas_call | solution.py:256
  (1 shorter events, 0.0 us)
Async XLA Ops:
  2.2 4.3 %collective-permute-start = (bf16[528,128]{1,0:T(8,128)(2,1)S(1)}, bf16[528,128]{1,0:T(8,128)(2,1)S(1)}, u32[]{:S(2)}, u32[]{:S(2)}) collective-permute-start(bf16[528,128]{1,0:T(8,128)(2,1)S(1)} %get-tuple-element.45.send_ref), channel_id=1, source_target_pairs={{0,4},{4,0},{8,12},{12,8},{16,20},{20,16},{24,28},{28,24},{32,36},... | collective-permute-start | bytes 405512 | tf_op jit(solution)/shard_map/ppermute | solution.py:284
  6.6 12.3 %collective-permute-start.3 = (bf16[528,128]{1,0:T(8,128)(2,1)S(1)}, bf16[528,128]{1,0:T(8,128)(2,1)S(1)}, u32[]{:S(2)}, u32[]{:S(2)}) collective-permute-start(bf16[528,128]{1,0:T(8,128)(2,1)S(1)} %get-tuple-element.46), channel_id=1, source_target_pairs={{0,8},{4,12},{8,16},{12,20},{16,24},{20,28},{24,32},{28,36},{32,40... | collective-permute-start | bytes 405512 | tf_op jit(solution)/shard_map/ppermute | solution.py:288
  6.7 12.2 %collective-permute-start.2 = (bf16[272,128]{1,0:T(8,128)(2,1)S(1)}, bf16[272,128]{1,0:T(8,128)(2,1)S(1)}, u32[]{:S(2)}, u32[]{:S(2)}) collective-permute-start(bf16[272,128]{1,0:T(8,128)(2,1)S(1)} %get-tuple-element.49), channel_id=1, source_target_pairs={{0,16},{4,20},{8,24},{12,28},{16,32},{20,36},{24,40},{28,44},{32,4... | collective-permute-start | bytes 208904 | tf_op jit(solution)/shard_map/ppermute | solution.py:288
  9.6 7.7 %collective-permute-start.1 = (bf16[256,128]{1,0:T(8,128)(2,1)S(1)}, bf16[256,128]{1,0:T(8,128)(2,1)S(1)}, u32[]{:S(2)}, u32[]{:S(2)}) collective-permute-start(bf16[256,128]{1,0:T(8,128)(2,1)S(1)} %get-tuple-element.48), channel_id=1, source_target_pairs={{0,16},{4,20},{8,24},{12,28},{16,32},{20,36},{24,40},{28,44},{32,4... | collective-permute-start | bytes 196616 | tf_op jit(solution)/shard_map/ppermute | solution.py:288
  19.1 2.7 %collective-permute-start.4 = (bf16[512,128]{1,0:T(8,128)(2,1)S(1)}, bf16[512,128]{1,0:T(8,128)(2,1)S(1)}, u32[]{:S(2)}, u32[]{:S(2)}) collective-permute-start(bf16[512,128]{1,0:T(8,128)(2,1)S(1)} %get-tuple-element.57), channel_id=1, source_target_pairs={{0,4},{4,0},{8,12},{12,8},{16,20},{20,16},{24,28},{28,24},{32,36},... | collective-permute-start | bytes 393224 | tf_op jit(solution)/shard_map/ppermute | solution.py:284
  22.3 4.0 %collective-permute-start.7 = (f32[2,256]{1,0:T(2,128)S(1)}, f32[2,256]{1,0:T(2,128)S(1)}, u32[]{:S(2)}, u32[]{:S(2)}) collective-permute-start(f32[2,256]{1,0:T(2,128)S(1)} %get-tuple-element.61.s0), channel_id=1, source_target_pairs={{0,2},{1,3},{2,0},{3,1},{4,6},{5,7},{6,4},{7,5},{8,10},{9,11},{10,... | collective-permute-start | bytes 6152 | tf_op jit(solution)/shard_map/ppermute | solution.py:316
  25.3 3.6 %collective-permute-start.6 = (f32[2,256]{1,0:T(2,128)S(1)}, f32[2,256]{1,0:T(2,128)S(1)}, u32[]{:S(2)}, u32[]{:S(2)}) collective-permute-start(f32[2,256]{1,0:T(2,128)S(1)} %get-tuple-element.61.s0), channel_id=1, source_target_pairs={{0,3},{1,2},{2,1},{3,0},{4,7},{5,6},{6,5},{7,4},{8,11},{9,10},{10,... | collective-permute-start | bytes 6152 | tf_op jit(solution)/shard_map/ppermute | solution.py:316
  26.1 2.9 %collective-permute-start.5 = (f32[2,256]{1,0:T(2,128)S(1)}, f32[2,256]{1,0:T(2,128)S(1)}, u32[]{:S(2)}, u32[]{:S(2)}) collective-permute-start(f32[2,256]{1,0:T(2,128)S(1)} %get-tuple-element.61.s0), channel_id=1, source_target_pairs={{0,1},{1,0},{2,3},{3,2},{4,5},{5,4},{6,7},{7,6},{8,9},{9,8},{10,11... | collective-permute-start | bytes 6152 | tf_op jit(solution)/shard_map/ppermute | solution.py:316
  29.0 7.5 %copy-start.1 = (bf16[256,1024]{1,0:T(8,128)(2,1)S(1)}, bf16[256,1024]{1,0:T(8,128)(2,1)}, u32[]{:S(2)}) copy-start(bf16[256,1024]{1,0:T(8,128)(2,1)} %g_ref.1) | copy-start | bytes 1572868
  29.5 7.0 %copy-start = (bf16[256,1024]{1,0:T(8,128)(2,1)S(1)}, bf16[256,1024]{1,0:T(8,128)(2,1)}, u32[]{:S(2)}) copy-start(bf16[256,1024]{1,0:T(8,128)(2,1)} %q_ref.1) | copy-start | bytes 1572868
  29.5 3.0 %collective-permute-start.8 = (bf16[1040,128]{1,0:T(8,128)(2,1)S(1)}, bf16[1040,128]{1,0:T(8,128)(2,1)S(1)}, u32[]{:S(2)}, u32[]{:S(2)}) collective-permute-start(bf16[1040,128]{1,0:T(8,128)(2,1)S(1)} %get-tuple-element.64.keep_ref.send_ref.mine_ref), channel_id=1, source_target_pairs={{0,4},{4,0},{8,12},{12,8},{16,20},{20,16},{24,28},{28,24},{32,36},... | collective-permute-start | bytes 798728 | tf_op jit(solution)/shard_map/ppermute | solution.py:284
  32.6 11.1 %collective-permute-start.10 = (bf16[784,128]{1,0:T(8,128)(2,1)S(1)}, bf16[784,128]{1,0:T(8,128)(2,1)S(1)}, u32[]{:S(2)}, u32[]{:S(2)}) collective-permute-start(bf16[784,128]{1,0:T(8,128)(2,1)S(1)} %get-tuple-element.65), channel_id=1, source_target_pairs={{0,248},{4,244},{8,0},{12,252},{16,8},{20,4},{24,16},{28,12},{32,2... | collective-permute-start | bytes 602120 | tf_op jit(solution)/shard_map/ppermute | solution.py:321
  35.2 8.6 %collective-permute-start.9 = (bf16[256,128]{1,0:T(8,128)(2,1)S(1)}, bf16[256,128]{1,0:T(8,128)(2,1)S(1)}, u32[]{:S(2)}, u32[]{:S(2)}) collective-permute-start(bf16[256,128]{1,0:T(8,128)(2,1)S(1)} %get-tuple-element.71), channel_id=1, source_target_pairs={{8,0},{16,8},{20,4},{24,16},{28,12},{32,24},{36,20},{40,32},{44,28... | collective-permute-start | bytes 196616 | tf_op jit(solution)/shard_map/ppermute | solution.py:321
  43.8 2.0 %collective-permute-start.11 = (bf16[784,128]{1,0:T(8,128)(2,1)S(1)}, bf16[784,128]{1,0:T(8,128)(2,1)S(1)}, u32[]{:S(2)}, u32[]{:S(2)}) collective-permute-start(bf16[784,128]{1,0:T(8,128)(2,1)S(1)} %collective-permute-done.10.front_ref), channel_id=1, source_target_pairs={{0,4},{4,0},{8,12},{12,8},{16,20},{20,16},{24,28},{28,24},{32,36},... | collective-permute-start | bytes 602120 | tf_op jit(solution)/shard_map/ppermute | solution.py:284
  44.5 1.3 %collective-permute-start.12 = (bf16[256,128]{1,0:T(8,128)(2,1)S(1)}, bf16[256,128]{1,0:T(8,128)(2,1)S(1)}, u32[]{:S(2)}, u32[]{:S(2)}) collective-permute-start(bf16[256,128]{1,0:T(8,128)(2,1)S(1)} %collective-permute-done.9.rear_ref), channel_id=1, source_target_pairs={{0,4},{4,0},{8,12},{12,8},{16,20},{20,16},{24,28},{28,24},{32,36},... | collective-permute-start | bytes 196616 | tf_op jit(solution)/shard_map/ppermute | solution.py:284

commit v7 on v6

--- a/solution.py
+++ b/solution.py
@@ -318,7 +318,9 @@
 
     def spread(x, wrap):
         pairs = [(i, i - (2 if i % 2 == 0 else 4)) for i in range(count)]
-        return lax.ppermute(x, "ctx", [(i, j % count) for i, j in pairs if wrap or j >= 0])
+        useful = [(i, j) for i, j in pairs if j >= 0]
+        spare = [(0, count - 3), (1, count - 2), (3, count - 1)] if wrap else []
+        return lax.ppermute(x, "ctx", useful + spare)
 
     lead_theirs = swap(lead)
     cut = 6 * heads // 8

time: 47.3 us -> 46.9 us (level)
  waiting for transfers between devices: 12.3 us -> 9.91 us
  starting transfers between devices: 23.4 us -> 25.4 us
    ppermute x2, waiting for transfers between devices: 3.41 us -> 1.24 us  [spread(): return lax.ppermute(x, 'ctx', useful + spare)]
    ppermute x2, starting transfers between devices: 3.81 us -> 5.98 us  [spread(): return lax.ppermute(x, 'ctx', useful + spare)]
where the time goes in v7:
time: 46.9 us; the launch traced here: 46.7 us
  starting transfers between devices  25.4 us (54%)
  Pallas kernels  10.6 us (23%)
  waiting for transfers between devices  9.91 us (21%)
  between operations  0.75 us (2%)
    pallas_call x9, Pallas kernels, call(): pl.pallas_call(kernel, out_shape=outs, in_specs=in_specs or [VMEM] * len(...  10.6 us
    ppermute x3, starting transfers between devices, shift(): return lax.ppermute(x, 'ctx', pairs)  8.16 us
    ppermute x5, starting transfers between devices, swap(): return lax.ppermute(x, 'ctx', [(i, i ^ 1) for i in range(count)])  7.46 us
    ppermute x2, starting transfers between devices, spread(): return lax.ppermute(x, 'ctx', useful + spare)  5.98 us
    ppermute x5, waiting for transfers between devices, swap(): return lax.ppermute(x, 'ctx', [(i, i ^ 1) for i in range(count)])  4.18 us
    ppermute x3, starting transfers between devices, body(): lax.ppermute(sums, 'tp', [(i, i ^ step) for i in range(ranks)])  3.78 us
    ppermute x3, waiting for transfers between devices, body(): lax.ppermute(sums, 'tp', [(i, i ^ step) for i in range(ranks)])  2.87 us
    ppermute x3, waiting for transfers between devices, shift(): return lax.ppermute(x, 'ctx', pairs)  1.61 us
  transfers between devices with their start and end apart: 13, of which 8 were waited for; matrix products, arithmetic and copies ran while one was open for 0% of the time, Pallas kernels for 14%

profile of v7, /device:TPU:1, one launch (start us, length us, event | category | flops | bytes accessed | tf_op | source)
XLA Modules:
  0.0 46.7 jit_solution(13193783112973919012)
XLA Ops:
  0.6 1.6 %tail_kernel.1 = (s32[1,256]{1,0:T(1,128)S(1)}, bf16[256,1024]{1,0:T(8,128)(2,1)S(1)}, bf16[256,1024]{1,0:T(8,128)(2,1)S(1)}, bf16[512,128]{1,0:T(8,128)(2,1)S(1)}, bf16[528,128]{1,0:T(8,128)(2,1)S(1)}) custom-call(s32[1,256]{1,0:T(1,128)} %bitcast.1, bf16[256,1024]{1,0:T(8,128)(2,1)} %k_hbm.1, bf16[256,1024]{1,0:T(8,128)(2,1)} %v_hbm.1, ...), custom_call_target="tpu_custom_call" | custom-call | flops 67108864 | bytes 2365952 | tf_op jit(solution)/shard_map/tail_kernel/pallas_call | solution.py:256
  2.2 3.3 %collective-permute-start = (bf16[528,128]{1,0:T(8,128)(2,1)S(1)}, bf16[528,128]{1,0:T(8,128)(2,1)S(1)}, u32[]{:S(2)}, u32[]{:S(2)}) collective-permute-start(bf16[528,128]{1,0:T(8,128)(2,1)S(1)} %get-tuple-element.45.send_ref), channel_id=1, source_target_pairs={{0,4},{4,0},{8,12},{12,8},{16,20},{20,16},{24,28},{28,24},{32,36},... | collective-permute-start | bytes 405512 | tf_op jit(solution)/shard_map/ppermute | solution.py:284
  5.6 1.0 %collective-permute-done.theirs_ref = bf16[528,128]{1,0:T(8,128)(2,1)S(1)} collective-permute-done((bf16[528,128]{1,0:T(8,128)(2,1)S(1)}, bf16[528,128]{1,0:T(8,128)(2,1)S(1)}, u32[]{:S(2)}, u32[]{:S(2)}) %collective-permute-start) | collective-permute-done | bytes 135200 | tf_op jit(solution)/shard_map/ppermute | solution.py:284
  6.5 0.1 chip_tail.1
  6.6 0.1 collective-permute-start.3
  6.7 2.9 %collective-permute-start.2 = (bf16[272,128]{1,0:T(8,128)(2,1)S(1)}, bf16[272,128]{1,0:T(8,128)(2,1)S(1)}, u32[]{:S(2)}, u32[]{:S(2)}) collective-permute-start(bf16[272,128]{1,0:T(8,128)(2,1)S(1)} %get-tuple-element.49), channel_id=1, source_target_pairs={{0,16},{4,20},{8,24},{12,28},{16,32},{20,36},{24,40},{28,44},{32,4... | collective-permute-start | bytes 208904 | tf_op jit(solution)/shard_map/ppermute | solution.py:288
  9.6 5.2 %collective-permute-start.1 = (bf16[256,128]{1,0:T(8,128)(2,1)S(1)}, bf16[256,128]{1,0:T(8,128)(2,1)S(1)}, u32[]{:S(2)}, u32[]{:S(2)}) collective-permute-start(bf16[256,128]{1,0:T(8,128)(2,1)S(1)} %get-tuple-element.48), channel_id=1, source_target_pairs={{0,16},{4,20},{8,24},{12,28},{16,32},{20,36},{24,40},{28,44},{32,4... | collective-permute-start | bytes 196616 | tf_op jit(solution)/shard_map/ppermute | solution.py:288
  14.8 2.5 %local_kernel.1 = (bf16[8,256,256]{2,1,0:T(8,128)(2,1)S(1)}, f32[256,1024]{1,0:T(8,128)S(1)}, f32[256,1024]{1,0:T(8,128)S(1)}, bf16[256,1024]{1,0:T(8,128)(2,1)S(1)}, bf16[1024,256]{1,0:T(8,128)(2,1)S(1)}) custom-call(s32[1,256]{1,0:T(1,128)S(1)} %get-tuple-element.66.ids_ref, bf16[256,1024]{1,0:T(8,128)(2,1)} %q_ref.1, ...), custom_call_target="tpu_custom_call" | custom-call | flops 268435456 | bytes 6816768 | tf_op jit(solution)/shard_map/local_kernel/pallas_call | solution.py:256
  17.3 0.0 collective-permute-done.1.far_rear_ref
  17.3 1.6 %collective-permute-done.2.far_ref = bf16[272,128]{1,0:T(8,128)(2,1)S(1)} collective-permute-done((bf16[272,128]{1,0:T(8,128)(2,1)S(1)}, bf16[272,128]{1,0:T(8,128)(2,1)S(1)}, u32[]{:S(2)}, u32[]{:S(2)}) %collective-permute-start.2) | collective-permute-done | bytes 69664 | tf_op jit(solution)/shard_map/ppermute | solution.py:288
  18.9 0.0 collective-permute-done.3.near_ref
  18.9 0.1 edge_kernel.1
  19.1 1.7 %collective-permute-start.4 = (bf16[512,128]{1,0:T(8,128)(2,1)S(1)}, bf16[512,128]{1,0:T(8,128)(2,1)S(1)}, u32[]{:S(2)}, u32[]{:S(2)}) collective-permute-start(bf16[512,128]{1,0:T(8,128)(2,1)S(1)} %get-tuple-element.57), channel_id=1, source_target_pairs={{0,4},{4,0},{8,12},{12,8},{16,20},{20,16},{24,28},{28,24},{32,36},... | collective-permute-start | bytes 393224 | tf_op jit(solution)/shard_map/ppermute | solution.py:284
  20.8 1.0 %collective-permute-done.4.other_ref = bf16[512,128]{1,0:T(8,128)(2,1)S(1)} collective-permute-done((bf16[512,128]{1,0:T(8,128)(2,1)S(1)}, bf16[512,128]{1,0:T(8,128)(2,1)S(1)}, u32[]{:S(2)}, u32[]{:S(2)}) %collective-permute-start.4) | collective-permute-done | bytes 131104 | tf_op jit(solution)/shard_map/ppermute | solution.py:284
  21.8 0.5 %attend_kernel.1 = (bf16[1024,128]{1,0:T(8,128)(2,1)S(1)}, f32[256,1024]{1,0:T(8,128)S(1)}, f32[2,256]{1,0:T(2,128)S(1)}) custom-call(s32[1,128]{1,0:T(1,128)S(1)} %broadcast_in_dim.3.odd_ref, bf16[512,128]{1,0:T(8,128)(2,1)S(1)} %get-tuple-element.56.mine_ref, bf16[512,128]{1,0:T(8,128)(2,1)S(1)} %collective-permute-done.4.other_ref, ...), custom_call_target="tpu_custom_call" | custom-call | flops 67108864 | bytes 4196864 | tf_op jit(solution)/shard_map/attend_kernel/pallas_call | solution.py:256
  22.3 3.0 %collective-permute-start.7 = (f32[2,256]{1,0:T(2,128)S(1)}, f32[2,256]{1,0:T(2,128)S(1)}, u32[]{:S(2)}, u32[]{:S(2)}) collective-permute-start(f32[2,256]{1,0:T(2,128)S(1)} %get-tuple-element.61.s0), channel_id=1, source_target_pairs={{0,2},{1,3},{2,0},{3,1},{4,6},{5,7},{6,4},{7,5},{8,10},{9,11},{10,... | collective-permute-start | bytes 6152 | tf_op jit(solution)/shard_map/ppermute | solution.py:316
  25.3 0.8 %collective-permute-start.6 = (f32[2,256]{1,0:T(2,128)S(1)}, f32[2,256]{1,0:T(2,128)S(1)}, u32[]{:S(2)}, u32[]{:S(2)}) collective-permute-start(f32[2,256]{1,0:T(2,128)S(1)} %get-tuple-element.61.s0), channel_id=1, source_target_pairs={{0,3},{1,2},{2,1},{3,0},{4,7},{5,6},{6,5},{7,4},{8,11},{9,10},{10,... | collective-permute-start | bytes 6152 | tf_op jit(solution)/shard_map/ppermute | solution.py:316
  26.1 0.0 collective-permute-start.5
  26.1 0.2 collective-permute-done.7.s3
  26.3 2.6 %collective-permute-done.6.s2 = f32[2,256]{1,0:T(2,128)S(1)} collective-permute-done((f32[2,256]{1,0:T(2,128)S(1)}, f32[2,256]{1,0:T(2,128)S(1)}, u32[]{:S(2)}, u32[]{:S(2)}) %collective-permute-start.6) | collective-permute-done | bytes 2080 | tf_op jit(solution)/shard_map/ppermute | solution.py:316
  29.0 0.0 collective-permute-done.5.s1
  29.0 0.0 copy-start.1
  29.0 0.5 %lead_kernel.1 = (bf16[256,1024]{1,0:T(8,128)(2,1)S(1)}, bf16[1040,128]{1,0:T(8,128)(2,1)S(1)}) custom-call(s32[1,256]{1,0:T(1,128)S(1)} %get-tuple-element.66.ids_ref, f32[2,256]{1,0:T(2,128)S(1)} %get-tuple-element.61.s0, f32[2,256]{1,0:T(2,128)S(1)} %collective-permute-done.5.s1, f32[2,256]{1,0:T(2,128)S(1)} %collective-permute-done.6.s2, ...), custom_call_target="tpu_custom_call" | custom-call | flops 67108864 | bytes 3421184 | tf_op jit(solution)/shard_map/lead_kernel/pallas_call | solution.py:256
  29.5 0.0 copy-start
  29.5 1.9 %collective-permute-start.8 = (bf16[1040,128]{1,0:T(8,128)(2,1)S(1)}, bf16[1040,128]{1,0:T(8,128)(2,1)S(1)}, u32[]{:S(2)}, u32[]{:S(2)}) collective-permute-start(bf16[1040,128]{1,0:T(8,128)(2,1)S(1)} %get-tuple-element.64.keep_ref.send_ref.mine_ref), channel_id=1, source_target_pairs={{0,4},{4,0},{8,12},{12,8},{16,20},{20,16},{24,28},{28,24},{32,36},... | collective-permute-start | bytes 798728 | tf_op jit(solution)/shard_map/ppermute | solution.py:284
  31.4 1.2 %collective-permute-done.8.theirs_ref = bf16[1040,128]{1,0:T(8,128)(2,1)S(1)} collective-permute-done((bf16[1040,128]{1,0:T(8,128)(2,1)S(1)}, bf16[1040,128]{1,0:T(8,128)(2,1)S(1)}, u32[]{:S(2)}, u32[]{:S(2)}) %collective-permute-start.8) | collective-permute-done | bytes 266272 | tf_op jit(solution)/shard_map/ppermute | solution.py:284
  32.5 0.1 chip_lead.1
  32.6 4.7 %collective-permute-start.10 = (bf16[784,128]{1,0:T(8,128)(2,1)S(1)}, bf16[784,128]{1,0:T(8,128)(2,1)S(1)}, u32[]{:S(2)}, u32[]{:S(2)}) collective-permute-start(bf16[784,128]{1,0:T(8,128)(2,1)S(1)} %get-tuple-element.65), channel_id=1, source_target_pairs={{8,0},{16,8},{20,4},{24,16},{28,12},{32,24},{36,20},{40,32},{44,28... | collective-permute-start | bytes 602120 | tf_op jit(solution)/shard_map/ppermute | solution.py:323
  37.3 1.3 %collective-permute-start.9 = (bf16[256,128]{1,0:T(8,128)(2,1)S(1)}, bf16[256,128]{1,0:T(8,128)(2,1)S(1)}, u32[]{:S(2)}, u32[]{:S(2)}) collective-permute-start(bf16[256,128]{1,0:T(8,128)(2,1)S(1)} %get-tuple-element.71), channel_id=1, source_target_pairs={{8,0},{16,8},{20,4},{24,16},{28,12},{32,24},{36,20},{40,32},{44,28... | collective-permute-start | bytes 196616 | tf_op jit(solution)/shard_map/ppermute | solution.py:323
  38.6 0.0 copy-done.1
  38.6 0.0 copy-done
  38.6 3.9 %back_kernel.1 = (bf16[256,1024]{1,0:T(8,128)(2,1)}, bf16[256,1024]{1,0:T(8,128)(2,1)}, f32[256,1024]{1,0:T(8,128)S(1)}, f32[256,1024]{1,0:T(8,128)S(1)}, bf16[2...) custom-call(s32[1,256]{1,0:T(1,128)S(1)} %get-tuple-element.66.ids_ref, f32[2,256]{1,0:T(2,128)S(1)} %get-tuple-element.61.s0, ...), custom_call_target="tpu_custom_call" | custom-call | flops 671088640 | bytes 10232832 | tf_op jit(solution)/shard_map/back_kernel/pallas_call | solution.py:256
  42.5 1.2 %collective-permute-done.9.rear_ref = bf16[256,128]{1,0:T(8,128)(2,1)S(1)} collective-permute-done((bf16[256,128]{1,0:T(8,128)(2,1)S(1)}, bf16[256,128]{1,0:T(8,128)(2,1)S(1)}, u32[]{:S(2)}, u32[]{:S(2)}) %collective-permute-start.9) | collective-permute-done | bytes 65568 | tf_op jit(solution)/shard_map/ppermute | solution.py:323
  43.8 0.0 collective-permute-done.10.front_ref
  43.8 0.0 collective-permute-start.11
  43.8 0.5 %collective-permute-start.12 = (bf16[256,128]{1,0:T(8,128)(2,1)S(1)}, bf16[256,128]{1,0:T(8,128)(2,1)S(1)}, u32[]{:S(2)}, u32[]{:S(2)}) collective-permute-start(bf16[256,128]{1,0:T(8,128)(2,1)S(1)} %collective-permute-done.9.rear_ref), channel_id=1, source_target_pairs={{0,4},{4,0},{8,12},{12,8},{16,20},{20,16},{24,28},{28,24},{32,36},... | collective-permute-start | bytes 196616 | tf_op jit(solution)/shard_map/ppermute | solution.py:284
  44.3 1.0 %collective-permute-done.12.rear_other_ref = bf16[256,128]{1,0:T(8,128)(2,1)S(1)} collective-permute-done((bf16[256,128]{1,0:T(8,128)(2,1)S(1)}, bf16[256,128]{1,0:T(8,128)(2,1)S(1)}, u32[]{:S(2)}, u32[]{:S(2)}) %collective-permute-start.12) | collective-permute-done | bytes 65568 | tf_op jit(solution)/shard_map/ppermute | solution.py:284
  45.3 0.0 collective-permute-done.11.front_other_ref
  45.3 1.4 %finish_kernel.1 = (bf16[256,1024]{1,0:T(8,128)(2,1)}, bf16[256,1024]{1,0:T(8,128)(2,1)}) custom-call(s32[1,128]{1,0:T(1,128)S(1)} %broadcast_in_dim.3.odd_ref, bf16[1040,128]{1,0:T(8,128)(2,1)S(1)} %get-tuple-element.64.keep_ref.send_ref.mine_ref, bf16[1040,128]{1,0:T(8,128)(2,1)S(1)} %collective-permute-done.8.theirs_ref, ...), custom_call_target="tpu_custom_call" | custom-call | flops 134217728 | bytes 5259776 | tf_op jit(solution)/shard_map/finish_kernel/pallas_call | solution.py:256
  (1 shorter events, 0.0 us)
Async XLA Ops:
  2.2 4.3 %collective-permute-start = (bf16[528,128]{1,0:T(8,128)(2,1)S(1)}, bf16[528,128]{1,0:T(8,128)(2,1)S(1)}, u32[]{:S(2)}, u32[]{:S(2)}) collective-permute-start(bf16[528,128]{1,0:T(8,128)(2,1)S(1)} %get-tuple-element.45.send_ref), channel_id=1, source_target_pairs={{0,4},{4,0},{8,12},{12,8},{16,20},{20,16},{24,28},{28,24},{32,36},... | collective-permute-start | bytes 405512 | tf_op jit(solution)/shard_map/ppermute | solution.py:284
  6.6 12.3 %collective-permute-start.3 = (bf16[528,128]{1,0:T(8,128)(2,1)S(1)}, bf16[528,128]{1,0:T(8,128)(2,1)S(1)}, u32[]{:S(2)}, u32[]{:S(2)}) collective-permute-start(bf16[528,128]{1,0:T(8,128)(2,1)S(1)} %get-tuple-element.46), channel_id=1, source_target_pairs={{0,8},{4,12},{8,16},{12,20},{16,24},{20,28},{24,32},{28,36},{32,40... | collective-permute-start | bytes 405512 | tf_op jit(solution)/shard_map/ppermute | solution.py:288
  6.7 12.2 %collective-permute-start.2 = (bf16[272,128]{1,0:T(8,128)(2,1)S(1)}, bf16[272,128]{1,0:T(8,128)(2,1)S(1)}, u32[]{:S(2)}, u32[]{:S(2)}) collective-permute-start(bf16[272,128]{1,0:T(8,128)(2,1)S(1)} %get-tuple-element.49), channel_id=1, source_target_pairs={{0,16},{4,20},{8,24},{12,28},{16,32},{20,36},{24,40},{28,44},{32,4... | collective-permute-start | bytes 208904 | tf_op jit(solution)/shard_map/ppermute | solution.py:288
  9.6 7.7 %collective-permute-start.1 = (bf16[256,128]{1,0:T(8,128)(2,1)S(1)}, bf16[256,128]{1,0:T(8,128)(2,1)S(1)}, u32[]{:S(2)}, u32[]{:S(2)}) collective-permute-start(bf16[256,128]{1,0:T(8,128)(2,1)S(1)} %get-tuple-element.48), channel_id=1, source_target_pairs={{0,16},{4,20},{8,24},{12,28},{16,32},{20,36},{24,40},{28,44},{32,4... | collective-permute-start | bytes 196616 | tf_op jit(solution)/shard_map/ppermute | solution.py:288
  19.1 2.7 %collective-permute-start.4 = (bf16[512,128]{1,0:T(8,128)(2,1)S(1)}, bf16[512,128]{1,0:T(8,128)(2,1)S(1)}, u32[]{:S(2)}, u32[]{:S(2)}) collective-permute-start(bf16[512,128]{1,0:T(8,128)(2,1)S(1)} %get-tuple-element.57), channel_id=1, source_target_pairs={{0,4},{4,0},{8,12},{12,8},{16,20},{20,16},{24,28},{28,24},{32,36},... | collective-permute-start | bytes 393224 | tf_op jit(solution)/shard_map/ppermute | solution.py:284
  22.3 4.0 %collective-permute-start.7 = (f32[2,256]{1,0:T(2,128)S(1)}, f32[2,256]{1,0:T(2,128)S(1)}, u32[]{:S(2)}, u32[]{:S(2)}) collective-permute-start(f32[2,256]{1,0:T(2,128)S(1)} %get-tuple-element.61.s0), channel_id=1, source_target_pairs={{0,2},{1,3},{2,0},{3,1},{4,6},{5,7},{6,4},{7,5},{8,10},{9,11},{10,... | collective-permute-start | bytes 6152 | tf_op jit(solution)/shard_map/ppermute | solution.py:316
  25.3 3.6 %collective-permute-start.6 = (f32[2,256]{1,0:T(2,128)S(1)}, f32[2,256]{1,0:T(2,128)S(1)}, u32[]{:S(2)}, u32[]{:S(2)}) collective-permute-start(f32[2,256]{1,0:T(2,128)S(1)} %get-tuple-element.61.s0), channel_id=1, source_target_pairs={{0,3},{1,2},{2,1},{3,0},{4,7},{5,6},{6,5},{7,4},{8,11},{9,10},{10,... | collective-permute-start | bytes 6152 | tf_op jit(solution)/shard_map/ppermute | solution.py:316
  26.1 2.9 %collective-permute-start.5 = (f32[2,256]{1,0:T(2,128)S(1)}, f32[2,256]{1,0:T(2,128)S(1)}, u32[]{:S(2)}, u32[]{:S(2)}) collective-permute-start(f32[2,256]{1,0:T(2,128)S(1)} %get-tuple-element.61.s0), channel_id=1, source_target_pairs={{0,1},{1,0},{2,3},{3,2},{4,5},{5,4},{6,7},{7,6},{8,9},{9,8},{10,11... | collective-permute-start | bytes 6152 | tf_op jit(solution)/shard_map/ppermute | solution.py:316
  29.0 9.7 %copy-start.1 = (bf16[256,1024]{1,0:T(8,128)(2,1)S(1)}, bf16[256,1024]{1,0:T(8,128)(2,1)}, u32[]{:S(2)}) copy-start(bf16[256,1024]{1,0:T(8,128)(2,1)} %g_ref.1) | copy-start | bytes 1572868
  29.5 9.2 %copy-start = (bf16[256,1024]{1,0:T(8,128)(2,1)S(1)}, bf16[256,1024]{1,0:T(8,128)(2,1)}, u32[]{:S(2)}) copy-start(bf16[256,1024]{1,0:T(8,128)(2,1)} %q_ref.1) | copy-start | bytes 1572868
  29.5 3.0 %collective-permute-start.8 = (bf16[1040,128]{1,0:T(8,128)(2,1)S(1)}, bf16[1040,128]{1,0:T(8,128)(2,1)S(1)}, u32[]{:S(2)}, u32[]{:S(2)}) collective-permute-start(bf16[1040,128]{1,0:T(8,128)(2,1)S(1)} %get-tuple-element.64.keep_ref.send_ref.mine_ref), channel_id=1, source_target_pairs={{0,4},{4,0},{8,12},{12,8},{16,20},{20,16},{24,28},{28,24},{32,36},... | collective-permute-start | bytes 798728 | tf_op jit(solution)/shard_map/ppermute | solution.py:284
  32.6 11.1 %collective-permute-start.10 = (bf16[784,128]{1,0:T(8,128)(2,1)S(1)}, bf16[784,128]{1,0:T(8,128)(2,1)S(1)}, u32[]{:S(2)}, u32[]{:S(2)}) collective-permute-start(bf16[784,128]{1,0:T(8,128)(2,1)S(1)} %get-tuple-element.65), channel_id=1, source_target_pairs={{8,0},{16,8},{20,4},{24,16},{28,12},{32,24},{36,20},{40,32},{44,28... | collective-permute-start | bytes 602120 | tf_op jit(solution)/shard_map/ppermute | solution.py:323
  37.3 6.4 %collective-permute-start.9 = (bf16[256,128]{1,0:T(8,128)(2,1)S(1)}, bf16[256,128]{1,0:T(8,128)(2,1)S(1)}, u32[]{:S(2)}, u32[]{:S(2)}) collective-permute-start(bf16[256,128]{1,0:T(8,128)(2,1)S(1)} %get-tuple-element.71), channel_id=1, source_target_pairs={{8,0},{16,8},{20,4},{24,16},{28,12},{32,24},{36,20},{40,32},{44,28... | collective-permute-start | bytes 196616 | tf_op jit(solution)/shard_map/ppermute | solution.py:323
  43.8 1.5 %collective-permute-start.11 = (bf16[784,128]{1,0:T(8,128)(2,1)S(1)}, bf16[784,128]{1,0:T(8,128)(2,1)S(1)}, u32[]{:S(2)}, u32[]{:S(2)}) collective-permute-start(bf16[784,128]{1,0:T(8,128)(2,1)S(1)} %collective-permute-done.10.front_ref), channel_id=1, source_target_pairs={{0,4},{4,0},{8,12},{12,8},{16,20},{20,16},{24,28},{28,24},{32,36},... | collective-permute-start | bytes 602120 | tf_op jit(solution)/shard_map/ppermute | solution.py:284
  43.8 1.5 %collective-permute-start.12 = (bf16[256,128]{1,0:T(8,128)(2,1)S(1)}, bf16[256,128]{1,0:T(8,128)(2,1)S(1)}, u32[]{:S(2)}, u32[]{:S(2)}) collective-permute-start(bf16[256,128]{1,0:T(8,128)(2,1)S(1)} %collective-permute-done.9.rear_ref), channel_id=1, source_target_pairs={{0,4},{4,0},{8,12},{12,8},{16,20},{20,16},{24,28},{28,24},{32,36},... | collective-permute-start | bytes 196616 | tf_op jit(solution)/shard_map/ppermute | solution.py:284

commit v8 on v7

--- a/solution.py
+++ b/solution.py
@@ -54,7 +54,9 @@
 
 
 def tail_kernel(ids_hbm, k_hbm, v_hbm, odd_ref, ids_ref, k_ref, v_ref, keep_ref, send_ref, kt_ref, sems):
-    loads = ((ids_hbm, ids_ref), (k_hbm, k_ref), (v_hbm, v_ref))
+    rows = k_ref.shape[0] // 2
+    parts = [slice(p * rows, (p + 1) * rows) for p in range(2)]
+    loads = [(ids_hbm, ids_ref)] + [(k_hbm.at[part], k_ref.at[part]) for part in parts] + [(v_hbm, v_ref)]
     copies = [pltpu.make_async_copy(hbm, ref, sems.at[i]) for i, (hbm, ref) in enumerate(loads)]
     for copy in copies:
         copy.start()
@@ -63,10 +65,11 @@
     ids = ids_ref[...]
     put_ids(ids, send_ref)
     hit = jnp.broadcast_to((ids == ids[:, -1:]).astype(F32).astype(BF), (HEAD, ids.shape[1]))
-    copies[1].wait()
-    for h in heads:
-        kt_ref[head(h), :] = k_ref[:, head(h)].T * hit
-    copies[2].wait()
+    for part, copy in zip(parts, copies[1:3]):
+        copy.wait()
+        for h in heads:
+            kt_ref[head(h), part] = k_ref[part, head(h)].T * hit[:, part]
+    copies[3].wait()
     states = [dot(kt_ref[head(h), :], v_ref[:, head(h)], NN) for h in heads]
     split(states, odd_ref[...] > 0, keep_ref, send_ref)
 
@@ -295,7 +298,7 @@
         tail_kernel,
         [pltpu.VMEM(ids.shape, ids.dtype)] + [pltpu.VMEM(a.shape, a.dtype) for a in (narrow, narrow, half, message)],
         unit // 2, in_hbm(ids), in_hbm(keys), in_hbm(values), odd,
-        in_specs=[HBM] * 3 + [VMEM], scratch=[pltpu.VMEM((states, length), BF), pltpu.SemaphoreType.DMA((3,))],
+        in_specs=[HBM] * 3 + [VMEM], scratch=[pltpu.VMEM((states, length), BF), pltpu.SemaphoreType.DMA((4,))],
     )
     tail_theirs = swap(tail_sent)
     outs = [message, shape((2 * HEAD + 2 * IDS, HEAD), BF), shape(((heads // 2 - 2) * HEAD, HEAD), BF)]

time: 46.9 us -> 46.9 us (level)
  no operation moved by 1% of the time
where the time goes in v8:
time: 46.9 us; the launch traced here: 46.6 us
  starting transfers between devices  25.4 us (54%)
  Pallas kernels  10.6 us (23%)
  waiting for transfers between devices  9.88 us (21%)
  between operations  0.75 us (2%)
    pallas_call x9, Pallas kernels, call(): pl.pallas_call(kernel, out_shape=outs, in_specs=in_specs or [VMEM] * len(...  10.6 us
    ppermute x3, starting transfers between devices, shift(): return lax.ppermute(x, 'ctx', pairs)  8.16 us
    ppermute x5, starting transfers between devices, swap(): return lax.ppermute(x, 'ctx', [(i, i ^ 1) for i in range(count)])  7.46 us
    ppermute x2, starting transfers between devices, spread(): return lax.ppermute(x, 'ctx', useful + spare)  5.99 us
    ppermute x5, waiting for transfers between devices, swap(): return lax.ppermute(x, 'ctx', [(i, i ^ 1) for i in range(count)])  4.18 us
    ppermute x3, starting transfers between devices, body(): lax.ppermute(sums, 'tp', [(i, i ^ step) for i in range(ranks)])  3.77 us
    ppermute x3, waiting for transfers between devices, body(): lax.ppermute(sums, 'tp', [(i, i ^ step) for i in range(ranks)])  2.87 us
    ppermute x3, waiting for transfers between devices, shift(): return lax.ppermute(x, 'ctx', pairs)  1.61 us
  transfers between devices with their start and end apart: 13, of which 8 were waited for; matrix products, arithmetic and copies ran while one was open for 0% of the time, Pallas kernels for 14%

profile of v8, /device:TPU:1, one launch (start us, length us, event | category | flops | bytes accessed | tf_op | source)
XLA Modules:
  0.0 46.6 jit_solution(11251045395549405195)
XLA Ops:
  0.6 1.6 %tail_kernel.1 = (s32[1,256]{1,0:T(1,128)S(1)}, bf16[256,1024]{1,0:T(8,128)(2,1)S(1)}, bf16[256,1024]{1,0:T(8,128)(2,1)S(1)}, bf16[512,128]{1,0:T(8,128)(2,1)S(1)}, bf16[528,128]{1,0:T(8,128)(2,1)S(1)}) custom-call(s32[1,256]{1,0:T(1,128)} %bitcast.1, bf16[256,1024]{1,0:T(8,128)(2,1)} %k_hbm.1, bf16[256,1024]{1,0:T(8,128)(2,1)} %v_hbm.1, ...), custom_call_target="tpu_custom_call" | custom-call | flops 67108864 | bytes 2365952 | tf_op jit(solution)/shard_map/tail_kernel/pallas_call | solution.py:259
  2.2 3.3 %collective-permute-start = (bf16[528,128]{1,0:T(8,128)(2,1)S(1)}, bf16[528,128]{1,0:T(8,128)(2,1)S(1)}, u32[]{:S(2)}, u32[]{:S(2)}) collective-permute-start(bf16[528,128]{1,0:T(8,128)(2,1)S(1)} %get-tuple-element.45.send_ref), channel_id=1, source_target_pairs={{0,4},{4,0},{8,12},{12,8},{16,20},{20,16},{24,28},{28,24},{32,36},... | collective-permute-start | bytes 405512 | tf_op jit(solution)/shard_map/ppermute | solution.py:287
  5.5 1.0 %collective-permute-done.theirs_ref = bf16[528,128]{1,0:T(8,128)(2,1)S(1)} collective-permute-done((bf16[528,128]{1,0:T(8,128)(2,1)S(1)}, bf16[528,128]{1,0:T(8,128)(2,1)S(1)}, u32[]{:S(2)}, u32[]{:S(2)}) %collective-permute-start) | collective-permute-done | bytes 135200 | tf_op jit(solution)/shard_map/ppermute | solution.py:287
  6.5 0.1 chip_tail.1
  6.6 0.1 collective-permute-start.3
  6.7 2.9 %collective-permute-start.2 = (bf16[272,128]{1,0:T(8,128)(2,1)S(1)}, bf16[272,128]{1,0:T(8,128)(2,1)S(1)}, u32[]{:S(2)}, u32[]{:S(2)}) collective-permute-start(bf16[272,128]{1,0:T(8,128)(2,1)S(1)} %get-tuple-element.49), channel_id=1, source_target_pairs={{0,16},{4,20},{8,24},{12,28},{16,32},{20,36},{24,40},{28,44},{32,4... | collective-permute-start | bytes 208904 | tf_op jit(solution)/shard_map/ppermute | solution.py:291
  9.6 5.2 %collective-permute-start.1 = (bf16[256,128]{1,0:T(8,128)(2,1)S(1)}, bf16[256,128]{1,0:T(8,128)(2,1)S(1)}, u32[]{:S(2)}, u32[]{:S(2)}) collective-permute-start(bf16[256,128]{1,0:T(8,128)(2,1)S(1)} %get-tuple-element.48), channel_id=1, source_target_pairs={{0,16},{4,20},{8,24},{12,28},{16,32},{20,36},{24,40},{28,44},{32,4... | collective-permute-start | bytes 196616 | tf_op jit(solution)/shard_map/ppermute | solution.py:291
  14.8 2.5 %local_kernel.1 = (bf16[8,256,256]{2,1,0:T(8,128)(2,1)S(1)}, f32[256,1024]{1,0:T(8,128)S(1)}, f32[256,1024]{1,0:T(8,128)S(1)}, bf16[256,1024]{1,0:T(8,128)(2,1)S(1)}, bf16[1024,256]{1,0:T(8,128)(2,1)S(1)}) custom-call(s32[1,256]{1,0:T(1,128)S(1)} %get-tuple-element.66.ids_ref, bf16[256,1024]{1,0:T(8,128)(2,1)} %q_ref.1, ...), custom_call_target="tpu_custom_call" | custom-call | flops 268435456 | bytes 6816768 | tf_op jit(solution)/shard_map/local_kernel/pallas_call | solution.py:259
  17.3 0.0 collective-permute-done.1.far_rear_ref
  17.3 1.6 %collective-permute-done.2.far_ref = bf16[272,128]{1,0:T(8,128)(2,1)S(1)} collective-permute-done((bf16[272,128]{1,0:T(8,128)(2,1)S(1)}, bf16[272,128]{1,0:T(8,128)(2,1)S(1)}, u32[]{:S(2)}, u32[]{:S(2)}) %collective-permute-start.2) | collective-permute-done | bytes 69664 | tf_op jit(solution)/shard_map/ppermute | solution.py:291
  18.9 0.0 collective-permute-done.3.near_ref
  18.9 0.1 edge_kernel.1
  19.1 1.7 %collective-permute-start.4 = (bf16[512,128]{1,0:T(8,128)(2,1)S(1)}, bf16[512,128]{1,0:T(8,128)(2,1)S(1)}, u32[]{:S(2)}, u32[]{:S(2)}) collective-permute-start(bf16[512,128]{1,0:T(8,128)(2,1)S(1)} %get-tuple-element.57), channel_id=1, source_target_pairs={{0,4},{4,0},{8,12},{12,8},{16,20},{20,16},{24,28},{28,24},{32,36},... | collective-permute-start | bytes 393224 | tf_op jit(solution)/shard_map/ppermute | solution.py:287
  20.8 1.0 %collective-permute-done.4.other_ref = bf16[512,128]{1,0:T(8,128)(2,1)S(1)} collective-permute-done((bf16[512,128]{1,0:T(8,128)(2,1)S(1)}, bf16[512,128]{1,0:T(8,128)(2,1)S(1)}, u32[]{:S(2)}, u32[]{:S(2)}) %collective-permute-start.4) | collective-permute-done | bytes 131104 | tf_op jit(solution)/shard_map/ppermute | solution.py:287
  21.8 0.5 %attend_kernel.1 = (bf16[1024,128]{1,0:T(8,128)(2,1)S(1)}, f32[256,1024]{1,0:T(8,128)S(1)}, f32[2,256]{1,0:T(2,128)S(1)}) custom-call(s32[1,128]{1,0:T(1,128)S(1)} %broadcast_in_dim.3.odd_ref, bf16[512,128]{1,0:T(8,128)(2,1)S(1)} %get-tuple-element.56.mine_ref, bf16[512,128]{1,0:T(8,128)(2,1)S(1)} %collective-permute-done.4.other_ref, ...), custom_call_target="tpu_custom_call" | custom-call | flops 67108864 | bytes 4196864 | tf_op jit(solution)/shard_map/attend_kernel/pallas_call | solution.py:259
  22.3 3.0 %collective-permute-start.7 = (f32[2,256]{1,0:T(2,128)S(1)}, f32[2,256]{1,0:T(2,128)S(1)}, u32[]{:S(2)}, u32[]{:S(2)}) collective-permute-start(f32[2,256]{1,0:T(2,128)S(1)} %get-tuple-element.61.s0), channel_id=1, source_target_pairs={{0,2},{1,3},{2,0},{3,1},{4,6},{5,7},{6,4},{7,5},{8,10},{9,11},{10,... | collective-permute-start | bytes 6152 | tf_op jit(solution)/shard_map/ppermute | solution.py:319
  25.3 0.8 %collective-permute-start.6 = (f32[2,256]{1,0:T(2,128)S(1)}, f32[2,256]{1,0:T(2,128)S(1)}, u32[]{:S(2)}, u32[]{:S(2)}) collective-permute-start(f32[2,256]{1,0:T(2,128)S(1)} %get-tuple-element.61.s0), channel_id=1, source_target_pairs={{0,3},{1,2},{2,1},{3,0},{4,7},{5,6},{6,5},{7,4},{8,11},{9,10},{10,... | collective-permute-start | bytes 6152 | tf_op jit(solution)/shard_map/ppermute | solution.py:319
  26.1 0.0 collective-permute-start.5
  26.1 0.2 collective-permute-done.7.s3
  26.3 2.6 %collective-permute-done.6.s2 = f32[2,256]{1,0:T(2,128)S(1)} collective-permute-done((f32[2,256]{1,0:T(2,128)S(1)}, f32[2,256]{1,0:T(2,128)S(1)}, u32[]{:S(2)}, u32[]{:S(2)}) %collective-permute-start.6) | collective-permute-done | bytes 2080 | tf_op jit(solution)/shard_map/ppermute | solution.py:319
  28.9 0.0 collective-permute-done.5.s1
  28.9 0.0 copy-start.1
  28.9 0.5 %lead_kernel.1 = (bf16[256,1024]{1,0:T(8,128)(2,1)S(1)}, bf16[1040,128]{1,0:T(8,128)(2,1)S(1)}) custom-call(s32[1,256]{1,0:T(1,128)S(1)} %get-tuple-element.66.ids_ref, f32[2,256]{1,0:T(2,128)S(1)} %get-tuple-element.61.s0, f32[2,256]{1,0:T(2,128)S(1)} %collective-permute-done.5.s1, f32[2,256]{1,0:T(2,128)S(1)} %collective-permute-done.6.s2, ...), custom_call_target="tpu_custom_call" | custom-call | flops 67108864 | bytes 3421184 | tf_op jit(solution)/shard_map/lead_kernel/pallas_call | solution.py:259
  29.4 0.0 copy-start
  29.5 1.9 %collective-permute-start.8 = (bf16[1040,128]{1,0:T(8,128)(2,1)S(1)}, bf16[1040,128]{1,0:T(8,128)(2,1)S(1)}, u32[]{:S(2)}, u32[]{:S(2)}) collective-permute-start(bf16[1040,128]{1,0:T(8,128)(2,1)S(1)} %get-tuple-element.64.keep_ref.send_ref.mine_ref), channel_id=1, source_target_pairs={{0,4},{4,0},{8,12},{12,8},{16,20},{20,16},{24,28},{28,24},{32,36},... | collective-permute-start | bytes 798728 | tf_op jit(solution)/shard_map/ppermute | solution.py:287
  31.3 1.2 %collective-permute-done.8.theirs_ref = bf16[1040,128]{1,0:T(8,128)(2,1)S(1)} collective-permute-done((bf16[1040,128]{1,0:T(8,128)(2,1)S(1)}, bf16[1040,128]{1,0:T(8,128)(2,1)S(1)}, u32[]{:S(2)}, u32[]{:S(2)}) %collective-permute-start.8) | collective-permute-done | bytes 266272 | tf_op jit(solution)/shard_map/ppermute | solution.py:287
  32.5 0.1 chip_lead.1
  32.6 4.7 %collective-permute-start.10 = (bf16[784,128]{1,0:T(8,128)(2,1)S(1)}, bf16[784,128]{1,0:T(8,128)(2,1)S(1)}, u32[]{:S(2)}, u32[]{:S(2)}) collective-permute-start(bf16[784,128]{1,0:T(8,128)(2,1)S(1)} %get-tuple-element.65), channel_id=1, source_target_pairs={{8,0},{16,8},{20,4},{24,16},{28,12},{32,24},{36,20},{40,32},{44,28... | collective-permute-start | bytes 602120 | tf_op jit(solution)/shard_map/ppermute | solution.py:326
  37.3 1.3 %collective-permute-start.9 = (bf16[256,128]{1,0:T(8,128)(2,1)S(1)}, bf16[256,128]{1,0:T(8,128)(2,1)S(1)}, u32[]{:S(2)}, u32[]{:S(2)}) collective-permute-start(bf16[256,128]{1,0:T(8,128)(2,1)S(1)} %get-tuple-element.71), channel_id=1, source_target_pairs={{8,0},{16,8},{20,4},{24,16},{28,12},{32,24},{36,20},{40,32},{44,28... | collective-permute-start | bytes 196616 | tf_op jit(solution)/shard_map/ppermute | solution.py:326
  38.6 0.0 copy-done.1
  38.6 0.0 copy-done
  38.6 3.9 %back_kernel.1 = (bf16[256,1024]{1,0:T(8,128)(2,1)}, bf16[256,1024]{1,0:T(8,128)(2,1)}, f32[256,1024]{1,0:T(8,128)S(1)}, f32[256,1024]{1,0:T(8,128)S(1)}, bf16[2...) custom-call(s32[1,256]{1,0:T(1,128)S(1)} %get-tuple-element.66.ids_ref, f32[2,256]{1,0:T(2,128)S(1)} %get-tuple-element.61.s0, ...), custom_call_target="tpu_custom_call" | custom-call | flops 671088640 | bytes 10232832 | tf_op jit(solution)/shard_map/back_kernel/pallas_call | solution.py:259
  42.5 1.2 %collective-permute-done.9.rear_ref = bf16[256,128]{1,0:T(8,128)(2,1)S(1)} collective-permute-done((bf16[256,128]{1,0:T(8,128)(2,1)S(1)}, bf16[256,128]{1,0:T(8,128)(2,1)S(1)}, u32[]{:S(2)}, u32[]{:S(2)}) %collective-permute-start.9) | collective-permute-done | bytes 65568 | tf_op jit(solution)/shard_map/ppermute | solution.py:326
  43.7 0.0 collective-permute-done.10.front_ref
  43.7 0.0 collective-permute-start.11
  43.7 0.5 %collective-permute-start.12 = (bf16[256,128]{1,0:T(8,128)(2,1)S(1)}, bf16[256,128]{1,0:T(8,128)(2,1)S(1)}, u32[]{:S(2)}, u32[]{:S(2)}) collective-permute-start(bf16[256,128]{1,0:T(8,128)(2,1)S(1)} %collective-permute-done.9.rear_ref), channel_id=1, source_target_pairs={{0,4},{4,0},{8,12},{12,8},{16,20},{20,16},{24,28},{28,24},{32,36},... | collective-permute-start | bytes 196616 | tf_op jit(solution)/shard_map/ppermute | solution.py:287
  44.2 1.0 %collective-permute-done.12.rear_other_ref = bf16[256,128]{1,0:T(8,128)(2,1)S(1)} collective-permute-done((bf16[256,128]{1,0:T(8,128)(2,1)S(1)}, bf16[256,128]{1,0:T(8,128)(2,1)S(1)}, u32[]{:S(2)}, u32[]{:S(2)}) %collective-permute-start.12) | collective-permute-done | bytes 65568 | tf_op jit(solution)/shard_map/ppermute | solution.py:287
  45.3 0.0 collective-permute-done.11.front_other_ref
  45.3 1.4 %finish_kernel.1 = (bf16[256,1024]{1,0:T(8,128)(2,1)}, bf16[256,1024]{1,0:T(8,128)(2,1)}) custom-call(s32[1,128]{1,0:T(1,128)S(1)} %broadcast_in_dim.3.odd_ref, bf16[1040,128]{1,0:T(8,128)(2,1)S(1)} %get-tuple-element.64.keep_ref.send_ref.mine_ref, bf16[1040,128]{1,0:T(8,128)(2,1)S(1)} %collective-permute-done.8.theirs_ref, ...), custom_call_target="tpu_custom_call" | custom-call | flops 134217728 | bytes 5259776 | tf_op jit(solution)/shard_map/finish_kernel/pallas_call | solution.py:259
  (1 shorter events, 0.0 us)
Async XLA Ops:
  2.2 4.3 %collective-permute-start = (bf16[528,128]{1,0:T(8,128)(2,1)S(1)}, bf16[528,128]{1,0:T(8,128)(2,1)S(1)}, u32[]{:S(2)}, u32[]{:S(2)}) collective-permute-start(bf16[528,128]{1,0:T(8,128)(2,1)S(1)} %get-tuple-element.45.send_ref), channel_id=1, source_target_pairs={{0,4},{4,0},{8,12},{12,8},{16,20},{20,16},{24,28},{28,24},{32,36},... | collective-permute-start | bytes 405512 | tf_op jit(solution)/shard_map/ppermute | solution.py:287
  6.6 12.3 %collective-permute-start.3 = (bf16[528,128]{1,0:T(8,128)(2,1)S(1)}, bf16[528,128]{1,0:T(8,128)(2,1)S(1)}, u32[]{:S(2)}, u32[]{:S(2)}) collective-permute-start(bf16[528,128]{1,0:T(8,128)(2,1)S(1)} %get-tuple-element.46), channel_id=1, source_target_pairs={{0,8},{4,12},{8,16},{12,20},{16,24},{20,28},{24,32},{28,36},{32,40... | collective-permute-start | bytes 405512 | tf_op jit(solution)/shard_map/ppermute | solution.py:291
  6.7 12.2 %collective-permute-start.2 = (bf16[272,128]{1,0:T(8,128)(2,1)S(1)}, bf16[272,128]{1,0:T(8,128)(2,1)S(1)}, u32[]{:S(2)}, u32[]{:S(2)}) collective-permute-start(bf16[272,128]{1,0:T(8,128)(2,1)S(1)} %get-tuple-element.49), channel_id=1, source_target_pairs={{0,16},{4,20},{8,24},{12,28},{16,32},{20,36},{24,40},{28,44},{32,4... | collective-permute-start | bytes 208904 | tf_op jit(solution)/shard_map/ppermute | solution.py:291
  9.6 7.7 %collective-permute-start.1 = (bf16[256,128]{1,0:T(8,128)(2,1)S(1)}, bf16[256,128]{1,0:T(8,128)(2,1)S(1)}, u32[]{:S(2)}, u32[]{:S(2)}) collective-permute-start(bf16[256,128]{1,0:T(8,128)(2,1)S(1)} %get-tuple-element.48), channel_id=1, source_target_pairs={{0,16},{4,20},{8,24},{12,28},{16,32},{20,36},{24,40},{28,44},{32,4... | collective-permute-start | bytes 196616 | tf_op jit(solution)/shard_map/ppermute | solution.py:291
  19.1 2.7 %collective-permute-start.4 = (bf16[512,128]{1,0:T(8,128)(2,1)S(1)}, bf16[512,128]{1,0:T(8,128)(2,1)S(1)}, u32[]{:S(2)}, u32[]{:S(2)}) collective-permute-start(bf16[512,128]{1,0:T(8,128)(2,1)S(1)} %get-tuple-element.57), channel_id=1, source_target_pairs={{0,4},{4,0},{8,12},{12,8},{16,20},{20,16},{24,28},{28,24},{32,36},... | collective-permute-start | bytes 393224 | tf_op jit(solution)/shard_map/ppermute | solution.py:287
  22.3 4.0 %collective-permute-start.7 = (f32[2,256]{1,0:T(2,128)S(1)}, f32[2,256]{1,0:T(2,128)S(1)}, u32[]{:S(2)}, u32[]{:S(2)}) collective-permute-start(f32[2,256]{1,0:T(2,128)S(1)} %get-tuple-element.61.s0), channel_id=1, source_target_pairs={{0,2},{1,3},{2,0},{3,1},{4,6},{5,7},{6,4},{7,5},{8,10},{9,11},{10,... | collective-permute-start | bytes 6152 | tf_op jit(solution)/shard_map/ppermute | solution.py:319
  25.3 3.6 %collective-permute-start.6 = (f32[2,256]{1,0:T(2,128)S(1)}, f32[2,256]{1,0:T(2,128)S(1)}, u32[]{:S(2)}, u32[]{:S(2)}) collective-permute-start(f32[2,256]{1,0:T(2,128)S(1)} %get-tuple-element.61.s0), channel_id=1, source_target_pairs={{0,3},{1,2},{2,1},{3,0},{4,7},{5,6},{6,5},{7,4},{8,11},{9,10},{10,... | collective-permute-start | bytes 6152 | tf_op jit(solution)/shard_map/ppermute | solution.py:319
  26.1 2.9 %collective-permute-start.5 = (f32[2,256]{1,0:T(2,128)S(1)}, f32[2,256]{1,0:T(2,128)S(1)}, u32[]{:S(2)}, u32[]{:S(2)}) collective-permute-start(f32[2,256]{1,0:T(2,128)S(1)} %get-tuple-element.61.s0), channel_id=1, source_target_pairs={{0,1},{1,0},{2,3},{3,2},{4,5},{5,4},{6,7},{7,6},{8,9},{9,8},{10,11... | collective-permute-start | bytes 6152 | tf_op jit(solution)/shard_map/ppermute | solution.py:319
  28.9 9.7 %copy-start.1 = (bf16[256,1024]{1,0:T(8,128)(2,1)S(1)}, bf16[256,1024]{1,0:T(8,128)(2,1)}, u32[]{:S(2)}) copy-start(bf16[256,1024]{1,0:T(8,128)(2,1)} %g_ref.1) | copy-start | bytes 1572868
  29.4 9.2 %copy-start = (bf16[256,1024]{1,0:T(8,128)(2,1)S(1)}, bf16[256,1024]{1,0:T(8,128)(2,1)}, u32[]{:S(2)}) copy-start(bf16[256,1024]{1,0:T(8,128)(2,1)} %q_ref.1) | copy-start | bytes 1572868
  29.5 3.0 %collective-permute-start.8 = (bf16[1040,128]{1,0:T(8,128)(2,1)S(1)}, bf16[1040,128]{1,0:T(8,128)(2,1)S(1)}, u32[]{:S(2)}, u32[]{:S(2)}) collective-permute-start(bf16[1040,128]{1,0:T(8,128)(2,1)S(1)} %get-tuple-element.64.keep_ref.send_ref.mine_ref), channel_id=1, source_target_pairs={{0,4},{4,0},{8,12},{12,8},{16,20},{20,16},{24,28},{28,24},{32,36},... | collective-permute-start | bytes 798728 | tf_op jit(solution)/shard_map/ppermute | solution.py:287
  32.6 11.1 %collective-permute-start.10 = (bf16[784,128]{1,0:T(8,128)(2,1)S(1)}, bf16[784,128]{1,0:T(8,128)(2,1)S(1)}, u32[]{:S(2)}, u32[]{:S(2)}) collective-permute-start(bf16[784,128]{1,0:T(8,128)(2,1)S(1)} %get-tuple-element.65), channel_id=1, source_target_pairs={{8,0},{16,8},{20,4},{24,16},{28,12},{32,24},{36,20},{40,32},{44,28... | collective-permute-start | bytes 602120 | tf_op jit(solution)/shard_map/ppermute | solution.py:326
  37.3 6.4 %collective-permute-start.9 = (bf16[256,128]{1,0:T(8,128)(2,1)S(1)}, bf16[256,128]{1,0:T(8,128)(2,1)S(1)}, u32[]{:S(2)}, u32[]{:S(2)}) collective-permute-start(bf16[256,128]{1,0:T(8,128)(2,1)S(1)} %get-tuple-element.71), channel_id=1, source_target_pairs={{8,0},{16,8},{20,4},{24,16},{28,12},{32,24},{36,20},{40,32},{44,28... | collective-permute-start | bytes 196616 | tf_op jit(solution)/shard_map/ppermute | solution.py:326
  43.7 1.5 %collective-permute-start.11 = (bf16[784,128]{1,0:T(8,128)(2,1)S(1)}, bf16[784,128]{1,0:T(8,128)(2,1)S(1)}, u32[]{:S(2)}, u32[]{:S(2)}) collective-permute-start(bf16[784,128]{1,0:T(8,128)(2,1)S(1)} %collective-permute-done.10.front_ref), channel_id=1, source_target_pairs={{0,4},{4,0},{8,12},{12,8},{16,20},{20,16},{24,28},{28,24},{32,36},... | collective-permute-start | bytes 602120 | tf_op jit(solution)/shard_map/ppermute | solution.py:287
  43.7 1.5 %collective-permute-start.12 = (bf16[256,128]{1,0:T(8,128)(2,1)S(1)}, bf16[256,128]{1,0:T(8,128)(2,1)S(1)}, u32[]{:S(2)}, u32[]{:S(2)}) collective-permute-start(bf16[256,128]{1,0:T(8,128)(2,1)S(1)} %collective-permute-done.9.rear_ref), channel_id=1, source_target_pairs={{0,4},{4,0},{8,12},{12,8},{16,20},{20,16},{24,28},{28,24},{32,36},... | collective-permute-start | bytes 196616 | tf_op jit(solution)/shard_map/ppermute | solution.py:287
